TPU v7x, 32 devices: a whole 2x2x4 slice. The times are simulated.
32 devices in a mesh: fsdp: 4 (over y, x), seq: 8 (over z, core).
Axes of the slice: x: 2, y: 2, z: 4, core: 2. Of those that a mesh axis runs over, the one named last changes fastest.
Arguments:
- tokens: bfloat16 [4, 2048, 4096], P('fsdp', 'seq'), may hold values from -6 to 6
- queries: bfloat16 [4, 2048, 4096], P('fsdp', 'seq'), may hold values from -70 to 70
- key_weight: bfloat16 [4096, 1024], P(('fsdp', 'seq')), may hold values from -0.09375 to 0.09375
- value_weight: bfloat16 [4096, 1024], P(('fsdp', 'seq')), may hold values from -0.09375 to 0.09375
- sorted_blocks: int32 [4, 8, 16], P('fsdp', None, 'seq'), may hold values from 0 to 15, as said below
Outputs:
- attended: bfloat16 [4, 2048, 4096], P('fsdp', 'seq')
Inputs may be any that keep to these rules, and one draw needn't show every extreme that they name: `sorted_blocks`: for each sequence and key-value head, a permutation of the 16 blocks. The 2 blocks of one device, over all key-value heads, name blocks that lie on one device at most 2 times, and for one head at most 1 times; both bounds are reached in every draw. Device d holds blocks d * 2 to d * 2 + 1.
All inputs are finite; a program needn't handle non-finite values.
Results may differ from a plain program's by a relative error of at most 0.012.
The roundings to bfloat16 on the way count: a program that leaves them out, or rounds other values in their place, can miss the bound.
Values may be sent and summed in bfloat16 or wider, within the bound.
No kernel may reach another device: no remote copies, remote signals or barrier semaphores. Data moves between devices by JAX's collectives and lax.ppermute only.
A program may use at most 128 MiB of HBM per device.

v0:
```python
import math

import jax
import jax.numpy as jnp
from jax import lax
from jax.sharding import PartitionSpec as P

DH = 128
KVH = 8
GROUP = 4
BLOCK = 128


def shifted(value, axis, steps):
    count = lax.axis_size(axis)
    first, last = (max(0, -steps), min(count, count - steps))
    return lax.ppermute(value, axis, [(source, source + steps) for source in range(first, last)])


def fetch_blocks(kv_table, target_dev, target_row, devices, capacity, send_requests, send_blocks):
    item_count = target_dev.shape[0]
    item_order = jnp.arange(item_count, dtype=jnp.int32)
    same_dev = target_dev[:, None] == target_dev[None, :]
    earlier = item_order[None, :] < item_order[:, None]
    ranking = jnp.sum((same_dev & earlier).astype(jnp.int32), axis=1)
    dev_hit = target_dev[:, None, None] == jnp.arange(devices, dtype=jnp.int32)[None, :, None]
    slot_hit = ranking[:, None, None] == jnp.arange(capacity, dtype=jnp.int32)[None, None, :]
    requests = jnp.sum(jnp.where(dev_hit & slot_hit, (target_row + 1)[:, None, None], 0), axis=0)
    wanted = send_requests(requests)
    replies = jnp.take(kv_table, jnp.maximum(wanted - 1, 0), axis=0)
    replies = jnp.where((wanted > 0)[:, :, None, None], replies, jnp.zeros_like(replies))
    arrived = send_blocks(replies)
    arrived = arrived.reshape(devices * capacity, arrived.shape[2], arrived.shape[3])
    return jnp.take(arrived, target_dev * capacity + ranking, axis=0)


def local(tokens, queries, key_weight, value_weight, sorted_blocks):
    token_rows = tokens[0]
    local_tokens = token_rows.shape[0]
    local_blocks = local_tokens // BLOCK
    devices = lax.axis_size("seq")
    key_sums = jnp.dot(
        token_rows,
        lax.all_gather(key_weight, ("fsdp", "seq"), axis=0, tiled=True),
        preferred_element_type=jnp.float32,
    )
    value_sums = jnp.dot(
        token_rows,
        lax.all_gather(value_weight, ("fsdp", "seq"), axis=0, tiled=True),
        preferred_element_type=jnp.float32,
    )
    key_blocks = key_sums.astype(jnp.bfloat16).reshape(local_blocks, BLOCK, KVH, DH)
    value_blocks = value_sums.astype(jnp.bfloat16).reshape(local_blocks, BLOCK, KVH, DH)
    packed = jnp.concatenate([key_blocks, value_blocks], axis=3).transpose(2, 0, 1, 3)
    prev_edge = shifted(packed[:, local_blocks - 1], "seq", 1)
    preceding = jnp.concatenate([prev_edge[:, None], packed[:, : local_blocks - 1]], axis=1)
    targets = sorted_blocks[0]
    target_dev = targets // local_blocks
    target_slot = targets % local_blocks
    capacity = (local_blocks + devices - 1) // devices
    gathered_heads = []
    for kv_head in range(KVH):
        gathered_heads.append(
            fetch_blocks(
                packed[kv_head],
                target_dev[kv_head],
                target_slot[kv_head],
                devices,
                capacity,
                lambda payload: lax.all_to_all(
                    payload, "seq", split_axis=0, concat_axis=0, tiled=True
                ),
                lambda payload: lax.all_to_all(
                    payload, "seq", split_axis=0, concat_axis=0, tiled=True
                ),
            )
        )
    sorted_kv = jnp.stack(gathered_heads, axis=0)
    candidates = jnp.concatenate([packed, preceding, sorted_kv], axis=2)
    key_part = candidates[:, :, :, :DH]
    value_part = candidates[:, :, :, DH:]
    query_blocks = queries[0].reshape(local_blocks, BLOCK, KVH, GROUP, DH)
    scores = jnp.einsum(
        "bthge,hbke->hgbtk", query_blocks, key_part, preferred_element_type=jnp.float32
    ) * (1.0 / math.sqrt(DH))
    block_index = lax.axis_index("seq") * local_blocks + jnp.arange(local_blocks, dtype=jnp.int32)
    key_index = jnp.arange(3 * BLOCK, dtype=jnp.int32)
    blocked = (
        (block_index[:, None] == 0)
        & (key_index[None, :] >= BLOCK)
        & (key_index[None, :] < 2 * BLOCK)
    )
    scores = jnp.where(blocked[None, None, :, None, :], -1e30, scores)
    highest = jnp.max(scores, axis=-1, keepdims=True)
    raised = jnp.exp(scores - highest)
    weights = (raised / jnp.sum(raised, axis=-1, keepdims=True)).astype(jnp.bfloat16)
    result = jnp.einsum(
        "hgbtk,hbke->bthge", weights, value_part, preferred_element_type=jnp.float32
    )
    return result.astype(jnp.bfloat16).reshape(1, local_tokens, KVH * GROUP * DH)


def solution(mesh):
    placed = (
        P("fsdp", "seq", None),
        P("fsdp", "seq", None),
        P(("fsdp", "seq"), None),
        P(("fsdp", "seq"), None),
        P("fsdp", None, "seq"),
    )
    return jax.shard_map(
        local, mesh=mesh, in_specs=placed, out_specs=P("fsdp", "seq", None), check_vma=False
    )
```

profile of v0, /device:TPU:16, one launch (start us, length us, event | category | flops | bytes accessed | tf_op | source)
XLA Modules:
  0.0 364.9 jit_solution(2306015606827828122)
XLA Ops:
  10.1 5.2 %all-to-all-start.14 = ((s32[8,1,1]{2,1,0:T(1,128)}), s32[8,1,1]{2,1,0:T(1,128)S(1)}, u32[]{:S(2)}, u32[]{:S(2)}) async-start(s32[8,1,1]{2,1,0:T(1,128)} %copy.82), calls=%async_computation.14 | async-start | bytes 8192 | tf_op jit(solution)/shard_map/all_to_all | solution.py:70
  22.2 4.4 %reshape_squeeze.3 = bf16[2,128,8,4,128]{4,3,2,1,0:T(4,128)(2,1)} reshape(bf16[1,256,4096]{2,1,0:T(8,128)(2,1)} %param.10) | data formatting | bytes 4194304 | tf_op jit(solution)/shard_map/reshape;squeeze | solution.py:82
  26.6 5.1 %all-to-all-start.10 = ((s32[8,1,1]{2,1,0:T(1,128)}), s32[8,1,1]{2,1,0:T(1,128)S(1)}, u32[]{:S(2)}, u32[]{:S(2)}) async-start(s32[8,1,1]{2,1,0:T(1,128)} %copy.78), calls=%async_computation.10 | async-start | bytes 8192 | tf_op jit(solution)/shard_map/all_to_all | solution.py:70
  34.9 5.6 %all-to-all-start.8 = ((s32[8,1,1]{2,1,0:T(1,128)}), s32[8,1,1]{2,1,0:T(1,128)S(1)}, u32[]{:S(2)}, u32[]{:S(2)}) async-start(s32[8,1,1]{2,1,0:T(1,128)} %copy.76), calls=%async_computation.8 | async-start | bytes 8192 | tf_op jit(solution)/shard_map/all_to_all | solution.py:70
  43.8 5.6 %all-to-all-start.6 = ((s32[8,1,1]{2,1,0:T(1,128)}), s32[8,1,1]{2,1,0:T(1,128)S(1)}, u32[]{:S(2)}, u32[]{:S(2)}) async-start(s32[8,1,1]{2,1,0:T(1,128)} %copy.74), calls=%async_computation.6 | async-start | bytes 8192 | tf_op jit(solution)/shard_map/all_to_all | solution.py:70
  52.5 5.6 %all-to-all-start.4 = ((s32[8,1,1]{2,1,0:T(1,128)}), s32[8,1,1]{2,1,0:T(1,128)S(1)}, u32[]{:S(2)}, u32[]{:S(2)}) async-start(s32[8,1,1]{2,1,0:T(1,128)} %copy.72), calls=%async_computation.4 | async-start | bytes 8192 | tf_op jit(solution)/shard_map/all_to_all | solution.py:70
  61.3 5.6 %all-to-all-start.2 = ((s32[8,1,1]{2,1,0:T(1,128)}), s32[8,1,1]{2,1,0:T(1,128)S(1)}, u32[]{:S(2)}, u32[]{:S(2)}) async-start(s32[8,1,1]{2,1,0:T(1,128)} %copy.70), calls=%async_computation.2 | async-start | bytes 8192 | tf_op jit(solution)/shard_map/all_to_all | solution.py:70
  70.2 5.6 %all-to-all-start = ((s32[8,1,1]{2,1,0:T(1,128)}), s32[8,1,1]{2,1,0:T(1,128)S(1)}, u32[]{:S(2)}, u32[]{:S(2)}) async-start(s32[8,1,1]{2,1,0:T(1,128)} %copy.68), calls=%async_computation | async-start | bytes 8192 | tf_op jit(solution)/shard_map/all_to_all | solution.py:70
  79.0 5.6 %all-to-all-start.12 = ((s32[8,1,1]{2,1,0:T(1,128)}), s32[8,1,1]{2,1,0:T(1,128)S(1)}, u32[]{:S(2)}, u32[]{:S(2)}) async-start(s32[8,1,1]{2,1,0:T(1,128)} %copy.80), calls=%async_computation.12 | async-start | bytes 8192 | tf_op jit(solution)/shard_map/all_to_all | solution.py:70
  85.1 3.3 all-gather.3.cloned.1.call-done
  88.4 5.7 %fusion.35 = bf16[32,8,8,128]{3,1,2,0:T(8,128)(2,1)S(1)} fusion(bf16[4096,1024]{1,0:T(8,128)(2,1)} %all-gather.3.cloned.1.call-done, bf16[1,256,4096]{2,1,0:T(8,128)(2,1)S(1)} %copy-done), kind=kOutput, calls=%fused_computation.44 | convolution fusion | flops 2147745792 | bytes 11010048 | tf_op jit(solution)/shard_map/dot_general | solution.py:42
  94.4 73.1 %all-gather.5.cloned.1.call-done = bf16[4096,1024]{1,0:T(8,128)(2,1)} async-done(((bf16[128,1024]{1,0:T(8,128)(2,1)}), bf16[4096,1024]{1,0:T(8,128)(2,1)}) %all-gather.5.cloned.1.call-update) | async-done | bytes 8388624 | tf_op jit(solution)/shard_map/all_gather | solution.py:49
  167.5 5.7 %fusion.32 = bf16[32,8,8,128]{3,1,2,0:T(8,128)(2,1)S(1)} fusion(bf16[4096,1024]{1,0:T(8,128)(2,1)} %all-gather.5.cloned.1.call-done, bf16[1,256,4096]{2,1,0:T(8,128)(2,1)S(1)} %copy-done), kind=kOutput, calls=%fused_computation.43 | convolution fusion | flops 2147745792 | bytes 11010048 | tf_op jit(solution)/shard_map/dot_general | solution.py:47
  175.2 4.4 %all-to-all-start.11 = ((bf16[8,1,128,256]{3,2,1,0:T(8,128)(2,1)}), bf16[8,1,128,256]{3,2,1,0:T(8,128)(2,1)S(1)}, u32[]{:S(2)}, u32[]{:S(2)}) async-start(bf16[8,1,128,256]{3,2,1,0:T(8,128)(2,1)} %fusion.43), calls=%async_computation.11 | async-start | bytes 1048576 | tf_op jit(solution)/shard_map/all_to_all | solution.py:73
  181.4 10.3 %all-to-all-done.11 = bf16[8,1,128,256]{3,2,1,0:T(8,128)(2,1)S(1)} async-done(((bf16[8,1,128,256]{3,2,1,0:T(8,128)(2,1)}), bf16[8,1,128,256]{3,2,1,0:T(8,128)(2,1)S(1)}, u32[]{:S(2)}, u32[]{:S(2)}) %all-to-all-start.11) | async-done | bytes 524320 | tf_op jit(solution)/shard_map/all_to_all | solution.py:73
  191.7 7.3 %all-to-all-start.9 = ((bf16[8,1,128,256]{3,2,1,0:T(8,128)(2,1)}), bf16[8,1,128,256]{3,2,1,0:T(8,128)(2,1)}, u32[]{:S(2)}, u32[]{:S(2)}) async-start(bf16[8,1,128,256]{3,2,1,0:T(8,128)(2,1)} %fusion.45), calls=%async_computation.9 | async-start | bytes 1048576 | tf_op jit(solution)/shard_map/all_to_all | solution.py:73
  200.8 10.3 %all-to-all-done.9 = bf16[8,1,128,256]{3,2,1,0:T(8,128)(2,1)} async-done(((bf16[8,1,128,256]{3,2,1,0:T(8,128)(2,1)}), bf16[8,1,128,256]{3,2,1,0:T(8,128)(2,1)}, u32[]{:S(2)}, u32[]{:S(2)}) %all-to-all-start.9) | async-done | bytes 524320 | tf_op jit(solution)/shard_map/all_to_all | solution.py:73
  211.1 7.4 %all-to-all-start.7 = ((bf16[8,1,128,256]{3,2,1,0:T(8,128)(2,1)}), bf16[8,1,128,256]{3,2,1,0:T(8,128)(2,1)}, u32[]{:S(2)}, u32[]{:S(2)}) async-start(bf16[8,1,128,256]{3,2,1,0:T(8,128)(2,1)} %fusion.47), calls=%async_computation.7 | async-start | bytes 1048576 | tf_op jit(solution)/shard_map/all_to_all | solution.py:73
  220.3 10.3 %all-to-all-done.7 = bf16[8,1,128,256]{3,2,1,0:T(8,128)(2,1)} async-done(((bf16[8,1,128,256]{3,2,1,0:T(8,128)(2,1)}), bf16[8,1,128,256]{3,2,1,0:T(8,128)(2,1)}, u32[]{:S(2)}, u32[]{:S(2)}) %all-to-all-start.7) | async-done | bytes 524320 | tf_op jit(solution)/shard_map/all_to_all | solution.py:73
  230.6 6.8 %all-to-all-start.5 = ((bf16[8,1,128,256]{3,2,1,0:T(8,128)(2,1)}), bf16[8,1,128,256]{3,2,1,0:T(8,128)(2,1)S(1)}, u32[]{:S(2)}, u32[]{:S(2)}) async-start(bf16[8,1,128,256]{3,2,1,0:T(8,128)(2,1)} %fusion.49), calls=%async_computation.5 | async-start | bytes 1048576 | tf_op jit(solution)/shard_map/all_to_all | solution.py:73
  239.2 10.3 %all-to-all-done.5 = bf16[8,1,128,256]{3,2,1,0:T(8,128)(2,1)S(1)} async-done(((bf16[8,1,128,256]{3,2,1,0:T(8,128)(2,1)}), bf16[8,1,128,256]{3,2,1,0:T(8,128)(2,1)S(1)}, u32[]{:S(2)}, u32[]{:S(2)}) %all-to-all-start.5) | async-done | bytes 524320 | tf_op jit(solution)/shard_map/all_to_all | solution.py:73
  249.5 7.3 %all-to-all-start.3 = ((bf16[8,1,128,256]{3,2,1,0:T(8,128)(2,1)}), bf16[8,1,128,256]{3,2,1,0:T(8,128)(2,1)}, u32[]{:S(2)}, u32[]{:S(2)}) async-start(bf16[8,1,128,256]{3,2,1,0:T(8,128)(2,1)} %fusion.51), calls=%async_computation.3 | async-start | bytes 1048576 | tf_op jit(solution)/shard_map/all_to_all | solution.py:73
  258.6 10.3 %all-to-all-done.3 = bf16[8,1,128,256]{3,2,1,0:T(8,128)(2,1)} async-done(((bf16[8,1,128,256]{3,2,1,0:T(8,128)(2,1)}), bf16[8,1,128,256]{3,2,1,0:T(8,128)(2,1)}, u32[]{:S(2)}, u32[]{:S(2)}) %all-to-all-start.3) | async-done | bytes 524320 | tf_op jit(solution)/shard_map/all_to_all | solution.py:73
  268.9 7.4 %all-to-all-start.1 = ((bf16[8,1,128,256]{3,2,1,0:T(8,128)(2,1)}), bf16[8,1,128,256]{3,2,1,0:T(8,128)(2,1)}, u32[]{:S(2)}, u32[]{:S(2)}) async-start(bf16[8,1,128,256]{3,2,1,0:T(8,128)(2,1)} %fusion.53), calls=%async_computation.1 | async-start | bytes 1048576 | tf_op jit(solution)/shard_map/all_to_all | solution.py:73
  278.1 10.3 %all-to-all-done.1 = bf16[8,1,128,256]{3,2,1,0:T(8,128)(2,1)} async-done(((bf16[8,1,128,256]{3,2,1,0:T(8,128)(2,1)}), bf16[8,1,128,256]{3,2,1,0:T(8,128)(2,1)}, u32[]{:S(2)}, u32[]{:S(2)}) %all-to-all-start.1) | async-done | bytes 524320 | tf_op jit(solution)/shard_map/all_to_all | solution.py:73
  288.4 7.4 %all-to-all-start.15 = ((bf16[8,1,128,256]{3,2,1,0:T(8,128)(2,1)}), bf16[8,1,128,256]{3,2,1,0:T(8,128)(2,1)}, u32[]{:S(2)}, u32[]{:S(2)}) async-start(bf16[8,1,128,256]{3,2,1,0:T(8,128)(2,1)} %fusion.39), calls=%async_computation.15 | async-start | bytes 1048576 | tf_op jit(solution)/shard_map/all_to_all | solution.py:73
  309.1 6.2 %all-to-all-start.13 = ((bf16[8,1,128,256]{3,2,1,0:T(8,128)(2,1)}), bf16[8,1,128,256]{3,2,1,0:T(8,128)(2,1)}, u32[]{:S(2)}, u32[]{:S(2)}) async-start(bf16[8,1,128,256]{3,2,1,0:T(8,128)(2,1)} %fusion.41), calls=%async_computation.13 | async-start | bytes 1048576 | tf_op jit(solution)/shard_map/all_to_all | solution.py:73
  317.3 10.1 %all-to-all-done.13 = bf16[8,1,128,256]{3,2,1,0:T(8,128)(2,1)} async-done(((bf16[8,1,128,256]{3,2,1,0:T(8,128)(2,1)}), bf16[8,1,128,256]{3,2,1,0:T(8,128)(2,1)}, u32[]{:S(2)}, u32[]{:S(2)}) %all-to-all-start.13) | async-done | bytes 524320 | tf_op jit(solution)/shard_map/all_to_all | solution.py:73
  331.9 9.2 %fusion.80 = (f32[8,4,2,128]{3,1,2,0:T(4,128)S(1)}, f32[8,4,2,128,384]{3,4,1,2,0:T(8,128)}) fusion(pred[2,384]{1,0:T(4,128)(4,1)S(1)} %and_and_fusion, bf16[2,128,8,4,128]{4,3,2,1,0:T(4,128)(2,1)} %reshape_squeeze.3, bf16[8,2,384,256]{3,2,1,0:T(8,128)(2,1)} %pad_maximum_fusion), kind=kOutput, calls=%fused_computation.230 | convolution fusion | flops 817889664 | bytes 16286464 | tf_op jit(solution)/shard_map/sub | solution.py:95
  341.1 7.7 %convert_bitcast_fusion = bf16[2,128,8,4,128]{1,4,3,2,0:T(8,128)(2,1)} fusion(f32[8,4,2,128,384]{3,4,1,2,0:T(8,128)} %get-tuple-element.60, f32[8,4,2,128]{3,1,2,0:T(4,128)S(1)} %get-tuple-element.59, bf16[8,2,384,256]{3,2,1,0:T(8,128)(2,1)} %pad_maximum_fusion), kind=kOutput, calls=%fused_computation.34 | convolution fusion | flops 812646400 | bytes 16285696 | tf_op jit(solution)/shard_map/hgbtk,hbke->bthge/dot_general | solution.py:97
  348.8 4.7 %copy.87 = bf16[2,128,8,4,128]{4,3,2,1,0:T(4,128)(2,1)} copy(bf16[2,128,8,4,128]{1,4,3,2,0:T(8,128)(2,1)} %convert_bitcast_fusion) | data formatting | bytes 4194304 | tf_op jit(solution)/shard_map/convert_element_type | solution.py:100
  353.5 4.5 %reshape.1238 = bf16[1,256,4096]{2,1,0:T(8,128)(2,1)} reshape(bf16[2,128,8,4,128]{4,3,2,1,0:T(4,128)(2,1)} %copy.87) | data formatting | bytes 4194304 | tf_op jit(solution)/shard_map/reshape | solution.py:100
  (146 shorter events, 62.6 us)
Async XLA Ops:
  6.5 81.9 %copy-start = (bf16[1,256,4096]{2,1,0:T(8,128)(2,1)S(1)}, bf16[1,256,4096]{2,1,0:T(8,128)(2,1)}, u32[]{:S(2)}) copy-start(bf16[1,256,4096]{2,1,0:T(8,128)(2,1)} %param.9) | copy-start | bytes 6291460
  6.5 81.9 %all-gather.3.cloned.1.call-start = ((), (), s32[]{:S(2)}) async-start(), calls=%async_computation.16 | async-start | bytes 8650752 | tf_op jit(solution)/shard_map/all_gather | solution.py:44
  7.3 160.2 %all-gather.5.cloned.1.call-start = ((), (), s32[]{:S(2)}) async-start(), calls=%async_computation.17 | async-start | bytes 8650752 | tf_op jit(solution)/shard_map/all_gather | solution.py:49
  10.1 16.5 %all-to-all-start.14 = ((s32[8,1,1]{2,1,0:T(1,128)}), s32[8,1,1]{2,1,0:T(1,128)S(1)}, u32[]{:S(2)}, u32[]{:S(2)}) async-start(s32[8,1,1]{2,1,0:T(1,128)} %copy.82), calls=%async_computation.14 | async-start | bytes 8192 | tf_op jit(solution)/shard_map/all_to_all | solution.py:70
  26.6 8.3 %all-to-all-start.10 = ((s32[8,1,1]{2,1,0:T(1,128)}), s32[8,1,1]{2,1,0:T(1,128)S(1)}, u32[]{:S(2)}, u32[]{:S(2)}) async-start(s32[8,1,1]{2,1,0:T(1,128)} %copy.78), calls=%async_computation.10 | async-start | bytes 8192 | tf_op jit(solution)/shard_map/all_to_all | solution.py:70
  34.9 8.8 %all-to-all-start.8 = ((s32[8,1,1]{2,1,0:T(1,128)}), s32[8,1,1]{2,1,0:T(1,128)S(1)}, u32[]{:S(2)}, u32[]{:S(2)}) async-start(s32[8,1,1]{2,1,0:T(1,128)} %copy.76), calls=%async_computation.8 | async-start | bytes 8192 | tf_op jit(solution)/shard_map/all_to_all | solution.py:70
  43.8 8.8 %all-to-all-start.6 = ((s32[8,1,1]{2,1,0:T(1,128)}), s32[8,1,1]{2,1,0:T(1,128)S(1)}, u32[]{:S(2)}, u32[]{:S(2)}) async-start(s32[8,1,1]{2,1,0:T(1,128)} %copy.74), calls=%async_computation.6 | async-start | bytes 8192 | tf_op jit(solution)/shard_map/all_to_all | solution.py:70
  52.5 8.8 %all-to-all-start.4 = ((s32[8,1,1]{2,1,0:T(1,128)}), s32[8,1,1]{2,1,0:T(1,128)S(1)}, u32[]{:S(2)}, u32[]{:S(2)}) async-start(s32[8,1,1]{2,1,0:T(1,128)} %copy.72), calls=%async_computation.4 | async-start | bytes 8192 | tf_op jit(solution)/shard_map/all_to_all | solution.py:70
  61.3 8.8 %all-to-all-start.2 = ((s32[8,1,1]{2,1,0:T(1,128)}), s32[8,1,1]{2,1,0:T(1,128)S(1)}, u32[]{:S(2)}, u32[]{:S(2)}) async-start(s32[8,1,1]{2,1,0:T(1,128)} %copy.70), calls=%async_computation.2 | async-start | bytes 8192 | tf_op jit(solution)/shard_map/all_to_all | solution.py:70
  70.2 8.9 %all-to-all-start = ((s32[8,1,1]{2,1,0:T(1,128)}), s32[8,1,1]{2,1,0:T(1,128)S(1)}, u32[]{:S(2)}, u32[]{:S(2)}) async-start(s32[8,1,1]{2,1,0:T(1,128)} %copy.68), calls=%async_computation | async-start | bytes 8192 | tf_op jit(solution)/shard_map/all_to_all | solution.py:70
  79.0 96.1 %all-to-all-start.12 = ((s32[8,1,1]{2,1,0:T(1,128)}), s32[8,1,1]{2,1,0:T(1,128)S(1)}, u32[]{:S(2)}, u32[]{:S(2)}) async-start(s32[8,1,1]{2,1,0:T(1,128)} %copy.80), calls=%async_computation.12 | async-start | bytes 8192 | tf_op jit(solution)/shard_map/all_to_all | solution.py:70
  175.2 16.5 %all-to-all-start.11 = ((bf16[8,1,128,256]{3,2,1,0:T(8,128)(2,1)}), bf16[8,1,128,256]{3,2,1,0:T(8,128)(2,1)S(1)}, u32[]{:S(2)}, u32[]{:S(2)}) async-start(bf16[8,1,128,256]{3,2,1,0:T(8,128)(2,1)} %fusion.43), calls=%async_computation.11 | async-start | bytes 1048576 | tf_op jit(solution)/shard_map/all_to_all | solution.py:73
  191.7 19.4 %all-to-all-start.9 = ((bf16[8,1,128,256]{3,2,1,0:T(8,128)(2,1)}), bf16[8,1,128,256]{3,2,1,0:T(8,128)(2,1)}, u32[]{:S(2)}, u32[]{:S(2)}) async-start(bf16[8,1,128,256]{3,2,1,0:T(8,128)(2,1)} %fusion.45), calls=%async_computation.9 | async-start | bytes 1048576 | tf_op jit(solution)/shard_map/all_to_all | solution.py:73
  211.1 19.5 %all-to-all-start.7 = ((bf16[8,1,128,256]{3,2,1,0:T(8,128)(2,1)}), bf16[8,1,128,256]{3,2,1,0:T(8,128)(2,1)}, u32[]{:S(2)}, u32[]{:S(2)}) async-start(bf16[8,1,128,256]{3,2,1,0:T(8,128)(2,1)} %fusion.47), calls=%async_computation.7 | async-start | bytes 1048576 | tf_op jit(solution)/shard_map/all_to_all | solution.py:73
  230.6 18.9 %all-to-all-start.5 = ((bf16[8,1,128,256]{3,2,1,0:T(8,128)(2,1)}), bf16[8,1,128,256]{3,2,1,0:T(8,128)(2,1)S(1)}, u32[]{:S(2)}, u32[]{:S(2)}) async-start(bf16[8,1,128,256]{3,2,1,0:T(8,128)(2,1)} %fusion.49), calls=%async_computation.5 | async-start | bytes 1048576 | tf_op jit(solution)/shard_map/all_to_all | solution.py:73
  249.5 28.6 %copy-start.2 = (bf16[8,1,128,256]{3,2,1,0:T(8,128)(2,1)}, bf16[8,1,128,256]{3,2,1,0:T(8,128)(2,1)S(1)}, u32[]{:S(2)}) copy-start(bf16[8,1,128,256]{3,2,1,0:T(8,128)(2,1)S(1)} %all-to-all-done.5) | copy-start | bytes 1572868
  249.5 19.4 %all-to-all-start.3 = ((bf16[8,1,128,256]{3,2,1,0:T(8,128)(2,1)}), bf16[8,1,128,256]{3,2,1,0:T(8,128)(2,1)}, u32[]{:S(2)}, u32[]{:S(2)}) async-start(bf16[8,1,128,256]{3,2,1,0:T(8,128)(2,1)} %fusion.51), calls=%async_computation.3 | async-start | bytes 1048576 | tf_op jit(solution)/shard_map/all_to_all | solution.py:73
  268.9 19.5 %all-to-all-start.1 = ((bf16[8,1,128,256]{3,2,1,0:T(8,128)(2,1)}), bf16[8,1,128,256]{3,2,1,0:T(8,128)(2,1)}, u32[]{:S(2)}, u32[]{:S(2)}) async-start(bf16[8,1,128,256]{3,2,1,0:T(8,128)(2,1)} %fusion.53), calls=%async_computation.1 | async-start | bytes 1048576 | tf_op jit(solution)/shard_map/all_to_all | solution.py:73
  288.4 20.7 %all-to-all-start.15 = ((bf16[8,1,128,256]{3,2,1,0:T(8,128)(2,1)}), bf16[8,1,128,256]{3,2,1,0:T(8,128)(2,1)}, u32[]{:S(2)}, u32[]{:S(2)}) async-start(bf16[8,1,128,256]{3,2,1,0:T(8,128)(2,1)} %fusion.39), calls=%async_computation.15 | async-start | bytes 1048576 | tf_op jit(solution)/shard_map/all_to_all | solution.py:73
  296.7 32.5 %collective-permute-start = (bf16[8,128,256]{2,1,0:T(8,128)(2,1)}, bf16[8,128,256]{2,1,0:T(8,128)(2,1)}, u32[]{:S(2)}, u32[]{:S(2)}) collective-permute-start(bf16[8,128,256]{2,1,0:T(8,128)(2,1)} %get-tuple-element.39), channel_id=1, source_target_pairs={{0,1},{1,2},{2,3},{3,4},{4,5},{5,6},{6,7},{8,9},{9,10},{10,11},{11... | collective-permute-start | bytes 1572872 | tf_op jit(solution)/shard_map/ppermute | solution.py:17
  309.1 18.3 %all-to-all-start.13 = ((bf16[8,1,128,256]{3,2,1,0:T(8,128)(2,1)}), bf16[8,1,128,256]{3,2,1,0:T(8,128)(2,1)}, u32[]{:S(2)}, u32[]{:S(2)}) async-start(bf16[8,1,128,256]{3,2,1,0:T(8,128)(2,1)} %fusion.41), calls=%async_computation.13 | async-start | bytes 1048576 | tf_op jit(solution)/shard_map/all_to_all | solution.py:73
  348.8 9.2 %copy-start.1 = (bf16[1,256,4096]{2,1,0:T(8,128)(2,1)S(1)}, bf16[1,256,4096]{2,1,0:T(8,128)(2,1)}, u32[]{:S(2)}) copy-start(bf16[1,256,4096]{2,1,0:T(8,128)(2,1)} %param.9) | copy-start | bytes 6291460
Sparse Core Ops, SparseCore 0:
  10.4 78.0 all-gather.2
  91.4 76.0 all-gather.4
where the time goes:
time: 371 us; the launch traced here: 365 us
  waiting for transfers between devices  167 us (45%)
  starting transfers between devices  100 us (27%)
  local copies, waits for them, and re-layouts  36.7 us (10%)
  matrix products  28.3 us (8%)
  other arithmetic  18.7 us (5%)
  between operations  13.9 us (4%)
    all_to_all x16, starting transfers between devices, local(): lax.all_to_all(payload, 'seq', split_axis=0, concat_axis=0, tiled=True)  98.2 us
    all_to_all x16, waiting for transfers between devices, local(): lax.all_to_all(payload, 'seq', split_axis=0, concat_axis=0, tiled=True)  89.1 us
    all_gather x1, waiting for transfers between devices, local(): lax.all_gather(value_weight, ('fsdp', 'seq'), axis=0, tiled=True)  73.1 us
    gather x8, local copies, waits for them, and re-layouts, fetch_blocks(): return jnp.take(arrived, target_dev * capacity + ranking, axis=0)  11.7 us
    sub x1, matrix products, local(): raised = jnp.exp(scores - highest)  9.18 us
    dot_general x1, matrix products, local(): jnp.einsum('hgbtk,hbke->bthge', weights, value_part, preferred_element_ty...  7.73 us
    select_n x8, other arithmetic, fetch_blocks(): jnp.where((wanted > 0)[:, :, None, None], replies, jnp.zeros_like(replies))  7.62 us
  transfers between devices with their start and end apart: 19, of which 15 were waited for; matrix products, arithmetic and copies ran while one was open for 15% of the time, Pallas kernels for 0%

commit v1 on v0

v1 whole, which is shorter than its diff:
```python
import functools
import math

import jax
import jax.numpy as jnp
from jax import lax
from jax.experimental import pallas as pl
from jax.experimental.pallas import tpu as pltpu
from jax.sharding import PartitionSpec as P

DH = 128
KVH = 8
GROUP = 4
BLOCK = 128
EXP2_SCALE = math.log2(math.e) / math.sqrt(DH)


def plan_sends(all_targets, me, local_blocks, capacity):
    devices = all_targets.shape[0]
    targets = all_targets.reshape(devices, -1)
    heads = jnp.arange(targets.shape[1], dtype=jnp.int32) // local_blocks
    mine = targets // local_blocks == me
    rank = jnp.cumsum(mine.astype(jnp.int32), axis=1) - 1
    row = heads[None, :] * local_blocks + targets % local_blocks
    hit = mine[:, :, None] & (rank[:, :, None] == jnp.arange(capacity, dtype=jnp.int32))
    return jnp.sum(jnp.where(hit, row[:, :, None], 0), axis=1)


def plan_receives(targets, local_blocks, capacity):
    owner = targets.reshape(-1) // local_blocks
    order = jnp.arange(owner.shape[0], dtype=jnp.int32)
    same = (owner[:, None] == owner[None, :]) & (order[None, :] < order[:, None])
    return owner * capacity + jnp.sum(same.astype(jnp.int32), axis=1)


def attend_kernel(place_ref, first_ref, q_ref, k_ref, v_ref, pk_ref, pv_ref, *rest):
    sorted_refs, out_ref = rest[:-1], rest[-1]
    blocks = k_ref.shape[0] // BLOCK
    for b in range(blocks):
        rows = pl.ds(b * BLOCK, BLOCK)
        before = pl.ds((b - 1) * BLOCK, BLOCK)
        k_prev = pk_ref[...] if b == 0 else k_ref[before, :]
        v_prev = pv_ref[...] if b == 0 else v_ref[before, :]
        sorted_kv = sorted_refs[b][0]
        keys = jnp.concatenate([k_ref[rows, :], k_prev, sorted_kv[:, :DH]], axis=0)
        values = jnp.concatenate([v_ref[rows, :], v_prev, sorted_kv[:, DH:]], axis=0)
        q = jnp.concatenate([q_ref[rows, pl.ds(g * DH, DH)] for g in range(GROUP)], axis=0)
        scores = lax.dot_general(q, keys, (((1,), (1,)), ((), ())), preferred_element_type=jnp.float32)
        if b == 0:
            column = lax.broadcasted_iota(jnp.int32, (1, 3 * BLOCK), 1)
            blocked = (column >= BLOCK) & (column < 2 * BLOCK) & (first_ref[0] == 1)
            scores = jnp.where(blocked, -1e30, scores)
        raised = jnp.exp2((scores - jnp.max(scores, axis=-1, keepdims=True)) * EXP2_SCALE)
        weights = (raised * (1.0 / jnp.sum(raised, axis=-1, keepdims=True))).astype(jnp.bfloat16)
        result = jnp.dot(weights, values, preferred_element_type=jnp.float32).astype(jnp.bfloat16)
        for g in range(GROUP):
            out_ref[rows, pl.ds(g * DH, DH)] = result[g * BLOCK : (g + 1) * BLOCK]


def attend(place, first, queries, keys, values, prev_keys, prev_values, arrived):
    tokens = queries.shape[0]
    blocks = tokens // BLOCK
    head_columns = lambda h, place, first: (0, h)
    sorted_specs = [
        pl.BlockSpec((1, BLOCK, 2 * DH), lambda h, place, first, b=b: (place[h * blocks + b], 0, 0))
        for b in range(blocks)
    ]
    return pl.pallas_call(
        attend_kernel,
        grid_spec=pltpu.PrefetchScalarGridSpec(
            num_scalar_prefetch=2,
            grid=(KVH,),
            in_specs=[
                pl.BlockSpec((tokens, GROUP * DH), head_columns),
                pl.BlockSpec((tokens, DH), head_columns),
                pl.BlockSpec((tokens, DH), head_columns),
                pl.BlockSpec((BLOCK, DH), head_columns),
                pl.BlockSpec((BLOCK, DH), head_columns),
                *sorted_specs,
            ],
            out_specs=pl.BlockSpec((tokens, GROUP * DH), head_columns),
        ),
        out_shape=jax.ShapeDtypeStruct(queries.shape, jnp.bfloat16),
        compiler_params=pltpu.CompilerParams(vmem_limit_bytes=32 * 1024 * 1024),
    )(place, first, queries, keys, values, prev_keys, prev_values, *([arrived] * blocks))


def project(token_rows, key_weight, value_weight):
    weights = lax.all_gather(
        jnp.concatenate([key_weight, value_weight], axis=1), ("fsdp", "seq"), axis=0, tiled=True
    )
    packed = jnp.dot(token_rows, weights, preferred_element_type=jnp.float32).astype(jnp.bfloat16)
    return packed[:, : KVH * DH], packed[:, KVH * DH :]


def local(tokens, queries, key_weight, value_weight, sorted_blocks):
    local_blocks = tokens.shape[1] // BLOCK
    devices = lax.axis_size("seq")
    me = lax.axis_index("seq")
    capacity = (KVH * local_blocks + devices - 1) // devices
    targets = sorted_blocks[0]
    wanted = plan_sends(lax.all_gather(targets, "seq", axis=0), me, local_blocks, capacity)
    place = plan_receives(targets, local_blocks, capacity)

    keys, values = project(tokens[0], key_weight, value_weight)
    edge = jnp.concatenate([keys[-BLOCK:], values[-BLOCK:]], axis=1)
    prev = lax.ppermute(edge, "seq", [(i, i + 1) for i in range(devices - 1)])

    def table(rows):
        return rows.reshape(local_blocks, BLOCK, KVH, DH).transpose(2, 0, 1, 3)

    packed = jnp.concatenate([table(keys), table(values)], axis=3).reshape(-1, BLOCK, 2 * DH)
    replies = jnp.take(packed, wanted.reshape(-1), axis=0)
    arrived = lax.all_to_all(replies, "seq", split_axis=0, concat_axis=0, tiled=True)
    first = (me == 0).astype(jnp.int32).reshape(1)
    out = attend(place, first, queries[0], keys, values, prev[:, : KVH * DH], prev[:, KVH * DH :], arrived)
    return out[None]


def solution(mesh):
    placed = (
        P("fsdp", "seq", None),
        P("fsdp", "seq", None),
        P(("fsdp", "seq"), None),
        P(("fsdp", "seq"), None),
        P("fsdp", None, "seq"),
    )
    return jax.shard_map(
        local, mesh=mesh, in_specs=placed, out_specs=P("fsdp", "seq", None), check_vma=False
    )
```

time: 371 us -> 199 us (0.54); the launches traced: 365 us -> 198 us
  starting transfers between devices: 100 us -> 6.97 us
  waiting for transfers between devices: 167 us -> 133 us
  local copies, waits for them, and re-layouts: 36.7 us -> 10.6 us
  matrix products: 28.3 us -> 8.25 us
  other arithmetic: 18.7 us -> 4.82 us
  Pallas kernels: 0 us -> 11.9 us
  blocking collectives: 0 us -> 9.27 us
    all_to_all x16 -> x1, starting transfers between devices: 98.2 us -> 4.91 us  [local(): lax.all_to_all(replies, 'seq', split_axis=0, concat_axis=0, tiled=True)]
    all_to_all x16 -> x1, waiting for transfers between devices: 89.1 us -> 0.01 us  [local(): lax.all_to_all(replies, 'seq', split_axis=0, concat_axis=0, tiled=True)]
    all_gather x2 -> x1, waiting for transfers between devices: 76.4 us -> 107 us  [project(): lax.all_gather(jnp.concatenate([key_weight, value_weight], axis=1), ('fsd...]
    ppermute x1, waiting for transfers between devices: 0.01 us -> 26.2 us  [local(): prev = lax.ppermute(edge, 'seq', [(i, i + 1) for i in range(devices - 1)])]
    gather x16 -> x1, local copies, waits for them, and re-layouts: 16.4 us -> 1.84 us  [local(): replies = jnp.take(packed, wanted.reshape(-1), axis=0)]
    pallas_call x0 -> x1, Pallas kernels: none -> 11.9 us  [attend(): pl.pallas_call(attend_kernel, grid_spec=pltpu.PrefetchScalarGridSpec(num_...]
    dot_general x3 -> x1, matrix products: 19.1 us -> 8.25 us  [project(): jnp.dot(token_rows, weights, preferred_element_type=jnp.float32)]
    all_gather x0 -> x1, blocking collectives: none -> 9.27 us  [local(): lax.all_gather(targets, 'seq', axis=0)]
  transfers between devices with their start and end apart: 19 -> 3, of which waited for: 15 -> 2; matrix products, arithmetic and copies ran while one was open for 15% -> 1% of each run, Pallas kernels for 0% -> 0%
where the time goes in v1:
time: 199 us; the launch traced here: 198 us
  waiting for transfers between devices  133 us (67%)
  between operations  13.5 us (7%)
  Pallas kernels  11.9 us (6%)
  local copies, waits for them, and re-layouts  10.6 us (5%)
  blocking collectives  9.27 us (5%)
  matrix products  8.25 us (4%)
  starting transfers between devices  6.97 us (4%)
  other arithmetic  4.82 us (2%)
    all_gather x1, waiting for transfers between devices, project(): lax.all_gather(jnp.concatenate([key_weight, value_weight], axis=1), ('fsd...  107 us
    ppermute x1, waiting for transfers between devices, local(): prev = lax.ppermute(edge, 'seq', [(i, i + 1) for i in range(devices - 1)])  26.2 us
    pallas_call x1, Pallas kernels, attend(): pl.pallas_call(attend_kernel, grid_spec=pltpu.PrefetchScalarGridSpec(num_...  11.9 us
    all_gather x1, blocking collectives, local(): lax.all_gather(targets, 'seq', axis=0)  9.27 us
    dot_general x1, matrix products, project(): jnp.dot(token_rows, weights, preferred_element_type=jnp.float32)  8.25 us
    unnamed x18, local copies, waits for them, and re-layouts  6.23 us
    all_to_all x1, starting transfers between devices, local(): lax.all_to_all(replies, 'seq', split_axis=0, concat_axis=0, tiled=True)  4.91 us
  transfers between devices with their start and end apart: 3, of which 2 were waited for; matrix products, arithmetic and copies ran while one was open for 1% of the time, Pallas kernels for 0%

profile of v1, /device:TPU:16, one launch (start us, length us, event | category | flops | bytes accessed | tf_op | source)
XLA Modules:
  0.0 198.3 jit_solution(11152932235653051620)
XLA Ops:
  6.5 2.0 %pad_maximum_fusion.1 = bf16[128,2048]{1,0:T(8,128)(2,1)} fusion(bf16[128,1024]{1,0:T(8,128)(2,1)} %param.8, bf16[128,1024]{1,0:T(8,128)(2,1)} %param.7), kind=kLoop, calls=%fused_computation.6 | loop fusion | flops 1048576 | bytes 1048576 | tf_op jit(solution)/shard_map/concatenate | solution.py:90
  8.6 0.0 all-gather.2.cloned.1.call-update
  8.6 9.3 %all_gather.7 = s32[8,8,2]{1,2,0:T(2,128)S(1)} all-gather(s32[1,8,2]{1,2,0:T(2,128)} %param.9), channel_id=1, replica_groups=mesh['fsdp'=4,'seq'=8] {'seq'}, dimensions={0}, use_global_device_ids=true | all-gather | bytes 576 | tf_op jit(solution)/shard_map/all_gather | solution.py:102
  17.9 0.1 copy.33
  17.9 0.1 copy.34
  18.0 0.2 reduce_window_sum.11
  18.2 0.2 select_reduce_fusion
  18.4 0.1 copy.38
  18.4 0.1 reshape.233
  18.5 0.1 reshape.229
  18.6 106.8 %all-gather.2.cloned.1.call-done = bf16[4096,2048]{1,0:T(8,128)(2,1)} async-done(((bf16[128,2048]{1,0:T(8,128)(2,1)}), bf16[4096,2048]{1,0:T(8,128)(2,1)}) %all-gather.2.cloned.1.call-update) | async-done | bytes 16777232 | tf_op jit(solution)/shard_map/all_gather | solution.py:89
  125.5 8.3 %fusion = bf16[256,2048]{1,0:T(8,128)(2,1)S(1)} fusion(bf16[4096,2048]{1,0:T(8,128)(2,1)} %all-gather.2.cloned.1.call-done, bf16[1,256,4096]{2,1,0:T(8,128)(2,1)S(1)} %copy-done), kind=kOutput, calls=%fused_computation.2 | convolution fusion | flops 4295491584 | bytes 19922944 | tf_op jit(solution)/shard_map/dot_general | solution.py:92
  133.7 1.3 slice_bitcast_fusion.1
  135.1 0.1 copy.43
  135.2 0.1 copy.44
  135.3 0.2 copy_bitcast_fusion
  135.5 1.1 pad_maximum_fusion
  136.6 1.8 gather_fusion
  138.5 1.1 broadcast_select_fusion
  139.6 4.9 %all-to-all-start = ((bf16[16,128,256]{2,1,0:T(8,128)(2,1)}), bf16[16,128,256]{2,1,0:T(8,128)(2,1)S(1)}, u32[]{:S(2)}, u32[]{:S(2)}) async-start(bf16[16,128,256]{2,1,0:T(8,128)(2,1)} %broadcast_select_fusion), calls=%async_computation | async-start | bytes 2097152 | tf_op jit(solution)/shard_map/all_to_all | solution.py:114
  144.5 0.1 copy.31
  144.6 0.1 reshape_squeeze.3
  144.7 1.1 concatenate.12
  145.8 2.1 %collective-permute-start = (bf16[128,2048]{1,0:T(8,128)(2,1)S(1)}, bf16[128,2048]{1,0:T(8,128)(2,1)S(1)}, u32[]{:S(2)}, u32[]{:S(2)}) collective-permute-start(bf16[128,2048]{1,0:T(8,128)(2,1)S(1)} %concatenate.12), channel_id=1, source_target_pairs={{0,1},{1,2},{2,3},{3,4},{4,5},{5,6},{6,7},{8,9},{9,10},{10,11},{11... | collective-permute-start | bytes 1572872 | tf_op jit(solution)/shard_map/ppermute | solution.py:107
  147.9 0.2 convert_reduce_fusion
  148.0 26.2 %collective-permute-done = bf16[128,2048]{1,0:T(8,128)(2,1)S(1)} collective-permute-done((bf16[128,2048]{1,0:T(8,128)(2,1)S(1)}, bf16[128,2048]{1,0:T(8,128)(2,1)S(1)}, u32[]{:S(2)}, u32[]{:S(2)}) %collective-permute-start) | collective-permute-done | bytes 524320 | tf_op jit(solution)/shard_map/ppermute | solution.py:107
  174.2 0.7 fusion.12
  174.9 1.0 copy-done.1
  176.0 1.0 copy-done.2
  177.0 1.6 copy-done.3
  178.6 0.9 copy-done.4
  179.6 11.9 %shard_map.55 = bf16[256,4096]{1,0:T(8,128)(2,1)} custom-call(s32[16]{0:T(128)S(1)} %multiply_add_fusion.place_ref, s32[1]{0:T(128)} %bitcast.first_ref, bf16[256,4096]{1,0:T(8,128)(2,1)S(1)} %bitcast.25, bf16[256,1024]{1,0:T(8,128)(2,1)S(1)} %copy-done.2, bf16[256,1024]{1,0:T(8,128)(2,1)S(1)} %copy-done.1, bf16[128,1024]{1,0:T(8,128)(2,1)S(1)} %copy-done.4, ...), custom_call_target="tpu_custom_call" | custom-call | tf_op jit(solution)/shard_map/pallas_call | solution.py:68
  (20 shorter events, 0.1 us)
Async XLA Ops:
  6.5 118.9 %copy-start = (bf16[1,256,4096]{2,1,0:T(8,128)(2,1)S(1)}, bf16[1,256,4096]{2,1,0:T(8,128)(2,1)}, u32[]{:S(2)}) copy-start(bf16[1,256,4096]{2,1,0:T(8,128)(2,1)} %param.5) | copy-start | bytes 6291460
  6.5 118.9 %all-gather.2.cloned.1.call-start = ((), (), s32[]{:S(2)}) async-start(), calls=%async_computation.1 | async-start | bytes 17301504 | tf_op jit(solution)/shard_map/all_gather | solution.py:89
  133.7 1.4 copy-start.5
  138.5 6.0 %copy-start.6 = (s32[1,8,2]{1,2,0:T(2,128)S(1)}, s32[1,8,2]{1,2,0:T(2,128)}, u32[]{:S(2)}) copy-start(s32[1,8,2]{1,2,0:T(2,128)} %param.9) | copy-start | bytes 196
  139.6 35.3 %all-to-all-start = ((bf16[16,128,256]{2,1,0:T(8,128)(2,1)}), bf16[16,128,256]{2,1,0:T(8,128)(2,1)S(1)}, u32[]{:S(2)}, u32[]{:S(2)}) async-start(bf16[16,128,256]{2,1,0:T(8,128)(2,1)} %broadcast_select_fusion), calls=%async_computation | async-start | bytes 2097152 | tf_op jit(solution)/shard_map/all_to_all | solution.py:114
  145.8 28.4 %collective-permute-start = (bf16[128,2048]{1,0:T(8,128)(2,1)S(1)}, bf16[128,2048]{1,0:T(8,128)(2,1)S(1)}, u32[]{:S(2)}, u32[]{:S(2)}) collective-permute-start(bf16[128,2048]{1,0:T(8,128)(2,1)S(1)} %concatenate.12), channel_id=1, source_target_pairs={{0,1},{1,2},{2,3},{3,4},{4,5},{5,6},{6,7},{8,9},{9,10},{10,11},{11... | collective-permute-start | bytes 1572872 | tf_op jit(solution)/shard_map/ppermute | solution.py:107
  174.9 1.0 copy-start.1
  176.0 1.0 copy-start.2
  177.0 1.6 copy-start.3
  178.6 0.9 copy-start.4
Sparse Core Ops, SparseCore 0:
  10.4 115.0 all-gather.1

commit v2 on v1

v2 whole, which is shorter than its diff:
```python
import functools
import math

import jax
import jax.numpy as jnp
from jax import lax
from jax.experimental import pallas as pl
from jax.experimental.pallas import tpu as pltpu
from jax.sharding import Mesh, PartitionSpec as P

DH = 128
KVH = 8
GROUP = 4
BLOCK = 128
EXP2_SCALE = math.log2(math.e) / math.sqrt(DH)


def plan_sends(all_targets, me, local_blocks, capacity):
    devices = all_targets.shape[0]
    targets = all_targets.reshape(devices, -1)
    heads = jnp.arange(targets.shape[1], dtype=jnp.int32) // local_blocks
    mine = targets // local_blocks == me
    rank = jnp.cumsum(mine.astype(jnp.int32), axis=1) - 1
    row = heads[None, :] * local_blocks + targets % local_blocks
    hit = mine[:, :, None] & (rank[:, :, None] == jnp.arange(capacity, dtype=jnp.int32))
    return jnp.sum(jnp.where(hit, row[:, :, None], 0), axis=1)


def plan_receives(targets, local_blocks, capacity):
    owner = targets.reshape(-1) // local_blocks
    order = jnp.arange(owner.shape[0], dtype=jnp.int32)
    same = (owner[:, None] == owner[None, :]) & (order[None, :] < order[:, None])
    return owner * capacity + jnp.sum(same.astype(jnp.int32), axis=1)


def attend_kernel(place_ref, where_ref, q_ref, k_ref, v_ref, pk_ref, pv_ref, *rest):
    sorted_refs, out_ref = rest[:-1], rest[-1]
    k_ref, v_ref, pk_ref, pv_ref = [ref.at[0, 0] for ref in (k_ref, v_ref, pk_ref, pv_ref)]
    blocks = k_ref.shape[0] // BLOCK
    for b in range(blocks):
        rows = pl.ds(b * BLOCK, BLOCK)
        before = pl.ds((b - 1) * BLOCK, BLOCK)
        k_prev = pk_ref[...] if b == 0 else k_ref[before, :]
        v_prev = pv_ref[...] if b == 0 else v_ref[before, :]
        keys = jnp.concatenate([k_ref[rows, :], k_prev, sorted_refs[2 * b][0, 0]], axis=0)
        values = jnp.concatenate([v_ref[rows, :], v_prev, sorted_refs[2 * b + 1][0, 0]], axis=0)
        q = jnp.concatenate([q_ref[rows, pl.ds(g * DH, DH)] for g in range(GROUP)], axis=0)
        scores = lax.dot_general(q, keys, (((1,), (1,)), ((), ())), preferred_element_type=jnp.float32)
        if b == 0:
            column = lax.broadcasted_iota(jnp.int32, (1, 3 * BLOCK), 1)
            blocked = (column >= BLOCK) & (column < 2 * BLOCK) & (where_ref[0] == 1)
            scores = jnp.where(blocked, -1e30, scores)
        raised = jnp.exp2((scores - jnp.max(scores, axis=-1, keepdims=True)) * EXP2_SCALE)
        weights = (raised * (1.0 / jnp.sum(raised, axis=-1, keepdims=True))).astype(jnp.bfloat16)
        result = jnp.dot(weights, values, preferred_element_type=jnp.float32).astype(jnp.bfloat16)
        for g in range(GROUP):
            out_ref[rows, pl.ds(g * DH, DH)] = result[g * BLOCK : (g + 1) * BLOCK]


def attend(place, where, queries, own, prev, arrived):
    tokens = queries.shape[0]
    blocks = tokens // BLOCK
    heads = own.shape[3] // DH

    def kv_spec(rows, kind, at):
        def index(h, place, where):
            return (where[1] ^ kind, (h // heads) ^ where[at], 0, h % heads)

        return pl.BlockSpec((1, 1, rows, DH), index)

    def sorted_spec(b, kind):
        return pl.BlockSpec((1, 1, BLOCK, DH), lambda h, place, where: (kind, place[h * blocks + b], 0, 0))

    q_spec = pl.BlockSpec((tokens, GROUP * DH), lambda h, place, where: (0, h))
    return pl.pallas_call(
        attend_kernel,
        grid_spec=pltpu.PrefetchScalarGridSpec(
            num_scalar_prefetch=2,
            grid=(KVH,),
            in_specs=[
                q_spec,
                kv_spec(tokens, 0, 2),
                kv_spec(tokens, 1, 2),
                kv_spec(BLOCK, 0, 3),
                kv_spec(BLOCK, 1, 3),
                *[sorted_spec(b, kind) for b in range(blocks) for kind in range(2)],
            ],
            out_specs=q_spec,
        ),
        out_shape=jax.ShapeDtypeStruct(queries.shape, jnp.bfloat16),
        compiler_params=pltpu.CompilerParams(vmem_limit_bytes=32 * 1024 * 1024),
    )(place, where, queries, own, own, prev, prev, *([arrived] * (2 * blocks)))


def local_gathered(tokens, queries, key_weight, value_weight, sorted_blocks):
    local_blocks = tokens.shape[1] // BLOCK
    devices = lax.axis_size("seq")
    me = lax.axis_index("seq")
    capacity = (KVH * local_blocks + devices - 1) // devices
    targets = sorted_blocks[0]
    wanted = plan_sends(lax.all_gather(targets, "seq", axis=0), me, local_blocks, capacity)
    place = plan_receives(targets, local_blocks, capacity)
    weights = lax.all_gather(
        jnp.concatenate([key_weight, value_weight], axis=1), ("fsdp", "seq"), axis=0, tiled=True
    )
    packed = jnp.dot(tokens[0], weights, preferred_element_type=jnp.float32).astype(jnp.bfloat16)
    own = jnp.stack([packed[:, : KVH * DH], packed[:, KVH * DH :]])[:, None]
    prev = lax.ppermute(own[:, :, -BLOCK:], "seq", [(i, i + 1) for i in range(devices - 1)])
    table = own.reshape(2, local_blocks, BLOCK, KVH, DH).transpose(3, 1, 0, 2, 4)
    replies = jnp.take(table.reshape(-1, 2, BLOCK, DH), wanted.reshape(-1), axis=0)
    arrived = lax.all_to_all(replies, "seq", split_axis=0, concat_axis=0, tiled=True)
    zero = jnp.zeros_like(me)
    where = jnp.stack([(me == 0).astype(jnp.int32), zero, zero, zero])
    return attend(place, where, queries[0], own, prev, arrived.transpose(1, 0, 2, 3))[None]


def project_kernel(pieces, column_ref, *refs):
    token_refs, refs = refs[:4], refs[4:]
    piece_refs, (keep_ref, send_ref, weights, total, sems) = refs[:pieces], refs[pieces:]
    step = pl.program_id(0)

    @pl.when(step == 0)
    def _():
        for i in range(pieces):
            pltpu.make_async_copy(piece_refs[i], weights.at[i], sems.at[i]).start()

    pltpu.make_async_copy(piece_refs[0], weights.at[step], sems.at[step]).wait()
    rows = token_refs[0].shape[0]
    for i, ref in enumerate(token_refs):
        product = jnp.dot(ref[...], weights[step], preferred_element_type=jnp.float32)

        @pl.when(step == 0)
        def _():
            total[i] = product

        @pl.when((step > 0) & (step < pieces - 1))
        def _():
            total[i] += product

        @pl.when(step == pieces - 1)
        def _():
            out_ref = keep_ref if i % 2 == 0 else send_ref
            out_ref[i // 2] = (total[i] + product).astype(jnp.bfloat16)


def project(columns, token_sets, pieces):
    tokens, depth, width = token_sets[0].shape[0], *pieces[0].shape
    spec = pl.BlockSpec((tokens, depth), lambda i, columns: (0, columns[i]))
    shape = (2, tokens, width)
    return pl.pallas_call(
        functools.partial(project_kernel, len(pieces)),
        grid_spec=pltpu.PrefetchScalarGridSpec(
            num_scalar_prefetch=1,
            grid=(len(pieces),),
            in_specs=[spec] * 4 + [pl.BlockSpec(memory_space=pl.ANY)] * len(pieces),
            out_specs=[pl.BlockSpec(shape, lambda i, columns: (0, 0, 0))] * 2,
            scratch_shapes=[
                pltpu.VMEM((len(pieces), depth, width), jnp.bfloat16),
                pltpu.VMEM((4, tokens, width), jnp.float32),
                pltpu.SemaphoreType.DMA((len(pieces),)),
            ],
        ),
        out_shape=[jax.ShapeDtypeStruct(shape, jnp.bfloat16)] * 2,
        compiler_params=pltpu.CompilerParams(vmem_limit_bytes=40 * 1024 * 1024),
    )(columns, *token_sets, *pieces)


def pack_kernel(items, row_ref, part_ref, mine_ref, other_ref, out_ref, sems):
    heads = mine_ref.shape[2] // DH
    blocks = mine_ref.shape[1] // BLOCK

    def copy(i, source_ref):
        row = row_ref[i]
        head, block = row // blocks, row % blocks
        source = source_ref.at[
            part_ref[0] ^ (i // (items // 2)),
            pl.ds(pl.multiple_of(block * BLOCK, BLOCK), BLOCK),
            pl.ds(pl.multiple_of((head % heads) * DH, DH), DH),
        ]
        return pltpu.make_async_copy(source, out_ref.at[i], sems.at[i])

    for i in range(items):
        part = (row_ref[i] // blocks // heads) ^ part_ref[1]

        @pl.when(part == 0)
        def _():
            copy(i, mine_ref).start()

        @pl.when(part != 0)
        def _():
            copy(i, other_ref).start()

    for i in range(items):
        copy(i, mine_ref).wait()


def pack(rows, part, mine, other):
    items = rows.shape[0]
    return pl.pallas_call(
        functools.partial(pack_kernel, items),
        grid_spec=pltpu.PrefetchScalarGridSpec(
            num_scalar_prefetch=2,
            grid=(),
            in_specs=[pl.BlockSpec(memory_space=pl.ANY)] * 2,
            out_specs=pl.BlockSpec(memory_space=pl.ANY),
            scratch_shapes=[pltpu.SemaphoreType.DMA((items,))],
        ),
        out_shape=jax.ShapeDtypeStruct((items, BLOCK, DH), jnp.bfloat16),
    )(rows, part, mine, other)


def local_split(tokens, queries, key_weight, value_weight, sorted_blocks):
    y, x, z, c = [lax.axis_index(name) for name in ("y", "x", "z", "c")]
    chips = lax.axis_size("z")
    devices = 2 * chips
    me = 2 * z + c
    local_tokens = tokens.shape[1]
    local_blocks = local_tokens // BLOCK
    capacity = (KVH * local_blocks + devices - 1) // devices
    half = KVH * DH // 2
    targets = sorted_blocks[0]
    swap = [(0, 1), (1, 0)]

    quarters = jnp.stack(
        [key_weight[:, :half], key_weight[:, half:], value_weight[:, :half], value_weight[:, half:]]
    )
    shared = lax.all_to_all(quarters, ("x", "c"), split_axis=0, concat_axis=0, tiled=True)
    x_tokens = lax.ppermute(tokens[0], "x", swap)
    c_tokens = lax.ppermute(tokens[0], "c", swap)
    xc_tokens = lax.ppermute(x_tokens, "c", swap)

    ring = [(i, (i + 1) % chips) for i in range(chips)]
    pieces, columns = [], []
    depth = 2 * key_weight.shape[0]
    held = [shared[2 * i : 2 * i + 2].reshape(depth, half) for i in range(2)]
    for step in range(chips):
        if step > 0:
            held = [lax.ppermute(value, "z", ring) for value in held]
        from_z = (z - step) % chips
        for i in range(2):
            pieces += [held[i], lax.ppermute(held[i], "y", swap)]
            columns += [(y * 2 + i) * chips + from_z, ((1 - y) * 2 + i) * chips + from_z]

    all_targets = lax.all_gather(targets, ("x", "z", "c"), axis=0).reshape(2, devices, KVH, local_blocks)
    wanted = [plan_sends(all_targets[i], me, local_blocks, capacity).reshape(-1) for i in range(2)]
    place = plan_receives(targets, local_blocks, capacity)

    mine, sent = project(
        jnp.stack(columns).astype(jnp.int32), [tokens[0], c_tokens, x_tokens, xc_tokens], pieces
    )
    other = lax.ppermute(sent, "c", swap)
    replies = pack(jnp.concatenate(wanted), jnp.stack([x, c]).astype(jnp.int32), mine, other)
    arrived = lax.all_to_all(replies, ("x", "z", "c"), split_axis=0, concat_axis=0, tiled=True)
    arrived = arrived.reshape(2, devices * capacity, BLOCK, DH)

    own = jnp.stack([mine[0], other[0]])
    own = jnp.stack([own, lax.ppermute(jnp.stack([mine[1], other[1]]), "x", swap)])
    prev = lax.ppermute(own[:, :, -BLOCK:], ("z", "c"), [(i, i + 1) for i in range(devices - 1)])
    where = jnp.stack([(me == 0).astype(jnp.int32), x, c, 1 - c]).astype(jnp.int32)
    return attend(place, where, queries[0], own, prev, arrived)[None]


def solution(mesh):
    fsdp, seq = mesh.shape["fsdp"], mesh.shape["seq"]
    if fsdp == 4 and seq % 2 == 0 and seq <= 8:
        mesh = Mesh(mesh.devices.reshape(2, 2, seq // 2, 2), ("y", "x", "z", "c"))
        step, fsdp, seq = local_split, ("y", "x"), ("z", "c")
    else:
        step, fsdp, seq = local_gathered, ("fsdp",), ("seq",)
    placed = (
        P(fsdp, seq, None),
        P(fsdp, seq, None),
        P((*fsdp, *seq), None),
        P((*fsdp, *seq), None),
        P(fsdp, None, seq),
    )
    return jax.shard_map(step, mesh=mesh, in_specs=placed, out_specs=P(fsdp, seq, None), check_vma=False)
```

time: 199 us -> 248 us (1.25)
  Pallas kernels: 11.9 us -> 67.5 us
  starting transfers between devices: 6.97 us -> 38.4 us
  waiting for transfers between devices: 133 us -> 109 us
  between operations: 13.5 us -> 0.17 us
  blocking collectives: 9.27 us -> 18.3 us
  matrix products: 8.25 us -> 0 us
    all_gather x1 -> x0, waiting for transfers between devices: 107 us -> none  [project(): lax.all_gather(jnp.concatenate([key_weight, value_weight], axis=1), ('fsd...]
    ppermute x1 -> x20, waiting for transfers between devices: 26.2 us -> 104 us  [the longest x1 41.4 us: local_split(): x_tokens = lax.ppermute(tokens[0], 'x', swap)]
    pallas_call x0 -> x2, Pallas kernels: none -> 55.3 us  [the longest x1 34 us: pack(): pl.pallas_call(functools.partial(pack_kernel, items), grid_spec=pltpu.Pre...]
    ppermute x1 -> x20, starting transfers between devices: 2.06 us -> 24.5 us  [the longest x6 10.5 us: local_split(): held = [lax.ppermute(value, 'z', ring) for value in held]]
    all_gather x1, blocking collectives: 9.27 us -> 18.3 us  [local_split(): lax.all_gather(targets, ('x', 'z', 'c'), axis=0)]
    all_to_all x1 -> x2, starting transfers between devices: 4.91 us -> 13.9 us  [the longest x1 10.5 us: local_split(): lax.all_to_all(replies, ('x', 'z', 'c'), split_axis=0, concat_axis=0, til...]
    dot_general x1 -> x0, matrix products: 8.25 us -> none  [project(): jnp.dot(token_rows, weights, preferred_element_type=jnp.float32)]
    all_to_all x1 -> x2, waiting for transfers between devices: 0.01 us -> 4.36 us  [the longest x1 4.36 us: local_split(): lax.all_to_all(quarters, ('x', 'c'), split_axis=0, concat_axis=0, tiled=T...]
  transfers between devices with their start and end apart: 3 -> 22, of which waited for: 2 -> 13; matrix products, arithmetic and copies ran while one was open for 1% -> 3% of each run, Pallas kernels for 0% -> 0%
where the time goes in v2:
time: 248 us; the launch traced here: 247 us
  waiting for transfers between devices  109 us (44%)
  Pallas kernels  67.5 us (27%)
  starting transfers between devices  38.4 us (15%)
  blocking collectives  18.3 us (7%)
  local copies, waits for them, and re-layouts  9.48 us (4%)
  other arithmetic  4.31 us (2%)
    ppermute x1, waiting for transfers between devices, local_split(): x_tokens = lax.ppermute(tokens[0], 'x', swap)  41.4 us
    pallas_call x1, Pallas kernels, pack(): pl.pallas_call(functools.partial(pack_kernel, items), grid_spec=pltpu.Pre...  34 us
    ppermute x1, waiting for transfers between devices, local_split(): lax.ppermute(jnp.stack([mine[1], other[1]]), 'x', swap)  23.2 us
    pallas_call x1, Pallas kernels, project(): pl.pallas_call(functools.partial(project_kernel, len(pieces)), grid_spec=...  21.3 us
    ppermute x6, waiting for transfers between devices, local_split(): held = [lax.ppermute(value, 'z', ring) for value in held]  20.8 us
    all_gather x1, blocking collectives, local_split(): lax.all_gather(targets, ('x', 'z', 'c'), axis=0)  18.3 us
    pallas_call x1, Pallas kernels, attend(): pl.pallas_call(attend_kernel, grid_spec=pltpu.PrefetchScalarGridSpec(num_...  12.2 us
    ppermute x8, waiting for transfers between devices, local_split(): pieces += [held[i], lax.ppermute(held[i], 'y', swap)]  11 us
  transfers between devices with their start and end apart: 22, of which 13 were waited for; matrix products, arithmetic and copies ran while one was open for 3% of the time, Pallas kernels for 0%

profile of v2, /device:TPU:16, one launch (start us, length us, event | category | flops | bytes accessed | tf_op | source)
XLA Modules:
  0.0 246.7 jit_solution(17929013453521581455)
XLA Ops:
  0.0 1.5 collective-permute-start.1
  1.5 1.1 slice_bitcast_fusion.1
  3.5 3.5 %all-to-all-start = ((bf16[4,128,512]{2,1,0:T(8,128)(2,1)}), bf16[4,128,512]{2,1,0:T(8,128)(2,1)S(1)}, u32[]{:S(2)}, u32[]{:S(2)}) async-start(bf16[4,128,512]{2,1,0:T(8,128)(2,1)} %pad_maximum_fusion.1), calls=%async_computation | async-start | bytes 1048576 | tf_op jit(solution)/shard_map/all_to_all | solution.py:227
  7.4 41.4 %collective-permute-done.1.refs_2_ = bf16[256,4096]{1,0:T(8,128)(2,1)} collective-permute-done((bf16[256,4096]{1,0:T(8,128)(2,1)}, bf16[256,4096]{1,0:T(8,128)(2,1)}, u32[]{:S(2)}, u32[]{:S(2)}) %collective-permute-start.1) | collective-permute-done | bytes 2097184 | tf_op jit(solution)/shard_map/ppermute | solution.py:228
  48.8 4.4 %all-to-all-done = bf16[4,128,512]{2,1,0:T(8,128)(2,1)S(1)} async-done(((bf16[4,128,512]{2,1,0:T(8,128)(2,1)}), bf16[4,128,512]{2,1,0:T(8,128)(2,1)S(1)}, u32[]{:S(2)}, u32[]{:S(2)}) %all-to-all-start) | async-done | bytes 524320 | tf_op jit(solution)/shard_map/all_to_all | solution.py:227
  53.2 1.6 collective-permute-start.5
  54.9 1.7 collective-permute-start.3
  56.6 5.9 %collective-permute-done.5.refs_8_ = bf16[256,512]{1,0:T(8,128)(2,1)S(1)} collective-permute-done((bf16[256,512]{1,0:T(8,128)(2,1)S(1)}, bf16[256,512]{1,0:T(8,128)(2,1)S(1)}, u32[]{:S(2)}, u32[]{:S(2)}) %collective-permute-start.5) | collective-permute-done | bytes 262176 | tf_op jit(solution)/shard_map/ppermute | solution.py:238
  62.5 1.5 collective-permute-start.4
  64.1 2.0 collective-permute-done.7.refs_10_
  66.1 1.6 collective-permute-start.9
  67.7 18.3 %all_gather.3 = s32[16,8,2]{1,2,0:T(2,128)S(1)} all-gather(s32[1,8,2]{1,2,0:T(2,128)S(1)} %copy-done.11), channel_id=1, replica_groups=mesh['y'=2,'x'=2,'z'=4,'c'=2] {'x','z','c'}, dimensions={0}, use_global_device_ids=true | all-gather | bytes 1088 | tf_op jit(solution)/shard_map/all_gather | solution.py:244
  86.0 1.5 collective-permute-start.6
  90.4 6.6 %collective-permute-done.11.refs_14_ = bf16[256,512]{1,0:T(8,128)(2,1)} collective-permute-done((bf16[256,512]{1,0:T(8,128)(2,1)S(1)}, bf16[256,512]{1,0:T(8,128)(2,1)}, u32[]{:S(2)}, u32[]{:S(2)}) %collective-permute-start.11) | collective-permute-done | bytes 262176 | tf_op jit(solution)/shard_map/ppermute | solution.py:238
  97.0 2.6 %collective-permute-start.13 = (bf16[256,512]{1,0:T(8,128)(2,1)}, bf16[256,512]{1,0:T(8,128)(2,1)}, u32[]{:S(2)}, u32[]{:S(2)}) collective-permute-start(bf16[256,512]{1,0:T(8,128)(2,1)} %copy-done.6), channel_id=1, source_target_pairs={{0,2},{2,4},{4,6},{6,0},{1,3},{3,5},{5,7},{7,1},{8,10},{10,12},{12... | collective-permute-start | bytes 786440 | tf_op jit(solution)/shard_map/ppermute | solution.py:238
  100.2 4.3 %collective-permute-start.15 = (bf16[256,512]{1,0:T(8,128)(2,1)}, bf16[256,512]{1,0:T(8,128)(2,1)}, u32[]{:S(2)}, u32[]{:S(2)}) collective-permute-start(bf16[256,512]{1,0:T(8,128)(2,1)} %collective-permute-done.11.refs_14_), channel_id=1, source_target_pairs={{0,2},{2,4},{4,6},{6,0},{1,3},{3,5},{5,7},{7,1},{8,10},{10,12},{12... | collective-permute-start | bytes 786440 | tf_op jit(solution)/shard_map/ppermute | solution.py:238
  104.7 2.4 collective-permute-done.13.refs_16_
  107.5 3.9 %collective-permute-done.15.refs_18_ = bf16[256,512]{1,0:T(8,128)(2,1)} collective-permute-done((bf16[256,512]{1,0:T(8,128)(2,1)}, bf16[256,512]{1,0:T(8,128)(2,1)}, u32[]{:S(2)}, u32[]{:S(2)}) %collective-permute-start.15) | collective-permute-done | bytes 262176 | tf_op jit(solution)/shard_map/ppermute | solution.py:238
  112.0 1.5 collective-permute-start.16
  114.1 6.9 %collective-permute-done.14.refs_17_ = bf16[256,512]{1,0:T(8,128)(2,1)} collective-permute-done((bf16[256,512]{1,0:T(8,128)(2,1)}, bf16[256,512]{1,0:T(8,128)(2,1)}, u32[]{:S(2)}, u32[]{:S(2)}) %collective-permute-start.14) | collective-permute-done | bytes 262176 | tf_op jit(solution)/shard_map/ppermute | solution.py:241
  121.0 3.9 %collective-permute-done.16.refs_19_ = bf16[256,512]{1,0:T(8,128)(2,1)} collective-permute-done((bf16[256,512]{1,0:T(8,128)(2,1)}, bf16[256,512]{1,0:T(8,128)(2,1)}, u32[]{:S(2)}, u32[]{:S(2)}) %collective-permute-start.16) | collective-permute-done | bytes 262176 | tf_op jit(solution)/shard_map/ppermute | solution.py:241
  125.0 0.9 copy-done.5
  126.9 21.3 %shard_map.55 = (bf16[2,256,512]{2,1,0:T(8,128)(2,1)S(1)}, bf16[2,256,512]{2,1,0:T(8,128)(2,1)}) custom-call(s32[16]{0:T(128)S(1)} %stack.126.column_ref, bf16[256,4096]{1,0:T(8,128)(2,1)S(1)} %bitcast.45, bf16[256,4096]{1,0:T(8,128)(2,1)} %collective-permute-done.refs_1_, bf16[256,4096]{1,0:T(8,128)(2,1)} %collective-permute-done.1.refs_2_, ...), custom_call_target="tpu_custom_call" | custom-call | tf_op jit(solution)/shard_map/pallas_call | solution.py:150
  152.0 34.0 %shard_map.56 = bf16[32,128,128]{2,1,0:T(8,128)(2,1)} custom-call(s32[32]{0:T(128)} %pad_add_fusion.1.row_ref, s32[2]{0:T(128)} %pad_add_fusion.2.part_ref, bf16[2,256,512]{2,1,0:T(8,128)(2,1)} %copy-done.1, bf16[2,256,512]{2,1,0:T(8,128)(2,1)} %copy-done.9), custom_call_target="tpu_custom_call" | custom-call | tf_op jit(solution)/shard_map/pallas_call | solution.py:199
  186.0 10.5 %all-to-all-start.1 = ((bf16[32,128,128]{2,1,0:T(8,128)(2,1)}), bf16[32,128,128]{2,1,0:T(8,128)(2,1)S(1)}, u32[]{:S(2)}, u32[]{:S(2)}) async-start(bf16[32,128,128]{2,1,0:T(8,128)(2,1)} %shard_map.56), calls=%async_computation.1 | async-start | bytes 2097152 | tf_op jit(solution)/shard_map/all_to_all | solution.py:253
  196.6 1.6 collective-permute-start.18
  198.4 23.2 %collective-permute-done.18 = bf16[2,256,512]{2,1,0:T(8,128)(2,1)S(1)} collective-permute-done((bf16[2,256,512]{2,1,0:T(8,128)(2,1)S(1)}, bf16[2,256,512]{2,1,0:T(8,128)(2,1)S(1)}, u32[]{:S(2)}, u32[]{:S(2)}) %collective-permute-start.18) | collective-permute-done | bytes 524320 | tf_op jit(solution)/shard_map/ppermute | solution.py:257
  222.5 1.9 collective-permute-start.19
  224.7 1.1 pad_maximum_fusion.k_ref.v_ref
  225.8 7.1 %collective-permute-done.19.pk_ref.pv_ref = bf16[2,2,128,512]{3,2,1,0:T(8,128)(2,1)S(1)} collective-permute-done((bf16[2,2,128,512]{3,2,1,0:T(8,128)(2,1)S(1)}, bf16[2,2,128,512]{3,2,1,0:T(8,128)(2,1)S(1)}, u32[]{:S(2)}, u32[]{:S(2)}) %collective-permute-start.19) | collective-permute-done | bytes 524320 | tf_op jit(solution)/shard_map/ppermute | solution.py:258
  233.0 1.6 copy-done.3
  234.6 12.2 %shard_map.57 = bf16[256,4096]{1,0:T(8,128)(2,1)} custom-call(s32[16]{0:T(128)S(1)} %multiply_add_fusion.place_ref, s32[4]{0:T(128)S(1)} %pad_add_fusion.where_ref, bf16[256,4096]{1,0:T(8,128)(2,1)S(1)} %bitcast.46, bf16[2,2,256,512]{3,2,1,0:T(8,128)(2,1)S(1)} %pad_maximum_fusion.k_ref.v_ref, bf16[2,2,256,512]{3,2,1,0:T(8,128)(2,1)S(1)} %pad_maximum_fusion.k_ref.v_ref, ...), custom_call_target="tpu_custom_call" | custom-call | tf_op jit(solution)/shard_map/pallas_call | solution.py:75
  (76 shorter events, 13.0 us)
Async XLA Ops:
  0.0 7.0 %copy-start = (bf16[1,256,4096]{2,1,0:T(8,128)(2,1)S(1)}, bf16[1,256,4096]{2,1,0:T(8,128)(2,1)}, u32[]{:S(2)}) copy-start(bf16[1,256,4096]{2,1,0:T(8,128)(2,1)} %param.5) | copy-start | bytes 6291460
  0.0 67.7 %copy-start.11 = (s32[1,8,2]{1,2,0:T(2,128)S(1)}, s32[1,8,2]{1,2,0:T(2,128)}, u32[]{:S(2)}) copy-start(s32[1,8,2]{1,2,0:T(2,128)} %param.9) | copy-start | bytes 196
  0.0 48.8 %collective-permute-start.1 = (bf16[256,4096]{1,0:T(8,128)(2,1)}, bf16[256,4096]{1,0:T(8,128)(2,1)}, u32[]{:S(2)}, u32[]{:S(2)}) collective-permute-start(bf16[256,4096]{1,0:T(8,128)(2,1)} %bitcast.43), channel_id=1, source_target_pairs={{0,8},{8,0},{1,9},{9,1},{2,10},{10,2},{3,11},{11,3},{4,12},{12,4},... | collective-permute-start | bytes 6291464 | tf_op jit(solution)/shard_map/ppermute | solution.py:228
  3.5 49.7 %all-to-all-start = ((bf16[4,128,512]{2,1,0:T(8,128)(2,1)}), bf16[4,128,512]{2,1,0:T(8,128)(2,1)S(1)}, u32[]{:S(2)}, u32[]{:S(2)}) async-start(bf16[4,128,512]{2,1,0:T(8,128)(2,1)} %pad_maximum_fusion.1), calls=%async_computation | async-start | bytes 1048576 | tf_op jit(solution)/shard_map/all_to_all | solution.py:227
  7.0 118.0 %collective-permute-start = (bf16[256,4096]{1,0:T(8,128)(2,1)S(1)}, bf16[256,4096]{1,0:T(8,128)(2,1)}, u32[]{:S(2)}, u32[]{:S(2)}) collective-permute-start(bf16[256,4096]{1,0:T(8,128)(2,1)S(1)} %bitcast.44), channel_id=1, source_target_pairs={{0,1},{1,0},{2,3},{3,2},{4,5},{5,4},{6,7},{7,6},{8,9},{9,8},{10,11... | collective-permute-start | bytes 6291464 | tf_op jit(solution)/shard_map/ppermute | solution.py:229
  48.8 76.1 %collective-permute-start.2 = (bf16[256,4096]{1,0:T(8,128)(2,1)}, bf16[256,4096]{1,0:T(8,128)(2,1)}, u32[]{:S(2)}, u32[]{:S(2)}) collective-permute-start(bf16[256,4096]{1,0:T(8,128)(2,1)} %collective-permute-done.1.refs_2_), channel_id=1, source_target_pairs={{0,1},{1,0},{2,3},{3,2},{4,5},{5,4},{6,7},{7,6},{8,9},{9,8},{10,11... | collective-permute-start | bytes 6291464 | tf_op jit(solution)/shard_map/ppermute | solution.py:230
  53.2 9.3 %collective-permute-start.5 = (bf16[256,512]{1,0:T(8,128)(2,1)S(1)}, bf16[256,512]{1,0:T(8,128)(2,1)S(1)}, u32[]{:S(2)}, u32[]{:S(2)}) collective-permute-start(bf16[256,512]{1,0:T(8,128)(2,1)S(1)} %bitcast.50), channel_id=1, source_target_pairs={{0,2},{2,4},{4,6},{6,0},{1,3},{3,5},{5,7},{7,1},{8,10},{10,12},{12... | collective-permute-start | bytes 786440 | tf_op jit(solution)/shard_map/ppermute | solution.py:238
  54.9 11.2 %collective-permute-start.7 = (bf16[256,512]{1,0:T(8,128)(2,1)S(1)}, bf16[256,512]{1,0:T(8,128)(2,1)S(1)}, u32[]{:S(2)}, u32[]{:S(2)}) collective-permute-start(bf16[256,512]{1,0:T(8,128)(2,1)S(1)} %bitcast.47), channel_id=1, source_target_pairs={{0,2},{2,4},{4,6},{6,0},{1,3},{3,5},{5,7},{7,1},{8,10},{10,12},{12... | collective-permute-start | bytes 786440 | tf_op jit(solution)/shard_map/ppermute | solution.py:238
  54.9 31.0 %collective-permute-start.3 = (bf16[256,512]{1,0:T(8,128)(2,1)S(1)}, bf16[256,512]{1,0:T(8,128)(2,1)S(1)}, u32[]{:S(2)}, u32[]{:S(2)}) collective-permute-start(bf16[256,512]{1,0:T(8,128)(2,1)S(1)} %bitcast.51), channel_id=1, source_target_pairs={{0,16},{16,0},{1,17},{17,1},{2,18},{18,2},{3,19},{19,3},{4,20},{20... | collective-permute-start | bytes 786440 | tf_op jit(solution)/shard_map/ppermute | solution.py:241
  62.5 25.0 %collective-permute-start.4 = (bf16[256,512]{1,0:T(8,128)(2,1)S(1)}, bf16[256,512]{1,0:T(8,128)(2,1)S(1)}, u32[]{:S(2)}, u32[]{:S(2)}) collective-permute-start(bf16[256,512]{1,0:T(8,128)(2,1)S(1)} %bitcast.48), channel_id=1, source_target_pairs={{0,16},{16,0},{1,17},{17,1},{2,18},{18,2},{3,19},{19,3},{4,20},{20... | collective-permute-start | bytes 786440 | tf_op jit(solution)/shard_map/ppermute | solution.py:241
  66.1 22.5 %collective-permute-start.9 = (bf16[256,512]{1,0:T(8,128)(2,1)S(1)}, bf16[256,512]{1,0:T(8,128)(2,1)S(1)}, u32[]{:S(2)}, u32[]{:S(2)}) collective-permute-start(bf16[256,512]{1,0:T(8,128)(2,1)S(1)} %collective-permute-done.5.refs_8_), channel_id=1, source_target_pairs={{0,2},{2,4},{4,6},{6,0},{1,3},{3,5},{5,7},{7,1},{8,10},{10,12},{12... | collective-permute-start | bytes 786440 | tf_op jit(solution)/shard_map/ppermute | solution.py:238
  86.0 13.6 %collective-permute-start.6 = (bf16[256,512]{1,0:T(8,128)(2,1)S(1)}, bf16[256,512]{1,0:T(8,128)(2,1)}, u32[]{:S(2)}, u32[]{:S(2)}) collective-permute-start(bf16[256,512]{1,0:T(8,128)(2,1)S(1)} %collective-permute-done.5.refs_8_), channel_id=1, source_target_pairs={{0,16},{16,0},{1,17},{17,1},{2,18},{18,2},{3,19},{19,3},{4,20},{20... | collective-permute-start | bytes 786440 | tf_op jit(solution)/shard_map/ppermute | solution.py:241
  88.2 8.8 %collective-permute-start.11 = (bf16[256,512]{1,0:T(8,128)(2,1)S(1)}, bf16[256,512]{1,0:T(8,128)(2,1)}, u32[]{:S(2)}, u32[]{:S(2)}) collective-permute-start(bf16[256,512]{1,0:T(8,128)(2,1)S(1)} %collective-permute-done.7.refs_10_), channel_id=1, source_target_pairs={{0,2},{2,4},{4,6},{6,0},{1,3},{3,5},{5,7},{7,1},{8,10},{10,12},{12... | collective-permute-start | bytes 786440 | tf_op jit(solution)/shard_map/ppermute | solution.py:238
  89.3 10.9 %collective-permute-start.8 = (bf16[256,512]{1,0:T(8,128)(2,1)S(1)}, bf16[256,512]{1,0:T(8,128)(2,1)}, u32[]{:S(2)}, u32[]{:S(2)}) collective-permute-start(bf16[256,512]{1,0:T(8,128)(2,1)S(1)} %collective-permute-done.7.refs_10_), channel_id=1, source_target_pairs={{0,16},{16,0},{1,17},{17,1},{2,18},{18,2},{3,19},{19,3},{4,20},{20... | collective-permute-start | bytes 786440 | tf_op jit(solution)/shard_map/ppermute | solution.py:241
  97.0 10.0 %collective-permute-start.13 = (bf16[256,512]{1,0:T(8,128)(2,1)}, bf16[256,512]{1,0:T(8,128)(2,1)}, u32[]{:S(2)}, u32[]{:S(2)}) collective-permute-start(bf16[256,512]{1,0:T(8,128)(2,1)} %copy-done.6), channel_id=1, source_target_pairs={{0,2},{2,4},{4,6},{6,0},{1,3},{3,5},{5,7},{7,1},{8,10},{10,12},{12... | collective-permute-start | bytes 786440 | tf_op jit(solution)/shard_map/ppermute | solution.py:238
  99.6 12.4 %collective-permute-start.10 = (bf16[256,512]{1,0:T(8,128)(2,1)}, bf16[256,512]{1,0:T(8,128)(2,1)}, u32[]{:S(2)}, u32[]{:S(2)}) collective-permute-start(bf16[256,512]{1,0:T(8,128)(2,1)} %copy-done.6), channel_id=1, source_target_pairs={{0,16},{16,0},{1,17},{17,1},{2,18},{18,2},{3,19},{19,3},{4,20},{20... | collective-permute-start | bytes 786440 | tf_op jit(solution)/shard_map/ppermute | solution.py:241
  100.2 11.2 %collective-permute-start.15 = (bf16[256,512]{1,0:T(8,128)(2,1)}, bf16[256,512]{1,0:T(8,128)(2,1)}, u32[]{:S(2)}, u32[]{:S(2)}) collective-permute-start(bf16[256,512]{1,0:T(8,128)(2,1)} %collective-permute-done.11.refs_14_), channel_id=1, source_target_pairs={{0,2},{2,4},{4,6},{6,0},{1,3},{3,5},{5,7},{7,1},{8,10},{10,12},{12... | collective-permute-start | bytes 786440 | tf_op jit(solution)/shard_map/ppermute | solution.py:238
  107.0 7.1 %collective-permute-start.12 = (bf16[256,512]{1,0:T(8,128)(2,1)}, bf16[256,512]{1,0:T(8,128)(2,1)}, u32[]{:S(2)}, u32[]{:S(2)}) collective-permute-start(bf16[256,512]{1,0:T(8,128)(2,1)} %collective-permute-done.11.refs_14_), channel_id=1, source_target_pairs={{0,16},{16,0},{1,17},{17,1},{2,18},{18,2},{3,19},{19,3},{4,20},{20... | collective-permute-start | bytes 786440 | tf_op jit(solution)/shard_map/ppermute | solution.py:241
  111.5 9.6 %collective-permute-start.14 = (bf16[256,512]{1,0:T(8,128)(2,1)}, bf16[256,512]{1,0:T(8,128)(2,1)}, u32[]{:S(2)}, u32[]{:S(2)}) collective-permute-start(bf16[256,512]{1,0:T(8,128)(2,1)} %collective-permute-done.13.refs_16_), channel_id=1, source_target_pairs={{0,16},{16,0},{1,17},{17,1},{2,18},{18,2},{3,19},{19,3},{4,20},{20... | collective-permute-start | bytes 786440 | tf_op jit(solution)/shard_map/ppermute | solution.py:241
  112.0 13.0 %collective-permute-start.16 = (bf16[256,512]{1,0:T(8,128)(2,1)}, bf16[256,512]{1,0:T(8,128)(2,1)}, u32[]{:S(2)}, u32[]{:S(2)}) collective-permute-start(bf16[256,512]{1,0:T(8,128)(2,1)} %collective-permute-done.15.refs_18_), channel_id=1, source_target_pairs={{0,16},{16,0},{1,17},{17,1},{2,18},{18,2},{3,19},{19,3},{4,20},{20... | collective-permute-start | bytes 786440 | tf_op jit(solution)/shard_map/ppermute | solution.py:241
  125.0 1.0 copy-start.5
  125.9 0.9 copy-start.7
  148.2 0.8 copy-start.1
  149.0 2.1 collective-permute-start.17
  151.1 0.8 copy-start.9
  152.0 44.5 %copy-start.2 = (bf16[2,256,512]{2,1,0:T(8,128)(2,1)S(1)}, bf16[2,256,512]{2,1,0:T(8,128)(2,1)}, u32[]{:S(2)}) copy-start(bf16[2,256,512]{2,1,0:T(8,128)(2,1)} %copy-done.1) | copy-start | bytes 1572868
  185.9 10.5 %copy-start.10 = (bf16[2,256,512]{2,1,0:T(8,128)(2,1)S(1)}, bf16[2,256,512]{2,1,0:T(8,128)(2,1)}, u32[]{:S(2)}) copy-start(bf16[2,256,512]{2,1,0:T(8,128)(2,1)} %copy-done.9) | copy-start | bytes 1572868
  186.0 47.0 %all-to-all-start.1 = ((bf16[32,128,128]{2,1,0:T(8,128)(2,1)}), bf16[32,128,128]{2,1,0:T(8,128)(2,1)S(1)}, u32[]{:S(2)}, u32[]{:S(2)}) async-start(bf16[32,128,128]{2,1,0:T(8,128)(2,1)} %shard_map.56), calls=%async_computation.1 | async-start | bytes 2097152 | tf_op jit(solution)/shard_map/all_to_all | solution.py:253
  196.6 25.0 %collective-permute-start.18 = (bf16[2,256,512]{2,1,0:T(8,128)(2,1)S(1)}, bf16[2,256,512]{2,1,0:T(8,128)(2,1)S(1)}, u32[]{:S(2)}, u32[]{:S(2)}) collective-permute-start(bf16[2,256,512]{2,1,0:T(8,128)(2,1)S(1)} %pad_maximum_fusion.2), channel_id=1, source_target_pairs={{0,8},{8,0},{1,9},{9,1},{2,10},{10,2},{3,11},{11,3},{4,12},{12,4},... | collective-permute-start | bytes 1572872 | tf_op jit(solution)/shard_map/ppermute | solution.py:257
  221.6 0.8 copy-start.8
  222.5 10.5 %collective-permute-start.19 = (bf16[2,2,128,512]{3,2,1,0:T(8,128)(2,1)S(1)}, bf16[2,2,128,512]{3,2,1,0:T(8,128)(2,1)S(1)}, u32[]{:S(2)}, u32[]{:S(2)}) collective-permute-start(bf16[2,2,128,512]{3,2,1,0:T(8,128)(2,1)S(1)} %fusion), channel_id=1, source_target_pairs={{0,1},{1,2},{2,3},{3,4},{4,5},{5,6},{6,7},{8,9},{9,10},{10,11},{11... | collective-permute-start | bytes 1572872 | tf_op jit(solution)/shard_map/ppermute | solution.py:258
  233.0 1.6 copy-start.3
  (2 other events, 1.4 us)

commit v3 on v1

v3 whole, which is shorter than its diff:
```python
import functools
import math

import jax
import jax.numpy as jnp
from jax import lax
from jax.experimental import pallas as pl
from jax.experimental.pallas import tpu as pltpu
from jax.sharding import Mesh, PartitionSpec as P

DH = 128
KVH = 8
GROUP = 4
BLOCK = 128
TALL = 2 * BLOCK
EXP2_SCALE = math.log2(math.e) / math.sqrt(DH)


def plan_sends(all_targets, me, local_blocks, capacity):
    devices = all_targets.shape[0]
    targets = all_targets.reshape(devices, -1)
    heads = jnp.arange(targets.shape[1], dtype=jnp.int32) // local_blocks
    mine = targets // local_blocks == me
    rank = jnp.cumsum(mine.astype(jnp.int32), axis=1) - 1
    row = heads[None, :] * local_blocks + targets % local_blocks
    hit = mine[:, :, None] & (rank[:, :, None] == jnp.arange(capacity, dtype=jnp.int32))
    return jnp.sum(jnp.where(hit, row[:, :, None], 0), axis=1)


def plan_receives(targets, local_blocks, capacity):
    owner = targets.reshape(-1) // local_blocks
    order = jnp.arange(owner.shape[0], dtype=jnp.int32)
    same = (owner[:, None] == owner[None, :]) & (order[None, :] < order[:, None])
    return owner * capacity + jnp.sum(same.astype(jnp.int32), axis=1)


def group_rows(head, b, part):
    for i in range(TALL // BLOCK):
        group = head * GROUP + part * (TALL // BLOCK) + i
        yield i, (pl.ds(b * BLOCK, BLOCK), pl.ds(group * DH, DH))


def ahead(runs, score, finish):
    scores = score(*runs[0])
    for now, later in zip(runs, runs[1:] + [None], strict=True):
        held, scores = scores, score(*later) if later else None
        finish(*now, held)


def near_kernel(where_ref, q_ref, k_ref, v_ref, pk_ref, pv_ref, out_ref, log_ref):
    blocks = k_ref.shape[2] // BLOCK
    heads = k_ref.shape[3] // DH
    lane = lax.broadcasted_iota(jnp.int32, (BLOCK, DH), 1)
    logs = [jnp.zeros((BLOCK, DH), jnp.float32) for _ in range(blocks)]

    def load(ref, prev_ref, head, b):
        own, before = pl.ds(b * BLOCK, BLOCK), pl.ds((b - 1) * BLOCK, BLOCK)
        columns = pl.ds(head * DH, DH)
        prev = prev_ref[0, 0, :, columns] if b == 0 else ref[0, 0, before, columns]
        return jnp.concatenate([ref[0, 0, own, columns], prev], axis=0)

    def score(head, b, part):
        q = jnp.concatenate([q_ref[at] for _, at in group_rows(head, b, part)], axis=0)
        keys = load(k_ref, pk_ref, head, b)
        scores = lax.dot_general(q, keys, (((1,), (1,)), ((), ())), preferred_element_type=jnp.float32)
        if b == 0:
            column = lax.broadcasted_iota(jnp.int32, (1, 2 * BLOCK), 1)
            scores = jnp.where((column >= BLOCK) & (where_ref[0] == 1), -1e30, scores)
        return scores

    def finish(head, b, part, scores):
        highest = jnp.max(scores, axis=-1, keepdims=True)
        raised = jnp.exp2((scores - highest) * EXP2_SCALE)
        total = jnp.sum(raised, axis=-1, keepdims=True)
        log = highest * EXP2_SCALE + jnp.log2(total)
        values = load(v_ref, pv_ref, head, b)
        result = jnp.dot(raised.astype(jnp.bfloat16), values, preferred_element_type=jnp.float32) * (1.0 / total)
        for i, at in group_rows(head, b, part):
            rows = slice(i * BLOCK, (i + 1) * BLOCK)
            out_ref[at] = result[rows]
            logs[b] = jnp.where(lane == head * GROUP + part * (TALL // BLOCK) + i, log[rows], logs[b])

    ahead([(h, b, p) for h in range(heads) for b in range(blocks) for p in range(GROUP * BLOCK // TALL)], score, finish)
    for b in range(blocks):
        log_ref[pl.ds(b * BLOCK, BLOCK)] = logs[b]


def far_kernel(place_ref, where_ref, q_ref, near_ref, log_ref, *rest):
    sorted_refs, out_ref = rest[:-1], rest[-1]
    blocks = q_ref.shape[0] // BLOCK
    heads = q_ref.shape[1] // (GROUP * DH)
    lane = lax.broadcasted_iota(jnp.int32, (BLOCK, DH), 1)

    def load(head, b, kind):
        return sorted_refs[2 * (head * blocks + b) + kind][0, 0]

    def score(head, b, part):
        q = jnp.concatenate([q_ref[at] for _, at in group_rows(head, b, part)], axis=0)
        return lax.dot_general(
            q, load(head, b, 0), (((1,), (1,)), ((), ())), preferred_element_type=jnp.float32
        )

    def finish(head, b, part, scores):
        spots = list(group_rows(head, b, part))
        picks = [
            jnp.where(lane == head * GROUP + part * (TALL // BLOCK) + i, log_ref[at[0]], 0.0) for i, at in spots
        ]
        log = jnp.sum(jnp.concatenate(picks, axis=0), axis=-1, keepdims=True)
        near = jnp.concatenate([near_ref[at] for _, at in spots], axis=0)
        highest = jnp.maximum(jnp.max(scores, axis=-1, keepdims=True) * EXP2_SCALE, log)
        raised = jnp.exp2(scores * EXP2_SCALE - highest)
        share = jnp.exp2(log - highest)
        scale = 1.0 / (share + jnp.sum(raised, axis=-1, keepdims=True))
        far = jnp.dot(raised.astype(jnp.bfloat16), load(head, b, 1), preferred_element_type=jnp.float32)
        result = (near * (share * scale) + far * scale).astype(jnp.bfloat16)
        for i, at in spots:
            out_ref[at] = result[i * BLOCK : (i + 1) * BLOCK]

    ahead([(h, b, p) for h in range(heads) for b in range(blocks) for p in range(GROUP * BLOCK // TALL)], score, finish)


def attend(place, where, queries, own, prev, arrived):
    tokens, columns = queries.shape
    blocks = tokens // BLOCK
    step = 2
    width = step * GROUP * DH
    steps = own.shape[3] // (step * DH)

    def kv_spec(rows, kind, at):
        def index(h, where):
            return (where[1] ^ kind, (h // steps) ^ where[at], 0, h % steps)

        return pl.BlockSpec((1, 1, rows, step * DH), index)

    def sorted_spec(item, kind):
        return pl.BlockSpec(
            (1, 1, BLOCK, DH), lambda h, place, where: (place[h * step * blocks + item], kind, 0, 0)
        )

    near, logs = pl.pallas_call(
        near_kernel,
        grid_spec=pltpu.PrefetchScalarGridSpec(
            num_scalar_prefetch=1,
            grid=(KVH // step,),
            in_specs=[
                pl.BlockSpec((tokens, width), lambda h, where: (0, h)),
                kv_spec(tokens, 0, 2),
                kv_spec(tokens, 1, 2),
                kv_spec(BLOCK, 0, 3),
                kv_spec(BLOCK, 1, 3),
            ],
            out_specs=[
                pl.BlockSpec((tokens, width), lambda h, where: (0, h)),
                pl.BlockSpec((tokens, DH), lambda h, where: (0, h)),
            ],
        ),
        out_shape=[
            jax.ShapeDtypeStruct(queries.shape, jnp.float32),
            jax.ShapeDtypeStruct((tokens, KVH // step * DH), jnp.float32),
        ],
        cost_estimate=pl.CostEstimate(
            flops=8 * tokens * columns * BLOCK, bytes_accessed=8 * tokens * columns, transcendentals=2 * tokens * columns
        ),
        compiler_params=pltpu.CompilerParams(vmem_limit_bytes=24 * 1024 * 1024),
    )(where, queries, own, own, prev, prev)
    q_spec = pl.BlockSpec((tokens, width), lambda h, place, where: (0, h))
    return pl.pallas_call(
        far_kernel,
        grid_spec=pltpu.PrefetchScalarGridSpec(
            num_scalar_prefetch=2,
            grid=(KVH // step,),
            in_specs=[
                q_spec,
                q_spec,
                pl.BlockSpec((tokens, DH), lambda h, place, where: (0, h)),
                *[sorted_spec(item, kind) for item in range(step * blocks) for kind in range(2)],
            ],
            out_specs=q_spec,
        ),
        out_shape=jax.ShapeDtypeStruct(queries.shape, jnp.bfloat16),
        cost_estimate=pl.CostEstimate(
            flops=4 * tokens * columns * BLOCK, bytes_accessed=8 * tokens * columns, transcendentals=tokens * columns
        ),
        compiler_params=pltpu.CompilerParams(vmem_limit_bytes=24 * 1024 * 1024),
    )(place, where, queries, near, logs, *([arrived] * (2 * step * blocks)))


def local_gathered(tokens, queries, key_weight, value_weight, sorted_blocks):
    local_blocks = tokens.shape[1] // BLOCK
    devices = lax.axis_size("seq")
    me = lax.axis_index("seq")
    capacity = (KVH * local_blocks + devices - 1) // devices
    targets = sorted_blocks[0]
    wanted = plan_sends(lax.all_gather(targets, "seq", axis=0), me, local_blocks, capacity)
    place = plan_receives(targets, local_blocks, capacity)
    weights = lax.all_gather(
        jnp.concatenate([key_weight, value_weight], axis=1), ("fsdp", "seq"), axis=0, tiled=True
    )
    packed = jnp.dot(tokens[0], weights, preferred_element_type=jnp.float32).astype(jnp.bfloat16)
    own = jnp.stack([packed[:, : KVH * DH], packed[:, KVH * DH :]])[:, None]
    prev = lax.ppermute(own[:, :, -BLOCK:], "seq", [(i, i + 1) for i in range(devices - 1)])
    table = own.reshape(2, local_blocks, BLOCK, KVH, DH).transpose(3, 1, 0, 2, 4)
    replies = jnp.take(table.reshape(-1, 2, BLOCK, DH), wanted.reshape(-1), axis=0)
    arrived = lax.all_to_all(replies, "seq", split_axis=0, concat_axis=0, tiled=True)
    zero = jnp.zeros_like(me)
    where = jnp.stack([(me == 0).astype(jnp.int32), zero, zero, zero])
    return attend(place, where, queries[0], own, prev, arrived)[None]


def project_kernel(runs, arrays, pieces, place_ref, *refs):
    token_refs, array_refs = refs[:runs], refs[runs : runs + arrays]
    out_refs, (tokens, weights, token_sems, piece_sems) = refs[runs + arrays : -4], refs[-4:]
    depth = weights.shape[0] // len(pieces)
    tall = out_refs[0].shape[0] // 2
    arrivals, copies, start = [], [], 0
    for i, (array, first) in enumerate(pieces):
        rows = pl.ds(pl.multiple_of(place_ref[i] * depth, depth), depth)
        source = array_refs[array].at[pl.ds(first, depth)]
        arrivals.append(pltpu.make_async_copy(source, weights.at[rows], piece_sems.at[i]))
    for i, ref in enumerate(token_refs):
        rows = ref.shape[0]
        copy = pltpu.make_async_copy(ref, tokens.at[pl.ds(start, rows)], token_sems.at[i])
        copies.append((copy, start // tall))
        start += rows
    for copy in arrivals:
        copy.start()
    for copy, _ in copies:
        copy.start()
    for copy in arrivals:
        copy.wait()
    for i in range(2 * len(out_refs)):
        for copy, of in copies:
            if of == i:
                copy.wait()
        product = jnp.dot(tokens[i * tall : (i + 1) * tall], weights[...], preferred_element_type=jnp.float32)
        out_refs[i // 2][i % 2 * tall : (i % 2 + 1) * tall] = product.astype(jnp.bfloat16)


def project(token_runs, arrays, pieces, places):
    tokens = sum(run.shape[0] for run in token_runs)
    depth, width = token_runs[0].shape[1], arrays[0].shape[1]
    anywhere = pl.BlockSpec(memory_space=pl.ANY)
    return pl.pallas_call(
        functools.partial(project_kernel, len(token_runs), len(arrays), pieces),
        grid_spec=pltpu.PrefetchScalarGridSpec(
            num_scalar_prefetch=1,
            grid=(),
            in_specs=[anywhere] * (len(token_runs) + len(arrays)),
            out_specs=[pl.BlockSpec(memory_space=pltpu.VMEM)] * 2,
            scratch_shapes=[
                pltpu.VMEM((tokens, depth), jnp.bfloat16),
                pltpu.VMEM((depth, width), jnp.bfloat16),
                pltpu.SemaphoreType.DMA((len(token_runs),)),
                pltpu.SemaphoreType.DMA((len(pieces),)),
            ],
        ),
        out_shape=[jax.ShapeDtypeStruct((tokens // 2, width), jnp.bfloat16)] * 2,
        cost_estimate=pl.CostEstimate(
            flops=2 * tokens * depth * width, bytes_accessed=2 * (tokens + width) * depth, transcendentals=0
        ),
        compiler_params=pltpu.CompilerParams(vmem_limit_bytes=60 * 1024 * 1024),
    )(places, *token_runs, *arrays)


def pack_kernel(row_ref, part_ref, *refs):
    half_refs, out_ref, table = refs[:4], refs[4], refs[5]
    heads = table.shape[3] // DH
    blocks = table.shape[2] // BLOCK
    for i, ref in enumerate(half_refs):
        table[i // 2, i % 2] = ref[...]
    for i in range(row_ref.shape[0]):
        head, block = row_ref[i] // blocks, row_ref[i] % blocks
        for kind in range(2):
            out_ref[i, kind] = table[
                part_ref[0] ^ kind,
                (head // heads) ^ part_ref[1],
                pl.ds(pl.multiple_of(block * BLOCK, BLOCK), BLOCK),
                pl.ds(pl.multiple_of((head % heads) * DH, DH), DH),
            ]


def pack(rows, part, halves):
    return pl.pallas_call(
        pack_kernel,
        grid_spec=pltpu.PrefetchScalarGridSpec(
            num_scalar_prefetch=2,
            grid=(),
            in_specs=[pl.BlockSpec(memory_space=pltpu.VMEM)] * 4,
            out_specs=pl.BlockSpec(memory_space=pltpu.VMEM),
            scratch_shapes=[pltpu.VMEM((2, 2, *halves[0].shape), jnp.bfloat16)],
        ),
        out_shape=jax.ShapeDtypeStruct((rows.shape[0], 2, BLOCK, DH), jnp.bfloat16),
        compiler_params=pltpu.CompilerParams(vmem_limit_bytes=16 * 1024 * 1024),
    )(rows, part, *halves)


def local_split(tokens, queries, key_weight, value_weight, sorted_blocks):
    y, x, z, c = [lax.axis_index(name) for name in ("y", "x", "z", "c")]
    chips = lax.axis_size("z")
    devices = 2 * chips
    me = 2 * z + c
    local_blocks = tokens.shape[1] // BLOCK
    capacity = (KVH * local_blocks + devices - 1) // devices
    half = KVH * DH // 2
    targets = sorted_blocks[0]

    near = jnp.where(x == 0, key_weight, value_weight)
    away = jnp.where(x == 0, value_weight, key_weight)

    def part(weight, core):
        return lax.dynamic_slice_in_dim(weight, core * half, half, 1)

    def along(axis, step):
        count = lax.axis_size(axis)
        return lambda value: lax.ppermute(value, axis, [(i, (i + step) % count) for i in range(count)])

    over_x, over_y, over_c, up, down = along("x", 1), along("y", 1), along("c", 1), along("z", 1), along("z", -1)

    def over_xc(value):
        return lax.ppermute(value, ("x", "c"), [(i, 3 - i) for i in range(4)])

    def by_core(same_core, other_core):
        pair = jnp.stack([same_core, other_core])
        return jnp.where(c == 0, pair, pair[::-1])

    rows = key_weight.shape[0]
    notes = jnp.zeros((16, half), jnp.bfloat16).at[0, : targets.size].set(targets.reshape(-1).astype(jnp.bfloat16))
    from_x, from_xc = over_x(part(away, c)), over_xc(part(away, 1 - c))
    from_c = over_c(jnp.concatenate([part(near, 1 - c), notes]))
    ours = by_core(part(near, c), from_c[:rows]).reshape(-1, half)
    theirs = by_core(from_x, from_xc).reshape(-1, half)
    notes = by_core(notes[:1], from_c[rows : rows + 1]).reshape(-1, half)
    unit = jnp.concatenate([ours, theirs, notes, jnp.zeros((14, half), jnp.bfloat16)])

    early, late = jnp.split(tokens[0], 2)
    early, late, unit = lax.optimization_barrier((early, late, unit))
    x_early = over_x(early)
    x_late = over_x(late)
    c_tokens = over_c(tokens[0])

    deep = 2 * rows
    from_up, from_down = up(unit), down(unit)
    y_unit = over_y(unit)
    from_up, y_unit = lax.optimization_barrier((from_up, y_unit))
    y_up = over_y(from_up)
    from_down, y_up, x_early = lax.optimization_barrier((from_down, y_up, x_early))
    y_down = over_y(from_down)
    far_ours, far_theirs = up(from_up[:deep]), down(from_down[deep:])
    far_ours, y_down = lax.optimization_barrier((far_ours, y_down))
    y_ours, y_theirs = over_y(far_ours), over_y(far_theirs)
    x_late, far_theirs, y_ours, y_theirs = lax.optimization_barrier((x_late, far_theirs, y_ours, y_theirs))
    arrays, pieces, places = [], [], []
    for value, across, from_z, kinds in (
        (unit, y_unit, z, (0, 1)),
        (from_up, y_up, z - 1, (0, 1)),
        (from_down, y_down, z + 1, (0, 1)),
        (far_ours, y_ours, z + 2, (0,)),
        (far_theirs, y_theirs, z + 2, (1,)),
    ):
        for array, from_y in ((value, y), (across, 1 - y)):
            for i, kind in enumerate(kinds):
                pieces.append((len(arrays), i * deep))
                places.append((from_y * 2 + (x ^ kind)) * chips + from_z % chips)
            arrays.append(array)
    places = jnp.stack(places).astype(jnp.int32)
    xc_early = over_c(x_early)
    xc_late = over_c(x_late)

    notes = jnp.stack([unit[2 * deep :], from_up[2 * deep :], from_down[2 * deep :], far_theirs[deep:]])
    notes = notes[:, :2, : targets.size].astype(jnp.int32)
    from_z = (z + jnp.array([0, -1, 1, 2], jnp.int32)) % chips
    own_row = from_z[:, None] == jnp.arange(chips, dtype=jnp.int32)[None]
    all_targets = jnp.sum(jnp.where(own_row[:, :, None, None], notes[:, None], 0), axis=0)
    wanted = plan_sends(all_targets.reshape(devices, *targets.shape), me, local_blocks, capacity).reshape(-1)
    place = plan_receives(targets, local_blocks, capacity)

    x_sent, xc_sent = project([x_early, x_late, xc_early, xc_late], arrays, pieces, places)
    x_same, x_diff = over_x(x_sent), over_xc(xc_sent)
    own_tokens, x_sent = lax.optimization_barrier((tokens[0], x_sent))
    same, sent = project([own_tokens, c_tokens], arrays, pieces, places)
    halves = [same, over_c(sent), x_same, x_diff]
    replies = pack(wanted, jnp.stack([x, c]).astype(jnp.int32), halves)
    arrived = lax.all_to_all(replies, ("z", "c"), split_axis=0, concat_axis=0, tiled=True)

    own = jnp.stack(halves).reshape(2, 2, *same.shape)
    prev = lax.ppermute(own[:, :, -BLOCK:], ("z", "c"), [(i, i + 1) for i in range(devices - 1)])
    where = jnp.stack([(me == 0).astype(jnp.int32), x, c, 1 - c]).astype(jnp.int32)
    return attend(place, where, queries[0], own, prev, arrived)[None]


def solution(mesh):
    fsdp, seq = mesh.shape["fsdp"], mesh.shape["seq"]
    if (fsdp, seq) == (4, 8):
        mesh = Mesh(mesh.devices.reshape(2, 2, seq // 2, 2), ("y", "x", "z", "c"))
        step, fsdp, seq = local_split, ("y", "x"), ("z", "c")
    else:
        step, fsdp, seq = local_gathered, ("fsdp",), ("seq",)
    placed = (
        P(fsdp, seq, None),
        P(fsdp, seq, None),
        P((*fsdp, *seq), None),
        P((*fsdp, *seq), None),
        P(fsdp, None, seq),
    )
    return jax.shard_map(step, mesh=mesh, in_specs=placed, out_specs=P(fsdp, seq, None), check_vma=False)
```

time: 199 us -> 151 us (0.76)
  waiting for transfers between devices: 133 us -> 82.2 us
  starting transfers between devices: 6.97 us -> 23.8 us
  Pallas kernels: 11.9 us -> 28.5 us
  between operations: 13.5 us -> 0.34 us
  blocking collectives: 9.27 us -> 0 us
  matrix products: 8.25 us -> 0 us
    all_gather x1 -> x0, waiting for transfers between devices: 107 us -> none  [project(): lax.all_gather(jnp.concatenate([key_weight, value_weight], axis=1), ('fsd...]
    ppermute x1 -> x21, waiting for transfers between devices: 26.2 us -> 82.2 us  [the longest x18 51.3 us: along(): lax.ppermute(value, axis, [(i, (i + step) % count) for i in range(count)])]
    pallas_call x1 -> x5, Pallas kernels: 11.9 us -> 28.5 us  [the longest x2 14.4 us: project(): pl.pallas_call(functools.partial(project_kernel, len(token_runs), len(arr...]
    ppermute x1 -> x21, starting transfers between devices: 2.06 us -> 18 us  [the longest x18 15.9 us: along(): lax.ppermute(value, axis, [(i, (i + step) % count) for i in range(count)])]
    all_gather x1 -> x0, blocking collectives: 9.27 us -> none  [local(): lax.all_gather(targets, 'seq', axis=0)]
    dot_general x1 -> x0, matrix products: 8.25 us -> none  [project(): jnp.dot(token_rows, weights, preferred_element_type=jnp.float32)]
    split x0 -> x1, local copies, waits for them, and re-layouts: none -> 3.12 us  [local_split(): early, late = jnp.split(tokens[0], 2)]
    concatenate x2, other arithmetic: 3.12 us -> 0.18 us  [the longest x1 0.17 us: local_split(): jnp.concatenate([ours, theirs, notes, jnp.zeros((14, half), jnp.bfloat16)])]
  transfers between devices with their start and end apart: 3 -> 22, of which waited for: 2 -> 12; matrix products, arithmetic and copies ran while one was open for 1% -> 5% of each run, Pallas kernels for 0% -> 13%
where the time goes in v3:
time: 151 us
  waiting for transfers between devices  82.2 us (54%)
  Pallas kernels  28.5 us (19%)
  starting transfers between devices  23.8 us (16%)
  local copies, waits for them, and re-layouts  12.1 us (8%)
  other arithmetic  3.7 us (2%)
    ppermute x18, waiting for transfers between devices, along(): lax.ppermute(value, axis, [(i, (i + step) % count) for i in range(count)])  51.3 us
    ppermute x1, waiting for transfers between devices, local_split(): lax.ppermute(own[:, :, -BLOCK:], ('z', 'c'), [(i, i + 1) for i in range(d...  25.7 us
    ppermute x18, starting transfers between devices, along(): lax.ppermute(value, axis, [(i, (i + step) % count) for i in range(count)])  15.9 us
    pallas_call x2, Pallas kernels, project(): pl.pallas_call(functools.partial(project_kernel, len(token_runs), len(arr...  14.4 us
    unnamed x37, local copies, waits for them, and re-layouts  7.56 us
    pallas_call x1, Pallas kernels, attend(): pl.pallas_call(far_kernel, grid_spec=pltpu.PrefetchScalarGridSpec(num_sca...  6.76 us
    all_to_all x1, starting transfers between devices, local_split(): lax.all_to_all(replies, ('z', 'c'), split_axis=0, concat_axis=0, tiled=True)  5.83 us
    pallas_call x1, Pallas kernels, attend(): pl.pallas_call(near_kernel, grid_spec=pltpu.PrefetchScalarGridSpec(num_sc...  5.35 us
  transfers between devices with their start and end apart: 22, of which 12 were waited for; matrix products, arithmetic and copies ran while one was open for 5% of the time, Pallas kernels for 13%

profile of v3, /device:TPU:16, one launch (start us, length us, event | category | flops | bytes accessed | tf_op | source)
XLA Modules:
  0.0 150.7 jit_solution(13246938146136371084)
XLA Ops:
  0.0 1.1 broadcast_select_fusion
  1.1 1.6 %collective-permute-start.1 = (bf16[128,512]{1,0:T(8,128)(2,1)S(1)}, bf16[128,512]{1,0:T(8,128)(2,1)S(1)}, u32[]{:S(2)}, u32[]{:S(2)}) collective-permute-start(bf16[128,512]{1,0:T(8,128)(2,1)S(1)} %get-tuple-element.67), channel_id=1, source_target_pairs={{0,8},{8,0},{1,9},{9,1},{2,10},{10,2},{3,11},{11,3},{4,12},{12,4},... | collective-permute-start | bytes 393224 | tf_op jit(solution)/shard_map/ppermute | solution.py:315
  3.6 3.1 %slice_bitcast_fusion = (bf16[128,4096]{1,0:T(8,128)(2,1)}, bf16[128,4096]{1,0:T(8,128)(2,1)}) fusion(bf16[1,256,4096]{2,1,0:T(8,128)(2,1)} %param.8), kind=kLoop, calls=%fused_computation.1 | loop fusion | bytes 4194304 | tf_op jit(solution)/shard_map/split | solution.py:335
  7.2 1.3 collective-permute-done.2
  9.1 1.6 %collective-permute-start.5 = (bf16[528,512]{1,0:T(8,128)(2,1)S(1)}, bf16[528,512]{1,0:T(8,128)(2,1)S(1)}, u32[]{:S(2)}, u32[]{:S(2)}) collective-permute-start(bf16[528,512]{1,0:T(8,128)(2,1)S(1)} %maximum_maximum_fusion.refs_4_.refs_2_), channel_id=1, source_target_pairs={{0,16},{16,0},{1,17},{17,1},{2,18},{18,2},{3,19},{19,3},{4,20},{20... | collective-permute-start | bytes 1622024 | tf_op jit(solution)/shard_map/ppermute | solution.py:315
  10.6 1.6 %collective-permute-start.4 = (bf16[528,512]{1,0:T(8,128)(2,1)S(1)}, bf16[528,512]{1,0:T(8,128)(2,1)S(1)}, u32[]{:S(2)}, u32[]{:S(2)}) collective-permute-start(bf16[528,512]{1,0:T(8,128)(2,1)S(1)} %maximum_maximum_fusion.refs_4_.refs_2_), channel_id=1, source_target_pairs={{0,2},{2,4},{4,6},{6,0},{1,3},{3,5},{5,7},{7,1},{8,10},{10,12},{12... | collective-permute-start | bytes 1622024 | tf_op jit(solution)/shard_map/ppermute | solution.py:315
  12.2 1.1 collective-permute-start.7
  13.8 10.1 %collective-permute-done.5.refs_5_.refs_3_ = bf16[528,512]{1,0:T(8,128)(2,1)S(1)} collective-permute-done((bf16[528,512]{1,0:T(8,128)(2,1)S(1)}, bf16[528,512]{1,0:T(8,128)(2,1)S(1)}, u32[]{:S(2)}, u32[]{:S(2)}) %collective-permute-start.5) | collective-permute-done | bytes 540704 | tf_op jit(solution)/shard_map/ppermute | solution.py:315
  23.9 12.8 %collective-permute-done.4.refs_6_.refs_4_ = bf16[528,512]{1,0:T(8,128)(2,1)S(1)} collective-permute-done((bf16[528,512]{1,0:T(8,128)(2,1)S(1)}, bf16[528,512]{1,0:T(8,128)(2,1)S(1)}, u32[]{:S(2)}, u32[]{:S(2)}) %collective-permute-start.4) | collective-permute-done | bytes 540704 | tf_op jit(solution)/shard_map/ppermute | solution.py:315
  37.2 1.5 collective-permute-start.8
  38.7 11.4 %collective-permute-done.6.refs_7_.refs_5_ = bf16[528,512]{1,0:T(8,128)(2,1)S(1)} collective-permute-done((bf16[528,512]{1,0:T(8,128)(2,1)S(1)}, bf16[528,512]{1,0:T(8,128)(2,1)S(1)}, u32[]{:S(2)}, u32[]{:S(2)}) %collective-permute-start.6) | collective-permute-done | bytes 540704 | tf_op jit(solution)/shard_map/ppermute | solution.py:315
  50.2 1.6 %collective-permute-start.10 = (bf16[256,512]{1,0:T(8,128)(2,1)S(1)}, bf16[256,512]{1,0:T(8,128)(2,1)S(1)}, u32[]{:S(2)}, u32[]{:S(2)}) collective-permute-start(bf16[256,512]{1,0:T(8,128)(2,1)S(1)} %slice.55), channel_id=1, source_target_pairs={{0,2},{2,4},{4,6},{6,0},{1,3},{3,5},{5,7},{7,1},{8,10},{10,12},{12... | collective-permute-start | bytes 786440 | tf_op jit(solution)/shard_map/ppermute | solution.py:315
  52.5 6.8 %collective-permute-done.9.refs_12_.refs_10_ = bf16[272,512]{1,0:T(8,128)(2,1)S(1)} collective-permute-done((bf16[272,512]{1,0:T(8,128)(2,1)S(1)}, bf16[272,512]{1,0:T(8,128)(2,1)S(1)}, u32[]{:S(2)}, u32[]{:S(2)}) %collective-permute-start.9) | collective-permute-done | bytes 278560 | tf_op jit(solution)/shard_map/ppermute | solution.py:315
  59.3 2.0 %collective-permute-start.13 = (bf16[272,512]{1,0:T(8,128)(2,1)S(1)}, bf16[272,512]{1,0:T(8,128)(2,1)}, u32[]{:S(2)}, u32[]{:S(2)}) collective-permute-start(bf16[272,512]{1,0:T(8,128)(2,1)S(1)} %collective-permute-done.9.refs_12_.refs_10_), channel_id=1, source_target_pairs={{0,16},{16,0},{1,17},{17,1},{2,18},{18,2},{3,19},{19,3},{4,20},{20... | collective-permute-start | bytes 835592 | tf_op jit(solution)/shard_map/ppermute | solution.py:315
  61.3 2.2 %collective-permute-done.11.refs_9_.refs_7_ = bf16[528,512]{1,0:T(8,128)(2,1)S(1)} collective-permute-done((bf16[528,512]{1,0:T(8,128)(2,1)S(1)}, bf16[528,512]{1,0:T(8,128)(2,1)S(1)}, u32[]{:S(2)}, u32[]{:S(2)}) %collective-permute-start.11) | collective-permute-done | bytes 540704 | tf_op jit(solution)/shard_map/ppermute | solution.py:315
  65.0 1.5 %collective-permute-done.13.refs_13_.refs_11_ = bf16[272,512]{1,0:T(8,128)(2,1)} collective-permute-done((bf16[272,512]{1,0:T(8,128)(2,1)S(1)}, bf16[272,512]{1,0:T(8,128)(2,1)}, u32[]{:S(2)}, u32[]{:S(2)}) %collective-permute-start.13) | collective-permute-done | bytes 278560 | tf_op jit(solution)/shard_map/ppermute | solution.py:315
  66.6 3.4 %collective-permute-done.12.refs_11_.refs_9_ = bf16[256,512]{1,0:T(8,128)(2,1)} collective-permute-done((bf16[256,512]{1,0:T(8,128)(2,1)S(1)}, bf16[256,512]{1,0:T(8,128)(2,1)}, u32[]{:S(2)}, u32[]{:S(2)}) %collective-permute-start.12) | collective-permute-done | bytes 262176 | tf_op jit(solution)/shard_map/ppermute | solution.py:315
  70.3 2.7 %collective-permute-done.15.refs_3_ = bf16[128,4096]{1,0:T(8,128)(2,1)} collective-permute-done((bf16[128,4096]{1,0:T(8,128)(2,1)}, bf16[128,4096]{1,0:T(8,128)(2,1)}, u32[]{:S(2)}, u32[]{:S(2)}) %collective-permute-start.15) | collective-permute-done | bytes 1048608 | tf_op jit(solution)/shard_map/ppermute | solution.py:315
  73.0 7.6 %shard_map.64 = (bf16[256,512]{1,0:T(8,128)(2,1)}, bf16[256,512]{1,0:T(8,128)(2,1)}) custom-call(s32[16]{0:T(128)} %stack.153.place_ref, bf16[128,4096]{1,0:T(8,128)(2,1)} %collective-permute-done.7.refs_0_, bf16[128,4096]{1,0:T(8,128)(2,1)} %collective-permute-done.8.refs_1_, bf16[128,4096]{1,0:T(8,128)(2,1)} %collective-permute-done.14.refs_2_, ...), custom_call_target="tpu_custom_call" | custom-call | flops 2147483648 | bytes 8388608 | tf_op jit(solution)/shard_map/pallas_call | solution.py:243
  80.6 1.6 %collective-permute-start.18 = (bf16[256,512]{1,0:T(8,128)(2,1)}, bf16[256,512]{1,0:T(8,128)(2,1)S(1)}, u32[]{:S(2)}, u32[]{:S(2)}) collective-permute-start(bf16[256,512]{1,0:T(8,128)(2,1)} %get-tuple-element.52), channel_id=1, source_target_pairs={{0,8},{8,0},{1,9},{9,1},{2,10},{10,2},{3,11},{11,3},{4,12},{12,4},... | collective-permute-start | bytes 786440 | tf_op jit(solution)/shard_map/ppermute | solution.py:315
  82.1 6.9 %shard_map.65 = (bf16[256,512]{1,0:T(8,128)(2,1)}, bf16[256,512]{1,0:T(8,128)(2,1)}) custom-call(s32[16]{0:T(128)} %stack.153.place_ref, bf16[256,4096]{1,0:T(8,128)(2,1)} %bitcast.21.refs_0_, bf16[256,4096]{1,0:T(8,128)(2,1)} %collective-permute-done.16.refs_1_, bf16[528,512]{1,0:T(8,128)(2,1)} %copy-done.8, bf16[528,512]{1,0:T(8,128)(2,1)} %copy-done.11, ...), custom_call_target="tpu_custom_call" | custom-call | flops 2147483648 | bytes 8388608 | tf_op jit(solution)/shard_map/pallas_call | solution.py:243
  90.0 3.9 %collective-permute-done.19.refs_3_ = bf16[256,512]{1,0:T(8,128)(2,1)S(1)} collective-permute-done((bf16[256,512]{1,0:T(8,128)(2,1)}, bf16[256,512]{1,0:T(8,128)(2,1)S(1)}, u32[]{:S(2)}, u32[]{:S(2)}) %collective-permute-start.19) | collective-permute-done | bytes 262176 | tf_op jit(solution)/shard_map/ppermute | solution.py:320
  94.0 1.1 copy-done.4
  95.1 1.9 %shard_map.67 = bf16[16,2,128,128]{3,2,1,0:T(8,128)(2,1)} custom-call(s32[16]{0:T(128)S(1)} %reshape.249.row_ref, s32[2]{0:T(128)S(1)} %pad_add_fusion.1.part_ref, bf16[256,512]{1,0:T(8,128)(2,1)S(1)} %copy-done.4, bf16[256,512]{1,0:T(8,128)(2,1)S(1)} %collective-permute-done.17.refs_1_, bf16[256,512]{1,0:T(8,128)(2,1)S(1)} %collective-permute-done.18.refs_2_, ...), custom_call_target="tpu_custom_call" | custom-call | tf_op jit(solution)/shard_map/pallas_call | solution.py:283
  97.1 5.8 %all-to-all-start = ((bf16[16,2,128,128]{3,2,1,0:T(8,128)(2,1)}), bf16[16,2,128,128]{3,2,1,0:T(8,128)(2,1)S(1)}, u32[]{:S(2)}, u32[]{:S(2)}) async-start(bf16[16,2,128,128]{3,2,1,0:T(8,128)(2,1)} %shard_map.67), calls=%async_computation | async-start | bytes 2097152 | tf_op jit(solution)/shard_map/all_to_all | solution.py:383
  103.1 1.4 pad_maximum_fusion
  104.6 2.1 %collective-permute-start.20 = (bf16[2,2,128,512]{3,2,1,0:T(8,128)(2,1)S(1)}, bf16[2,2,128,512]{3,2,1,0:T(8,128)(2,1)S(1)}, u32[]{:S(2)}, u32[]{:S(2)}) collective-permute-start(bf16[2,2,128,512]{3,2,1,0:T(8,128)(2,1)S(1)} %slice.64), channel_id=1, source_target_pairs={{0,1},{1,2},{2,3},{3,4},{4,5},{5,6},{6,7},{8,9},{9,10},{10,11},{11... | collective-permute-start | bytes 1572872 | tf_op jit(solution)/shard_map/ppermute | solution.py:386
  106.8 25.7 %collective-permute-done.20.pk_ref.pv_ref = bf16[2,2,128,512]{3,2,1,0:T(8,128)(2,1)S(1)} collective-permute-done((bf16[2,2,128,512]{3,2,1,0:T(8,128)(2,1)S(1)}, bf16[2,2,128,512]{3,2,1,0:T(8,128)(2,1)S(1)}, u32[]{:S(2)}, u32[]{:S(2)}) %collective-permute-start.20) | collective-permute-done | bytes 524320 | tf_op jit(solution)/shard_map/ppermute | solution.py:386
  132.6 5.3 %shard_map.66 = (f32[256,4096]{1,0:T(8,128)S(1)}, f32[256,512]{1,0:T(8,128)S(1)}) custom-call(s32[4]{0:T(128)S(1)} %pad_add_fusion.where_ref, bf16[256,4096]{1,0:T(8,128)(2,1)S(1)} %bitcast.58, bf16[2,2,256,512]{3,2,1,0:T(8,128)(2,1)S(1)} %bitcast.56, bf16[2,2,256,512]{3,2,1,0:T(8,128)(2,1)S(1)} %bitcast.57, ...), custom_call_target="tpu_custom_call" | custom-call | flops 1073741824 | bytes 8388608 | tf_op jit(solution)/shard_map/pallas_call | solution.py:140
  138.0 2.0 %copy-done.1 = f32[256,4096]{1,0:T(8,128)} copy-done((f32[256,4096]{1,0:T(8,128)}, f32[256,4096]{1,0:T(8,128)S(1)}, u32[]{:S(2)}) %copy-start.1) | copy-done | bytes 4194328
  140.7 2.2 %copy-done.2 = f32[256,4096]{1,0:T(8,128)S(1)} copy-done((f32[256,4096]{1,0:T(8,128)S(1)}, f32[256,4096]{1,0:T(8,128)}, u32[]{:S(2)}) %copy-start.2) | copy-done | bytes 4194328
  144.0 6.8 %shard_map.68 = bf16[256,4096]{1,0:T(8,128)(2,1)} custom-call(s32[16]{0:T(128)S(1)} %multiply_add_fusion.place_ref, s32[4]{0:T(128)S(1)} %pad_add_fusion.where_ref, bf16[256,4096]{1,0:T(8,128)(2,1)S(1)} %bitcast.59, f32[256,4096]{1,0:T(8,128)S(1)} %copy-done.2, f32[256,512]{1,0:T(8,128)S(1)} %copy-done.7, ...), custom_call_target="tpu_custom_call" | custom-call | flops 536870912 | bytes 8388608 | tf_op jit(solution)/shard_map/pallas_call | solution.py:167
  (103 shorter events, 8.7 us)
Async XLA Ops:
  1.1 6.1 %collective-permute-start.1 = (bf16[128,512]{1,0:T(8,128)(2,1)S(1)}, bf16[128,512]{1,0:T(8,128)(2,1)S(1)}, u32[]{:S(2)}, u32[]{:S(2)}) collective-permute-start(bf16[128,512]{1,0:T(8,128)(2,1)S(1)} %get-tuple-element.67), channel_id=1, source_target_pairs={{0,8},{8,0},{1,9},{9,1},{2,10},{10,2},{3,11},{11,3},{4,12},{12,4},... | collective-permute-start | bytes 393224 | tf_op jit(solution)/shard_map/ppermute | solution.py:315
  2.7 5.8 %collective-permute-start.2 = (bf16[128,512]{1,0:T(8,128)(2,1)S(1)}, bf16[128,512]{1,0:T(8,128)(2,1)S(1)}, u32[]{:S(2)}, u32[]{:S(2)}) collective-permute-start(bf16[128,512]{1,0:T(8,128)(2,1)S(1)} %get-tuple-element.68), channel_id=1, source_target_pairs={{0,9},{1,8},{8,1},{9,0},{2,11},{3,10},{10,3},{11,2},{4,13},{5,12},... | collective-permute-start | bytes 393224 | tf_op jit(solution)/shard_map/ppermute | solution.py:320
  2.9 5.6 %collective-permute-start = (bf16[144,512]{1,0:T(8,128)(2,1)S(1)}, bf16[144,512]{1,0:T(8,128)(2,1)S(1)}, u32[]{:S(2)}, u32[]{:S(2)}) collective-permute-start(bf16[144,512]{1,0:T(8,128)(2,1)S(1)} %pad_maximum_fusion.3), channel_id=1, source_target_pairs={{0,1},{1,0},{2,3},{3,2},{4,5},{5,4},{6,7},{7,6},{8,9},{9,8},{10,11... | collective-permute-start | bytes 442376 | tf_op jit(solution)/shard_map/ppermute | solution.py:315
  8.6 41.6 %copy-start.17 = (s32[4]{0:T(128)S(1)}, s32[4]{0:T(128)}, u32[]{:S(2)}) copy-start(s32[4]{0:T(128)} %constant.159.clone) | copy-start | bytes 52
  9.0 63.9 %copy-start.8 = (bf16[528,512]{1,0:T(8,128)(2,1)}, bf16[528,512]{1,0:T(8,128)(2,1)S(1)}, u32[]{:S(2)}) copy-start(bf16[528,512]{1,0:T(8,128)(2,1)S(1)} %maximum_maximum_fusion.refs_4_.refs_2_) | copy-start | bytes 1622020
  9.1 14.8 %collective-permute-start.5 = (bf16[528,512]{1,0:T(8,128)(2,1)S(1)}, bf16[528,512]{1,0:T(8,128)(2,1)S(1)}, u32[]{:S(2)}, u32[]{:S(2)}) collective-permute-start(bf16[528,512]{1,0:T(8,128)(2,1)S(1)} %maximum_maximum_fusion.refs_4_.refs_2_), channel_id=1, source_target_pairs={{0,16},{16,0},{1,17},{17,1},{2,18},{18,2},{3,19},{19,3},{4,20},{20... | collective-permute-start | bytes 1622024 | tf_op jit(solution)/shard_map/ppermute | solution.py:315
  10.6 26.1 %collective-permute-start.4 = (bf16[528,512]{1,0:T(8,128)(2,1)S(1)}, bf16[528,512]{1,0:T(8,128)(2,1)S(1)}, u32[]{:S(2)}, u32[]{:S(2)}) collective-permute-start(bf16[528,512]{1,0:T(8,128)(2,1)S(1)} %maximum_maximum_fusion.refs_4_.refs_2_), channel_id=1, source_target_pairs={{0,2},{2,4},{4,6},{6,0},{1,3},{3,5},{5,7},{7,1},{8,10},{10,12},{12... | collective-permute-start | bytes 1622024 | tf_op jit(solution)/shard_map/ppermute | solution.py:315
  12.2 26.5 %collective-permute-start.7 = (bf16[128,4096]{1,0:T(8,128)(2,1)}, bf16[128,4096]{1,0:T(8,128)(2,1)}, u32[]{:S(2)}, u32[]{:S(2)}) collective-permute-start(bf16[128,4096]{1,0:T(8,128)(2,1)} %get-tuple-element.40), channel_id=1, source_target_pairs={{0,8},{8,0},{1,9},{9,1},{2,10},{10,2},{3,11},{11,3},{4,12},{12,4},... | collective-permute-start | bytes 3145736 | tf_op jit(solution)/shard_map/ppermute | solution.py:315
  13.3 25.4 %collective-permute-start.3 = (bf16[528,512]{1,0:T(8,128)(2,1)S(1)}, bf16[528,512]{1,0:T(8,128)(2,1)S(1)}, u32[]{:S(2)}, u32[]{:S(2)}) collective-permute-start(bf16[528,512]{1,0:T(8,128)(2,1)S(1)} %maximum_maximum_fusion.refs_4_.refs_2_), channel_id=1, source_target_pairs={{0,6},{2,0},{4,2},{6,4},{1,7},{3,1},{5,3},{7,5},{8,14},{10,8},{12,... | collective-permute-start | bytes 1622024 | tf_op jit(solution)/shard_map/ppermute | solution.py:315
  23.9 49.1 %copy-start.11 = (bf16[528,512]{1,0:T(8,128)(2,1)}, bf16[528,512]{1,0:T(8,128)(2,1)S(1)}, u32[]{:S(2)}) copy-start(bf16[528,512]{1,0:T(8,128)(2,1)S(1)} %collective-permute-done.5.refs_5_.refs_3_) | copy-start | bytes 1622020
  36.7 36.2 %copy-start.10 = (bf16[528,512]{1,0:T(8,128)(2,1)}, bf16[528,512]{1,0:T(8,128)(2,1)S(1)}, u32[]{:S(2)}) copy-start(bf16[528,512]{1,0:T(8,128)(2,1)S(1)} %collective-permute-done.4.refs_6_.refs_4_) | copy-start | bytes 1622020
  36.7 13.4 %collective-permute-start.6 = (bf16[528,512]{1,0:T(8,128)(2,1)S(1)}, bf16[528,512]{1,0:T(8,128)(2,1)S(1)}, u32[]{:S(2)}, u32[]{:S(2)}) collective-permute-start(bf16[528,512]{1,0:T(8,128)(2,1)S(1)} %collective-permute-done.4.refs_6_.refs_4_), channel_id=1, source_target_pairs={{0,16},{16,0},{1,17},{17,1},{2,18},{18,2},{3,19},{19,3},{4,20},{20... | collective-permute-start | bytes 1622024 | tf_op jit(solution)/shard_map/ppermute | solution.py:315
  37.2 27.8 %collective-permute-start.8 = (bf16[128,4096]{1,0:T(8,128)(2,1)}, bf16[128,4096]{1,0:T(8,128)(2,1)}, u32[]{:S(2)}, u32[]{:S(2)}) collective-permute-start(bf16[128,4096]{1,0:T(8,128)(2,1)} %get-tuple-element.42), channel_id=1, source_target_pairs={{0,8},{8,0},{1,9},{9,1},{2,10},{10,2},{3,11},{11,3},{4,12},{12,4},... | collective-permute-start | bytes 3145736 | tf_op jit(solution)/shard_map/ppermute | solution.py:315
  38.7 43.4 %collective-permute-start.16 = (bf16[256,4096]{1,0:T(8,128)(2,1)}, bf16[256,4096]{1,0:T(8,128)(2,1)}, u32[]{:S(2)}, u32[]{:S(2)}) collective-permute-start(bf16[256,4096]{1,0:T(8,128)(2,1)} %bitcast.21.refs_0_), channel_id=1, source_target_pairs={{0,1},{1,0},{2,3},{3,2},{4,5},{5,4},{6,7},{7,6},{8,9},{9,8},{10,11... | collective-permute-start | bytes 6291464 | tf_op jit(solution)/shard_map/ppermute | solution.py:315
  38.7 34.2 %copy-start.9 = (bf16[528,512]{1,0:T(8,128)(2,1)}, bf16[528,512]{1,0:T(8,128)(2,1)S(1)}, u32[]{:S(2)}) copy-start(bf16[528,512]{1,0:T(8,128)(2,1)S(1)} %collective-permute-done.3.refs_8_.refs_6_) | copy-start | bytes 1622020
  50.2 22.8 %copy-start.12 = (bf16[528,512]{1,0:T(8,128)(2,1)}, bf16[528,512]{1,0:T(8,128)(2,1)S(1)}, u32[]{:S(2)}) copy-start(bf16[528,512]{1,0:T(8,128)(2,1)S(1)} %collective-permute-done.6.refs_7_.refs_5_) | copy-start | bytes 1622020
  50.2 13.3 %collective-permute-start.11 = (bf16[528,512]{1,0:T(8,128)(2,1)S(1)}, bf16[528,512]{1,0:T(8,128)(2,1)S(1)}, u32[]{:S(2)}, u32[]{:S(2)}) collective-permute-start(bf16[528,512]{1,0:T(8,128)(2,1)S(1)} %collective-permute-done.3.refs_8_.refs_6_), channel_id=1, source_target_pairs={{0,16},{16,0},{1,17},{17,1},{2,18},{18,2},{3,19},{19,3},{4,20},{20... | collective-permute-start | bytes 1622024 | tf_op jit(solution)/shard_map/ppermute | solution.py:315
  50.2 11.1 %collective-permute-start.10 = (bf16[256,512]{1,0:T(8,128)(2,1)S(1)}, bf16[256,512]{1,0:T(8,128)(2,1)S(1)}, u32[]{:S(2)}, u32[]{:S(2)}) collective-permute-start(bf16[256,512]{1,0:T(8,128)(2,1)S(1)} %slice.55), channel_id=1, source_target_pairs={{0,2},{2,4},{4,6},{6,0},{1,3},{3,5},{5,7},{7,1},{8,10},{10,12},{12... | collective-permute-start | bytes 786440 | tf_op jit(solution)/shard_map/ppermute | solution.py:315
  51.9 7.4 %collective-permute-start.9 = (bf16[272,512]{1,0:T(8,128)(2,1)S(1)}, bf16[272,512]{1,0:T(8,128)(2,1)S(1)}, u32[]{:S(2)}, u32[]{:S(2)}) collective-permute-start(bf16[272,512]{1,0:T(8,128)(2,1)S(1)} %slice.54), channel_id=1, source_target_pairs={{0,6},{2,0},{4,2},{6,4},{1,7},{3,1},{5,3},{7,5},{8,14},{10,8},{12,... | collective-permute-start | bytes 835592 | tf_op jit(solution)/shard_map/ppermute | solution.py:315
  59.3 13.7 %copy-start.14 = (bf16[272,512]{1,0:T(8,128)(2,1)}, bf16[272,512]{1,0:T(8,128)(2,1)S(1)}, u32[]{:S(2)}) copy-start(bf16[272,512]{1,0:T(8,128)(2,1)S(1)} %collective-permute-done.9.refs_12_.refs_10_) | copy-start | bytes 835588
  59.3 7.3 %collective-permute-start.13 = (bf16[272,512]{1,0:T(8,128)(2,1)S(1)}, bf16[272,512]{1,0:T(8,128)(2,1)}, u32[]{:S(2)}, u32[]{:S(2)}) collective-permute-start(bf16[272,512]{1,0:T(8,128)(2,1)S(1)} %collective-permute-done.9.refs_12_.refs_10_), channel_id=1, source_target_pairs={{0,16},{16,0},{1,17},{17,1},{2,18},{18,2},{3,19},{19,3},{4,20},{20... | collective-permute-start | bytes 835592 | tf_op jit(solution)/shard_map/ppermute | solution.py:315
  61.3 11.7 %copy-start.15 = (bf16[256,512]{1,0:T(8,128)(2,1)}, bf16[256,512]{1,0:T(8,128)(2,1)S(1)}, u32[]{:S(2)}) copy-start(bf16[256,512]{1,0:T(8,128)(2,1)S(1)} %collective-permute-done.10.refs_10_.refs_8_) | copy-start | bytes 786436
  63.5 6.5 %collective-permute-start.12 = (bf16[256,512]{1,0:T(8,128)(2,1)S(1)}, bf16[256,512]{1,0:T(8,128)(2,1)}, u32[]{:S(2)}, u32[]{:S(2)}) collective-permute-start(bf16[256,512]{1,0:T(8,128)(2,1)S(1)} %collective-permute-done.10.refs_10_.refs_8_), channel_id=1, source_target_pairs={{0,16},{16,0},{1,17},{17,1},{2,18},{18,2},{3,19},{19,3},{4,20},{20... | collective-permute-start | bytes 786440 | tf_op jit(solution)/shard_map/ppermute | solution.py:315
  65.0 5.3 %collective-permute-start.14 = (bf16[128,4096]{1,0:T(8,128)(2,1)}, bf16[128,4096]{1,0:T(8,128)(2,1)}, u32[]{:S(2)}, u32[]{:S(2)}) collective-permute-start(bf16[128,4096]{1,0:T(8,128)(2,1)} %collective-permute-done.7.refs_0_), channel_id=1, source_target_pairs={{0,1},{1,0},{2,3},{3,2},{4,5},{5,4},{6,7},{7,6},{8,9},{9,8},{10,11... | collective-permute-start | bytes 3145736 | tf_op jit(solution)/shard_map/ppermute | solution.py:315
  69.9 3.0 %collective-permute-start.15 = (bf16[128,4096]{1,0:T(8,128)(2,1)}, bf16[128,4096]{1,0:T(8,128)(2,1)}, u32[]{:S(2)}, u32[]{:S(2)}) collective-permute-start(bf16[128,4096]{1,0:T(8,128)(2,1)} %collective-permute-done.8.refs_1_), channel_id=1, source_target_pairs={{0,1},{1,0},{2,3},{3,2},{4,5},{5,4},{6,7},{7,6},{8,9},{9,8},{10,11... | collective-permute-start | bytes 3145736 | tf_op jit(solution)/shard_map/ppermute | solution.py:315
  80.6 13.4 %collective-permute-start.18 = (bf16[256,512]{1,0:T(8,128)(2,1)}, bf16[256,512]{1,0:T(8,128)(2,1)S(1)}, u32[]{:S(2)}, u32[]{:S(2)}) collective-permute-start(bf16[256,512]{1,0:T(8,128)(2,1)} %get-tuple-element.52), channel_id=1, source_target_pairs={{0,8},{8,0},{1,9},{9,1},{2,10},{10,2},{3,11},{11,3},{4,12},{12,4},... | collective-permute-start | bytes 786440 | tf_op jit(solution)/shard_map/ppermute | solution.py:315
  82.1 11.8 %collective-permute-start.19 = (bf16[256,512]{1,0:T(8,128)(2,1)}, bf16[256,512]{1,0:T(8,128)(2,1)S(1)}, u32[]{:S(2)}, u32[]{:S(2)}) collective-permute-start(bf16[256,512]{1,0:T(8,128)(2,1)} %get-tuple-element.56), channel_id=1, source_target_pairs={{0,9},{1,8},{8,1},{9,0},{2,11},{3,10},{10,3},{11,2},{4,13},{5,12},... | collective-permute-start | bytes 786440 | tf_op jit(solution)/shard_map/ppermute | solution.py:320
  89.0 4.9 %collective-permute-start.17 = (bf16[256,512]{1,0:T(8,128)(2,1)}, bf16[256,512]{1,0:T(8,128)(2,1)S(1)}, u32[]{:S(2)}, u32[]{:S(2)}) collective-permute-start(bf16[256,512]{1,0:T(8,128)(2,1)} %get-tuple-element.55), channel_id=1, source_target_pairs={{0,1},{1,0},{2,3},{3,2},{4,5},{5,4},{6,7},{7,6},{8,9},{9,8},{10,11... | collective-permute-start | bytes 786440 | tf_op jit(solution)/shard_map/ppermute | solution.py:315
  94.0 3.1 %copy-start.3 = (bf16[256,512]{1,0:T(8,128)(2,1)}, bf16[256,512]{1,0:T(8,128)(2,1)S(1)}, u32[]{:S(2)}) copy-start(bf16[256,512]{1,0:T(8,128)(2,1)S(1)} %collective-permute-done.19.refs_3_) | copy-start | bytes 786436
  97.1 43.7 %all-to-all-start = ((bf16[16,2,128,128]{3,2,1,0:T(8,128)(2,1)}), bf16[16,2,128,128]{3,2,1,0:T(8,128)(2,1)S(1)}, u32[]{:S(2)}, u32[]{:S(2)}) async-start(bf16[16,2,128,128]{3,2,1,0:T(8,128)(2,1)} %shard_map.67), calls=%async_computation | async-start | bytes 2097152 | tf_op jit(solution)/shard_map/all_to_all | solution.py:383
  103.1 29.5 %copy-start = (bf16[1,256,4096]{2,1,0:T(8,128)(2,1)S(1)}, bf16[1,256,4096]{2,1,0:T(8,128)(2,1)}, u32[]{:S(2)}) copy-start(bf16[1,256,4096]{2,1,0:T(8,128)(2,1)} %param.9) | copy-start | bytes 6291460
  104.6 28.0 %collective-permute-start.20 = (bf16[2,2,128,512]{3,2,1,0:T(8,128)(2,1)S(1)}, bf16[2,2,128,512]{3,2,1,0:T(8,128)(2,1)S(1)}, u32[]{:S(2)}, u32[]{:S(2)}) collective-permute-start(bf16[2,2,128,512]{3,2,1,0:T(8,128)(2,1)S(1)} %slice.64), channel_id=1, source_target_pairs={{0,1},{1,2},{2,3},{3,4},{4,5},{5,6},{6,7},{8,9},{9,10},{10,11},{11... | collective-permute-start | bytes 1572872 | tf_op jit(solution)/shard_map/ppermute | solution.py:386
  (8 other events, 13.7 us)

commit v4 on v3

--- a/solution.py
+++ b/solution.py
@@ -12,7 +12,8 @@
 KVH = 8
 GROUP = 4
 BLOCK = 128
-TALL = 2 * BLOCK
+TALL = GROUP * BLOCK
+DIGITS = 3
 EXP2_SCALE = math.log2(math.e) / math.sqrt(DH)
 
 
@@ -47,6 +48,12 @@
         finish(*now, held)
 
 
+def weighted(raised, values):
+    both = jnp.concatenate([values, jnp.ones_like(values)], axis=1)
+    result = jnp.dot(raised.astype(jnp.bfloat16), both, preferred_element_type=jnp.float32)
+    return result[:, :DH], result[:, DH:]
+
+
 def near_kernel(where_ref, q_ref, k_ref, v_ref, pk_ref, pv_ref, out_ref, log_ref):
     blocks = k_ref.shape[2] // BLOCK
     heads = k_ref.shape[3] // DH
@@ -71,28 +78,42 @@
     def finish(head, b, part, scores):
         highest = jnp.max(scores, axis=-1, keepdims=True)
         raised = jnp.exp2((scores - highest) * EXP2_SCALE)
-        total = jnp.sum(raised, axis=-1, keepdims=True)
+        result, total = weighted(raised, load(v_ref, pv_ref, head, b))
+        result = result * (1.0 / total)
         log = highest * EXP2_SCALE + jnp.log2(total)
-        values = load(v_ref, pv_ref, head, b)
-        result = jnp.dot(raised.astype(jnp.bfloat16), values, preferred_element_type=jnp.float32) * (1.0 / total)
         for i, at in group_rows(head, b, part):
             rows = slice(i * BLOCK, (i + 1) * BLOCK)
             out_ref[at] = result[rows]
-            logs[b] = jnp.where(lane == head * GROUP + part * (TALL // BLOCK) + i, log[rows], logs[b])
+            group, rest = head * GROUP + part * (TALL // BLOCK) + i, log[rows]
+            for digit in range(DIGITS):
+                rounded = rest.astype(jnp.bfloat16).astype(jnp.float32)
+                logs[b] = jnp.where(lane == digit * heads * GROUP + group, rounded, logs[b])
+                rest = rest - rounded
 
     ahead([(h, b, p) for h in range(heads) for b in range(blocks) for p in range(GROUP * BLOCK // TALL)], score, finish)
     for b in range(blocks):
-        log_ref[pl.ds(b * BLOCK, BLOCK)] = logs[b]
-
-
-def far_kernel(place_ref, where_ref, q_ref, near_ref, log_ref, *rest):
-    sorted_refs, out_ref = rest[:-1], rest[-1]
+        log_ref[pl.ds(b * BLOCK, BLOCK)] = logs[b].astype(jnp.bfloat16)
+
+
+def far_kernel(arrays, place_ref, where_ref, q_ref, near_ref, log_ref, spread_ref, *refs):
+    array_refs, (out_ref, table) = refs[:arrays], refs[arrays:]
     blocks = q_ref.shape[0] // BLOCK
     heads = q_ref.shape[1] // (GROUP * DH)
-    lane = lax.broadcasted_iota(jnp.int32, (BLOCK, DH), 1)
+    first = pl.program_id(0) * heads * blocks
+
+    @pl.when(pl.program_id(0) == 0)
+    def _():
+        for i, ref in enumerate(array_refs):
+            kind, start = i // (arrays // 2), i % (arrays // 2) * ref.shape[0]
+            table[kind, pl.ds(start, ref.shape[0])] = ref[...]
+
+    logs = [
+        jnp.dot(log_ref[pl.ds(b * BLOCK, BLOCK)], spread_ref[...], preferred_element_type=jnp.float32)
+        for b in range(blocks)
+    ]
 
     def load(head, b, kind):
-        return sorted_refs[2 * (head * blocks + b) + kind][0, 0]
+        return table[where_ref[1] ^ kind, place_ref[first + head * blocks + b]]
 
     def score(head, b, part):
         q = jnp.concatenate([q_ref[at] for _, at in group_rows(head, b, part)], axis=0)
@@ -102,17 +123,12 @@
 
     def finish(head, b, part, scores):
         spots = list(group_rows(head, b, part))
-        picks = [
-            jnp.where(lane == head * GROUP + part * (TALL // BLOCK) + i, log_ref[at[0]], 0.0) for i, at in spots
-        ]
-        log = jnp.sum(jnp.concatenate(picks, axis=0), axis=-1, keepdims=True)
+        log = jnp.concatenate([logs[b][:, at[1].start : at[1].start + DH] for _, at in spots], axis=0)
         near = jnp.concatenate([near_ref[at] for _, at in spots], axis=0)
         highest = jnp.maximum(jnp.max(scores, axis=-1, keepdims=True) * EXP2_SCALE, log)
-        raised = jnp.exp2(scores * EXP2_SCALE - highest)
+        far, total = weighted(jnp.exp2(scores * EXP2_SCALE - highest), load(head, b, 1))
         share = jnp.exp2(log - highest)
-        scale = 1.0 / (share + jnp.sum(raised, axis=-1, keepdims=True))
-        far = jnp.dot(raised.astype(jnp.bfloat16), load(head, b, 1), preferred_element_type=jnp.float32)
-        result = (near * (share * scale) + far * scale).astype(jnp.bfloat16)
+        result = ((near * share + far) * (1.0 / (share + total))).astype(jnp.bfloat16)
         for i, at in spots:
             out_ref[at] = result[i * BLOCK : (i + 1) * BLOCK]
 
@@ -122,7 +138,7 @@
 def attend(place, where, queries, own, prev, arrived):
     tokens, columns = queries.shape
     blocks = tokens // BLOCK
-    step = 2
+    step = 4
     width = step * GROUP * DH
     steps = own.shape[3] // (step * DH)
 
@@ -131,11 +147,6 @@
             return (where[1] ^ kind, (h // steps) ^ where[at], 0, h % steps)
 
         return pl.BlockSpec((1, 1, rows, step * DH), index)
-
-    def sorted_spec(item, kind):
-        return pl.BlockSpec(
-            (1, 1, BLOCK, DH), lambda h, place, where: (place[h * step * blocks + item], kind, 0, 0)
-        )
 
     near, logs = pl.pallas_call(
         near_kernel,
@@ -156,7 +167,7 @@
         ),
         out_shape=[
             jax.ShapeDtypeStruct(queries.shape, jnp.float32),
-            jax.ShapeDtypeStruct((tokens, KVH // step * DH), jnp.float32),
+            jax.ShapeDtypeStruct((tokens, KVH // step * DH), jnp.bfloat16),
         ],
         cost_estimate=pl.CostEstimate(
             flops=8 * tokens * columns * BLOCK, bytes_accessed=8 * tokens * columns, transcendentals=2 * tokens * columns
@@ -164,8 +175,11 @@
         compiler_params=pltpu.CompilerParams(vmem_limit_bytes=24 * 1024 * 1024),
     )(where, queries, own, own, prev, prev)
     q_spec = pl.BlockSpec((tokens, width), lambda h, place, where: (0, h))
+    digit = jnp.arange(DH)[:, None] - jnp.arange(width)[None] // DH
+    groups = step * GROUP
+    spread = ((digit >= 0) & (digit % groups == 0) & (digit < DIGITS * groups)).astype(jnp.bfloat16)
     return pl.pallas_call(
-        far_kernel,
+        functools.partial(far_kernel, len(arrived)),
         grid_spec=pltpu.PrefetchScalarGridSpec(
             num_scalar_prefetch=2,
             grid=(KVH // step,),
@@ -173,16 +187,20 @@
                 q_spec,
                 q_spec,
                 pl.BlockSpec((tokens, DH), lambda h, place, where: (0, h)),
-                *[sorted_spec(item, kind) for item in range(step * blocks) for kind in range(2)],
+                pl.BlockSpec(spread.shape, lambda h, place, where: (0, 0)),
+                *[pl.BlockSpec(array.shape, lambda h, place, where: (0, 0, 0)) for array in arrived],
             ],
             out_specs=q_spec,
+            scratch_shapes=[
+                pltpu.VMEM((2, sum(array.shape[0] for array in arrived) // 2, BLOCK, DH), jnp.bfloat16),
+            ],
         ),
         out_shape=jax.ShapeDtypeStruct(queries.shape, jnp.bfloat16),
         cost_estimate=pl.CostEstimate(
             flops=4 * tokens * columns * BLOCK, bytes_accessed=8 * tokens * columns, transcendentals=tokens * columns
         ),
         compiler_params=pltpu.CompilerParams(vmem_limit_bytes=24 * 1024 * 1024),
-    )(place, where, queries, near, logs, *([arrived] * (2 * step * blocks)))
+    )(place, where, queries, near, logs, spread, *arrived)
 
 
 def local_gathered(tokens, queries, key_weight, value_weight, sorted_blocks):
@@ -204,7 +222,7 @@
     arrived = lax.all_to_all(replies, "seq", split_axis=0, concat_axis=0, tiled=True)
     zero = jnp.zeros_like(me)
     where = jnp.stack([(me == 0).astype(jnp.int32), zero, zero, zero])
-    return attend(place, where, queries[0], own, prev, arrived)[None]
+    return attend(place, where, queries[0], own, prev, [arrived[:, 0], arrived[:, 1]])[None]
 
 
 def project_kernel(runs, arrays, pieces, place_ref, *refs):
@@ -262,36 +280,36 @@
     )(places, *token_runs, *arrays)
 
 
-def pack_kernel(row_ref, part_ref, *refs):
-    half_refs, out_ref, table = refs[:4], refs[4], refs[5]
-    heads = table.shape[3] // DH
-    blocks = table.shape[2] // BLOCK
-    for i, ref in enumerate(half_refs):
-        table[i // 2, i % 2] = ref[...]
+def pack_kernel(row_ref, part_ref, same_ref, diff_ref, *refs):
+    out_refs, table = refs[:-1], refs[-1]
+    heads = table.shape[2] // DH
+    blocks = table.shape[1] // BLOCK
+    capacity = out_refs[0].shape[0]
+    table[0] = same_ref[...]
+    table[1] = diff_ref[...]
     for i in range(row_ref.shape[0]):
         head, block = row_ref[i] // blocks, row_ref[i] % blocks
-        for kind in range(2):
-            out_ref[i, kind] = table[
-                part_ref[0] ^ kind,
-                (head // heads) ^ part_ref[1],
-                pl.ds(pl.multiple_of(block * BLOCK, BLOCK), BLOCK),
-                pl.ds(pl.multiple_of((head % heads) * DH, DH), DH),
-            ]
-
-
-def pack(rows, part, halves):
+        out_refs[i // capacity][i % capacity] = table[
+            (head // heads) ^ part_ref[0],
+            pl.ds(pl.multiple_of(block * BLOCK, BLOCK), BLOCK),
+            pl.ds(pl.multiple_of((head % heads) * DH, DH), DH),
+        ]
+
+
+def pack(wanted, part, same, diff):
+    devices, capacity = wanted.shape
     return pl.pallas_call(
         pack_kernel,
         grid_spec=pltpu.PrefetchScalarGridSpec(
             num_scalar_prefetch=2,
             grid=(),
-            in_specs=[pl.BlockSpec(memory_space=pltpu.VMEM)] * 4,
-            out_specs=pl.BlockSpec(memory_space=pltpu.VMEM),
-            scratch_shapes=[pltpu.VMEM((2, 2, *halves[0].shape), jnp.bfloat16)],
-        ),
-        out_shape=jax.ShapeDtypeStruct((rows.shape[0], 2, BLOCK, DH), jnp.bfloat16),
+            in_specs=[pl.BlockSpec(memory_space=pltpu.VMEM)] * 2,
+            out_specs=[pl.BlockSpec(memory_space=pltpu.VMEM)] * devices,
+            scratch_shapes=[pltpu.VMEM((2, *same.shape), jnp.bfloat16)],
+        ),
+        out_shape=[jax.ShapeDtypeStruct((capacity, BLOCK, DH), jnp.bfloat16)] * devices,
         compiler_params=pltpu.CompilerParams(vmem_limit_bytes=16 * 1024 * 1024),
-    )(rows, part, *halves)
+    )(wanted.reshape(-1), part, same, diff)
 
 
 def local_split(tokens, queries, key_weight, value_weight, sorted_blocks):
@@ -371,21 +389,35 @@
     from_z = (z + jnp.array([0, -1, 1, 2], jnp.int32)) % chips
     own_row = from_z[:, None] == jnp.arange(chips, dtype=jnp.int32)[None]
     all_targets = jnp.sum(jnp.where(own_row[:, :, None, None], notes[:, None], 0), axis=0)
-    wanted = plan_sends(all_targets.reshape(devices, *targets.shape), me, local_blocks, capacity).reshape(-1)
-    place = plan_receives(targets, local_blocks, capacity)
-
+    wanted = plan_sends(all_targets.reshape(devices, *targets.shape), me, local_blocks, capacity)
+    wanted = jnp.take(wanted, me ^ jnp.arange(devices, dtype=jnp.int32), axis=0)
+    place = plan_receives(targets, local_blocks, capacity) ^ (me * capacity)
+    core = c.astype(jnp.int32).reshape(1)
+
+    def swap_blocks(replies):
+        return [replies[0]] + [
+            lax.ppermute(replies[k], ("z", "c"), [(i, i ^ k) for i in range(devices)]) for k in range(1, devices)
+        ]
+
+    def last_block(same, diff):
+        edge = jnp.stack([same[-BLOCK:], diff[-BLOCK:]])
+        return lax.ppermute(edge, ("z", "c"), [(i, i + 1) for i in range(devices - 1)])
+
+    same, sent = project([tokens[0], c_tokens], arrays, pieces, places)
+    diff = over_c(sent)
+    x_late, sent = lax.optimization_barrier((x_late, sent))
     x_sent, xc_sent = project([x_early, x_late, xc_early, xc_late], arrays, pieces, places)
     x_same, x_diff = over_x(x_sent), over_xc(xc_sent)
-    own_tokens, x_sent = lax.optimization_barrier((tokens[0], x_sent))
-    same, sent = project([own_tokens, c_tokens], arrays, pieces, places)
-    halves = [same, over_c(sent), x_same, x_diff]
-    replies = pack(wanted, jnp.stack([x, c]).astype(jnp.int32), halves)
-    arrived = lax.all_to_all(replies, ("z", "c"), split_axis=0, concat_axis=0, tiled=True)
-
-    own = jnp.stack(halves).reshape(2, 2, *same.shape)
-    prev = lax.ppermute(own[:, :, -BLOCK:], ("z", "c"), [(i, i + 1) for i in range(devices - 1)])
+    same, diff, x_sent = lax.optimization_barrier((same, diff, x_sent))
+    arrived = swap_blocks(pack(wanted, core, same, diff))
+    prev = last_block(same, diff)
+    x_same, x_diff, prev, *arrived = lax.optimization_barrier((x_same, x_diff, prev, *arrived))
+    x_prev = last_block(x_same, x_diff)
+    arrived += swap_blocks(pack(wanted, core, x_same, x_diff))
+
+    own = jnp.stack([same, diff, x_same, x_diff]).reshape(2, 2, *same.shape)
     where = jnp.stack([(me == 0).astype(jnp.int32), x, c, 1 - c]).astype(jnp.int32)
-    return attend(place, where, queries[0], own, prev, arrived)[None]
+    return attend(place, where, queries[0], own, jnp.stack([prev, x_prev]), arrived)[None]
 
 
 def solution(mesh):

time: 151 us -> 140 us (0.927)
  waiting for transfers between devices: 82.2 us -> 62 us
  starting transfers between devices: 23.8 us -> 35 us
  local copies, waits for them, and re-layouts: 12.1 us -> 9.76 us
    ppermute x1 -> x16, starting transfers between devices: 2.06 us -> 16.6 us  [the longest x14 12 us: swap_blocks(): lax.ppermute(replies[k], ('z', 'c'), [(i, i ^ k) for i in range(devices)])]
    ppermute x1 -> x16, waiting for transfers between devices: 25.7 us -> 14.5 us  [the longest x14 13.7 us: swap_blocks(): lax.ppermute(replies[k], ('z', 'c'), [(i, i ^ k) for i in range(devices)])]
    ppermute x18, waiting for transfers between devices: 51.3 us -> 45.4 us  [along(): lax.ppermute(value, axis, [(i, (i + step) % count) for i in range(count)])]
    all_to_all x1 -> x0, starting transfers between devices: 5.83 us -> none  [local_split(): lax.all_to_all(replies, ('z', 'c'), split_axis=0, concat_axis=0, tiled=True)]
    unnamed x37 -> x31, local copies, waits for them, and re-layouts: 7.56 us -> 2.37 us
    ppermute x2, waiting for transfers between devices: 5.18 us -> 1.97 us  [over_xc(): return lax.ppermute(value, ('x', 'c'), [(i, 3 - i) for i in range(4)])]
    slice x2, local copies, waits for them, and re-layouts: 0.04 us -> 2.41 us  [local_split(): far_ours, far_theirs = (up(from_up[:deep]), down(from_down[deep:]))]
    ppermute x2, starting transfers between devices: 0.01 us -> 2.34 us  [over_xc(): return lax.ppermute(value, ('x', 'c'), [(i, 3 - i) for i in range(4)])]
  transfers between devices with their start and end apart: 22 -> 36, of which waited for: 12 -> 14; matrix products, arithmetic and copies ran while one was open for 5% -> 7% of each run, Pallas kernels for 13% -> 15%
where the time goes in v4:
time: 140 us; the launch traced here: 138 us
  waiting for transfers between devices  62 us (44%)
  starting transfers between devices  35 us (25%)
  Pallas kernels  27.1 us (19%)
  local copies, waits for them, and re-layouts  9.76 us (7%)
  other arithmetic  4.02 us (3%)
    ppermute x18, waiting for transfers between devices, along(): lax.ppermute(value, axis, [(i, (i + step) % count) for i in range(count)])  45.4 us
    ppermute x18, starting transfers between devices, along(): lax.ppermute(value, axis, [(i, (i + step) % count) for i in range(count)])  16.1 us
    pallas_call x2, Pallas kernels, project(): pl.pallas_call(functools.partial(project_kernel, len(token_runs), len(arr...  14.6 us
    ppermute x14, waiting for transfers between devices, swap_blocks(): lax.ppermute(replies[k], ('z', 'c'), [(i, i ^ k) for i in range(devices)])  13.7 us
    ppermute x14, starting transfers between devices, swap_blocks(): lax.ppermute(replies[k], ('z', 'c'), [(i, i ^ k) for i in range(devices)])  12 us
    pallas_call x1, Pallas kernels, attend(): pl.pallas_call(functools.partial(far_kernel, len(arrived)), grid_spec=plt...  5.66 us
    pallas_call x1, Pallas kernels, attend(): pl.pallas_call(near_kernel, grid_spec=pltpu.PrefetchScalarGridSpec(num_sc...  5.14 us
    ppermute x2, starting transfers between devices, last_block(): lax.ppermute(edge, ('z', 'c'), [(i, i + 1) for i in range(devices - 1)])  4.53 us
  transfers between devices with their start and end apart: 36, of which 14 were waited for; matrix products, arithmetic and copies ran while one was open for 7% of the time, Pallas kernels for 15%

profile of v4, /device:TPU:16, one launch (start us, length us, event | category | flops | bytes accessed | tf_op | source)
XLA Modules:
  0.0 138.3 jit_solution(12051752128918679981)
XLA Ops:
  2.3 1.6 %collective-permute-start.2 = (bf16[128,512]{1,0:T(8,128)(2,1)S(1)}, bf16[128,512]{1,0:T(8,128)(2,1)S(1)}, u32[]{:S(2)}, u32[]{:S(2)}) collective-permute-start(bf16[128,512]{1,0:T(8,128)(2,1)S(1)} %get-tuple-element.125), channel_id=1, source_target_pairs={{0,8},{8,0},{1,9},{9,1},{2,10},{10,2},{3,11},{11,3},{4,12},{12,4},... | collective-permute-start | bytes 393224 | tf_op jit(solution)/shard_map/ppermute | solution.py:333
  4.5 1.5 %slice_bitcast_fusion = (bf16[128,4096]{1,0:T(8,128)(2,1)}, bf16[128,4096]{1,0:T(8,128)(2,1)}) fusion(bf16[1,256,4096]{2,1,0:T(8,128)(2,1)S(1)} %copy-done.2), kind=kLoop, calls=%fused_computation.12 | loop fusion | bytes 4194304 | tf_op jit(solution)/shard_map/split | solution.py:353
  6.1 2.5 %collective-permute-done.2 = bf16[128,512]{1,0:T(8,128)(2,1)S(1)} collective-permute-done((bf16[128,512]{1,0:T(8,128)(2,1)S(1)}, bf16[128,512]{1,0:T(8,128)(2,1)S(1)}, u32[]{:S(2)}, u32[]{:S(2)}) %collective-permute-start.2) | collective-permute-done | bytes 131104 | tf_op jit(solution)/shard_map/ppermute | solution.py:333
  8.6 2.0 %collective-permute-done.3 = bf16[128,512]{1,0:T(8,128)(2,1)S(1)} collective-permute-done((bf16[128,512]{1,0:T(8,128)(2,1)S(1)}, bf16[128,512]{1,0:T(8,128)(2,1)S(1)}, u32[]{:S(2)}, u32[]{:S(2)}) %collective-permute-start.3) | collective-permute-done | bytes 131104 | tf_op jit(solution)/shard_map/ppermute | solution.py:338
  11.2 1.6 %collective-permute-start.4 = (bf16[528,512]{1,0:T(8,128)(2,1)S(1)}, bf16[528,512]{1,0:T(8,128)(2,1)S(1)}, u32[]{:S(2)}, u32[]{:S(2)}) collective-permute-start(bf16[528,512]{1,0:T(8,128)(2,1)S(1)} %maximum_maximum_fusion.refs_2_.refs_4_), channel_id=1, source_target_pairs={{0,2},{2,4},{4,6},{6,0},{1,3},{3,5},{5,7},{7,1},{8,10},{10,12},{12... | collective-permute-start | bytes 1622024 | tf_op jit(solution)/shard_map/ppermute | solution.py:333
  12.9 1.5 %collective-permute-start.5 = (bf16[528,512]{1,0:T(8,128)(2,1)S(1)}, bf16[528,512]{1,0:T(8,128)(2,1)S(1)}, u32[]{:S(2)}, u32[]{:S(2)}) collective-permute-start(bf16[528,512]{1,0:T(8,128)(2,1)S(1)} %maximum_maximum_fusion.refs_2_.refs_4_), channel_id=1, source_target_pairs={{0,16},{16,0},{1,17},{17,1},{2,18},{18,2},{3,19},{19,3},{4,20},{20... | collective-permute-start | bytes 1622024 | tf_op jit(solution)/shard_map/ppermute | solution.py:333
  14.4 1.5 %collective-permute-start.8 = (bf16[128,4096]{1,0:T(8,128)(2,1)S(1)}, bf16[128,4096]{1,0:T(8,128)(2,1)S(1)}, u32[]{:S(2)}, u32[]{:S(2)}) collective-permute-start(bf16[128,4096]{1,0:T(8,128)(2,1)S(1)} %copy-done.11), channel_id=1, source_target_pairs={{0,8},{8,0},{1,9},{9,1},{2,10},{10,2},{3,11},{11,3},{4,12},{12,4},... | collective-permute-start | bytes 3145736 | tf_op jit(solution)/shard_map/ppermute | solution.py:333
  16.4 20.9 %collective-permute-done.4.refs_4_.refs_6_ = bf16[528,512]{1,0:T(8,128)(2,1)S(1)} collective-permute-done((bf16[528,512]{1,0:T(8,128)(2,1)S(1)}, bf16[528,512]{1,0:T(8,128)(2,1)S(1)}, u32[]{:S(2)}, u32[]{:S(2)}) %collective-permute-start.4) | collective-permute-done | bytes 540704 | tf_op jit(solution)/shard_map/ppermute | solution.py:333
  38.1 1.5 %collective-permute-start.7 = (bf16[528,512]{1,0:T(8,128)(2,1)S(1)}, bf16[528,512]{1,0:T(8,128)(2,1)S(1)}, u32[]{:S(2)}, u32[]{:S(2)}) collective-permute-start(bf16[528,512]{1,0:T(8,128)(2,1)S(1)} %collective-permute-done.4.refs_4_.refs_6_), channel_id=1, source_target_pairs={{0,16},{16,0},{1,17},{17,1},{2,18},{18,2},{3,19},{19,3},{4,20},{20... | collective-permute-start | bytes 1622024 | tf_op jit(solution)/shard_map/ppermute | solution.py:333
  40.3 1.6 %collective-permute-start.11 = (bf16[128,4096]{1,0:T(8,128)(2,1)}, bf16[128,4096]{1,0:T(8,128)(2,1)}, u32[]{:S(2)}, u32[]{:S(2)}) collective-permute-start(bf16[128,4096]{1,0:T(8,128)(2,1)} %get-tuple-element.75), channel_id=1, source_target_pairs={{0,8},{8,0},{1,9},{9,1},{2,10},{10,2},{3,11},{11,3},{4,12},{12,4},... | collective-permute-start | bytes 3145736 | tf_op jit(solution)/shard_map/ppermute | solution.py:333
  41.9 10.5 %collective-permute-done.7.refs_5_.refs_7_ = bf16[528,512]{1,0:T(8,128)(2,1)S(1)} collective-permute-done((bf16[528,512]{1,0:T(8,128)(2,1)S(1)}, bf16[528,512]{1,0:T(8,128)(2,1)S(1)}, u32[]{:S(2)}, u32[]{:S(2)}) %collective-permute-start.7) | collective-permute-done | bytes 540704 | tf_op jit(solution)/shard_map/ppermute | solution.py:333
  53.8 1.6 %collective-permute-start.9 = (bf16[256,512]{1,0:T(8,128)(2,1)}, bf16[256,512]{1,0:T(8,128)(2,1)}, u32[]{:S(2)}, u32[]{:S(2)}) collective-permute-start(bf16[256,512]{1,0:T(8,128)(2,1)} %slice.63), channel_id=1, source_target_pairs={{0,2},{2,4},{4,6},{6,0},{1,3},{3,5},{5,7},{7,1},{8,10},{10,12},{12... | collective-permute-start | bytes 786440 | tf_op jit(solution)/shard_map/ppermute | solution.py:333
  55.4 1.7 %slice.64 = bf16[272,512]{1,0:T(8,128)(2,1)} slice(bf16[528,512]{1,0:T(8,128)(2,1)} %collective-permute-done.6.refs_6_.refs_8_), slice={[256:528], [0:512]} | slice | bytes 557056 | tf_op jit(solution)/shard_map/slice | solution.py:366
  58.4 5.5 %collective-permute-done.12.refs_10_.refs_12_ = bf16[272,512]{1,0:T(8,128)(2,1)S(1)} collective-permute-done((bf16[272,512]{1,0:T(8,128)(2,1)}, bf16[272,512]{1,0:T(8,128)(2,1)S(1)}, u32[]{:S(2)}, u32[]{:S(2)}) %collective-permute-start.12) | collective-permute-done | bytes 278560 | tf_op jit(solution)/shard_map/ppermute | solution.py:333
  67.3 3.1 %collective-permute-done.14.refs_11_.refs_13_ = bf16[272,512]{1,0:T(8,128)(2,1)S(1)} collective-permute-done((bf16[272,512]{1,0:T(8,128)(2,1)S(1)}, bf16[272,512]{1,0:T(8,128)(2,1)S(1)}, u32[]{:S(2)}, u32[]{:S(2)}) %collective-permute-start.14) | collective-permute-done | bytes 278560 | tf_op jit(solution)/shard_map/ppermute | solution.py:333
  71.1 2.1 %collective-permute-done.13.refs_9_.refs_11_ = bf16[256,512]{1,0:T(8,128)(2,1)S(1)} collective-permute-done((bf16[256,512]{1,0:T(8,128)(2,1)}, bf16[256,512]{1,0:T(8,128)(2,1)S(1)}, u32[]{:S(2)}, u32[]{:S(2)}) %collective-permute-start.13) | collective-permute-done | bytes 262176 | tf_op jit(solution)/shard_map/ppermute | solution.py:333
  75.0 6.9 %shard_map.64 = (bf16[256,512]{1,0:T(8,128)(2,1)}, bf16[256,512]{1,0:T(8,128)(2,1)}) custom-call(s32[16]{0:T(128)} %stack.175.place_ref, bf16[256,4096]{1,0:T(8,128)(2,1)} %bitcast.75, bf16[256,4096]{1,0:T(8,128)(2,1)} %collective-permute-done.refs_1_, bf16[528,512]{1,0:T(8,128)(2,1)} %copy-done.3, bf16[528,512]{1,0:T(8,128)(2,1)} %copy-done.5, ...), custom_call_target="tpu_custom_call" | custom-call | flops 2147483648 | bytes 8388608 | tf_op jit(solution)/shard_map/pallas_call | solution.py:261
  82.6 7.7 %shard_map.65 = (bf16[256,512]{1,0:T(8,128)(2,1)}, bf16[256,512]{1,0:T(8,128)(2,1)}) custom-call(s32[16]{0:T(128)} %stack.175.place_ref, bf16[128,4096]{1,0:T(8,128)(2,1)} %copy-done.9, bf16[128,4096]{1,0:T(8,128)(2,1)} %collective-permute-done.11.refs_1_, bf16[128,4096]{1,0:T(8,128)(2,1)} %collective-permute-done.16.refs_2_, ...), custom_call_target="tpu_custom_call" | custom-call | flops 2147483648 | bytes 8388608 | tf_op jit(solution)/shard_map/pallas_call | solution.py:261
  90.4 1.5 %collective-permute-start.18 = (bf16[256,512]{1,0:T(8,128)(2,1)}, bf16[256,512]{1,0:T(8,128)(2,1)S(1)}, u32[]{:S(2)}, u32[]{:S(2)}) collective-permute-start(bf16[256,512]{1,0:T(8,128)(2,1)} %get-tuple-element.84), channel_id=1, source_target_pairs={{0,8},{8,0},{1,9},{9,1},{2,10},{10,2},{3,11},{11,3},{4,12},{12,4},... | collective-permute-start | bytes 786440 | tf_op jit(solution)/shard_map/ppermute | solution.py:333
  92.9 1.9 %collective-permute-start.22 = (bf16[2,128,128]{2,1,0:T(8,128)(2,1)S(1)}, bf16[2,128,128]{2,1,0:T(8,128)(2,1)S(1)}, u32[]{:S(2)}, u32[]{:S(2)}) collective-permute-start(bf16[2,128,128]{2,1,0:T(8,128)(2,1)S(1)} %get-tuple-element.90), channel_id=1, source_target_pairs={{0,2},{1,3},{2,0},{3,1},{4,6},{5,7},{6,4},{7,5},{8,10},{9,11},{10,... | collective-permute-start | bytes 196616 | tf_op jit(solution)/shard_map/ppermute | solution.py:399
  94.8 1.3 collective-permute-start.24
  97.5 2.4 %collective-permute-start.20 = (bf16[2,128,512]{2,1,0:T(8,128)(2,1)S(1)}, bf16[2,128,512]{2,1,0:T(8,128)(2,1)S(1)}, u32[]{:S(2)}, u32[]{:S(2)}) collective-permute-start(bf16[2,128,512]{2,1,0:T(8,128)(2,1)S(1)} %pad_maximum_fusion.4), channel_id=1, source_target_pairs={{0,1},{1,2},{2,3},{3,4},{4,5},{5,6},{6,7},{8,9},{9,10},{10,11},{11... | collective-permute-start | bytes 786440 | tf_op jit(solution)/shard_map/ppermute | solution.py:404
  99.9 2.0 %collective-permute-start.19 = (bf16[256,512]{1,0:T(8,128)(2,1)S(1)}, bf16[256,512]{1,0:T(8,128)(2,1)S(1)}, u32[]{:S(2)}, u32[]{:S(2)}) collective-permute-start(bf16[256,512]{1,0:T(8,128)(2,1)S(1)} %copy-done.13), channel_id=1, source_target_pairs={{0,9},{1,8},{8,1},{9,0},{2,11},{3,10},{10,3},{11,2},{4,13},{5,12},... | collective-permute-start | bytes 786440 | tf_op jit(solution)/shard_map/ppermute | solution.py:338
  103.7 3.4 %collective-permute-done.26.refs_6_ = bf16[2,128,128]{2,1,0:T(8,128)(2,1)S(1)} collective-permute-done((bf16[2,128,128]{2,1,0:T(8,128)(2,1)S(1)}, bf16[2,128,128]{2,1,0:T(8,128)(2,1)S(1)}, u32[]{:S(2)}, u32[]{:S(2)}) %collective-permute-start.26) | collective-permute-done | bytes 65568 | tf_op jit(solution)/shard_map/ppermute | solution.py:399
  107.0 5.7 %collective-permute-done.27.refs_7_ = bf16[2,128,128]{2,1,0:T(8,128)(2,1)S(1)} collective-permute-done((bf16[2,128,128]{2,1,0:T(8,128)(2,1)S(1)}, bf16[2,128,128]{2,1,0:T(8,128)(2,1)S(1)}, u32[]{:S(2)}, u32[]{:S(2)}) %collective-permute-start.27) | collective-permute-done | bytes 65568 | tf_op jit(solution)/shard_map/ppermute | solution.py:399
  112.9 2.1 %collective-permute-start.28 = (bf16[2,128,512]{2,1,0:T(8,128)(2,1)S(1)}, bf16[2,128,512]{2,1,0:T(8,128)(2,1)S(1)}, u32[]{:S(2)}, u32[]{:S(2)}) collective-permute-start(bf16[2,128,512]{2,1,0:T(8,128)(2,1)S(1)} %pad_maximum_fusion.5), channel_id=1, source_target_pairs={{0,1},{1,2},{2,3},{3,4},{4,5},{5,6},{6,7},{8,9},{9,10},{10,11},{11... | collective-permute-start | bytes 786440 | tf_op jit(solution)/shard_map/ppermute | solution.py:404
  116.1 1.8 %collective-permute-start.31 = (bf16[2,128,128]{2,1,0:T(8,128)(2,1)S(1)}, bf16[2,128,128]{2,1,0:T(8,128)(2,1)S(1)}, u32[]{:S(2)}, u32[]{:S(2)}) collective-permute-start(bf16[2,128,128]{2,1,0:T(8,128)(2,1)S(1)} %get-tuple-element.112), channel_id=1, source_target_pairs={{0,3},{1,2},{2,1},{3,0},{4,7},{5,6},{6,5},{7,4},{8,11},{9,10},{10,... | collective-permute-start | bytes 196616 | tf_op jit(solution)/shard_map/ppermute | solution.py:399
  117.9 1.7 %collective-permute-start.32 = (bf16[2,128,128]{2,1,0:T(8,128)(2,1)S(1)}, bf16[2,128,128]{2,1,0:T(8,128)(2,1)S(1)}, u32[]{:S(2)}, u32[]{:S(2)}) collective-permute-start(bf16[2,128,128]{2,1,0:T(8,128)(2,1)S(1)} %get-tuple-element.113), channel_id=1, source_target_pairs={{0,4},{1,5},{2,6},{3,7},{4,0},{5,1},{6,2},{7,3},{8,12},{9,13},{10,... | collective-permute-start | bytes 196616 | tf_op jit(solution)/shard_map/ppermute | solution.py:399
  120.7 2.1 %collective-permute-start.34 = (bf16[2,128,128]{2,1,0:T(8,128)(2,1)S(1)}, bf16[2,128,128]{2,1,0:T(8,128)(2,1)S(1)}, u32[]{:S(2)}, u32[]{:S(2)}) collective-permute-start(bf16[2,128,128]{2,1,0:T(8,128)(2,1)S(1)} %get-tuple-element.115), channel_id=1, source_target_pairs={{0,6},{1,7},{2,4},{3,5},{4,2},{5,3},{6,0},{7,1},{8,14},{9,15},{10,... | collective-permute-start | bytes 196616 | tf_op jit(solution)/shard_map/ppermute | solution.py:399
  122.9 5.1 %shard_map.67 = (f32[256,4096]{1,0:T(8,128)S(1)}, bf16[256,256]{1,0:T(8,128)(2,1)S(1)}) custom-call(s32[4]{0:T(128)S(1)} %pad_add_fusion.where_ref, bf16[256,4096]{1,0:T(8,128)(2,1)S(1)} %bitcast.69, bf16[2,2,256,512]{3,2,1,0:T(8,128)(2,1)S(1)} %bitcast.67, bf16[2,2,256,512]{3,2,1,0:T(8,128)(2,1)S(1)} %bitcast.68, ...), custom_call_target="tpu_custom_call" | custom-call | flops 1073741824 | bytes 8388608 | tf_op jit(solution)/shard_map/pallas_call | solution.py:151
  128.4 3.2 %collective-permute-done.34.refs_14_ = bf16[2,128,128]{2,1,0:T(8,128)(2,1)S(1)} collective-permute-done((bf16[2,128,128]{2,1,0:T(8,128)(2,1)S(1)}, bf16[2,128,128]{2,1,0:T(8,128)(2,1)S(1)}, u32[]{:S(2)}, u32[]{:S(2)}) %collective-permute-start.34) | collective-permute-done | bytes 65568 | tf_op jit(solution)/shard_map/ppermute | solution.py:399
  132.6 5.7 %shard_map.69 = bf16[256,4096]{1,0:T(8,128)(2,1)} custom-call(s32[16]{0:T(128)S(1)} %add_xor_fusion.place_ref, s32[4]{0:T(128)S(1)} %pad_add_fusion.where_ref, bf16[256,4096]{1,0:T(8,128)(2,1)S(1)} %bitcast.70, f32[256,4096]{1,0:T(8,128)S(1)} %get-tuple-element.99.near_ref, bf16[256,256]{1,0:T(8,128)(2,1)S(1)} %get-tuple-element.100.log_ref, ...), custom_call_target="tpu_custom_call" | custom-call | flops 536870912 | bytes 8388608 | tf_op jit(solution)/shard_map/pallas_call | solution.py:181
  (137 shorter events, 22.6 us)
Async XLA Ops:
  2.2 8.5 %collective-permute-start.1 = (bf16[144,512]{1,0:T(8,128)(2,1)S(1)}, bf16[144,512]{1,0:T(8,128)(2,1)S(1)}, u32[]{:S(2)}, u32[]{:S(2)}) collective-permute-start(bf16[144,512]{1,0:T(8,128)(2,1)S(1)} %pad_maximum_fusion.6), channel_id=1, source_target_pairs={{0,1},{1,0},{2,3},{3,2},{4,5},{5,4},{6,7},{7,6},{8,9},{9,8},{10,11... | collective-permute-start | bytes 442376 | tf_op jit(solution)/shard_map/ppermute | solution.py:333
  2.3 6.4 %collective-permute-start.2 = (bf16[128,512]{1,0:T(8,128)(2,1)S(1)}, bf16[128,512]{1,0:T(8,128)(2,1)S(1)}, u32[]{:S(2)}, u32[]{:S(2)}) collective-permute-start(bf16[128,512]{1,0:T(8,128)(2,1)S(1)} %get-tuple-element.125), channel_id=1, source_target_pairs={{0,8},{8,0},{1,9},{9,1},{2,10},{10,2},{3,11},{11,3},{4,12},{12,4},... | collective-permute-start | bytes 393224 | tf_op jit(solution)/shard_map/ppermute | solution.py:333
  3.8 6.8 %collective-permute-start.3 = (bf16[128,512]{1,0:T(8,128)(2,1)S(1)}, bf16[128,512]{1,0:T(8,128)(2,1)S(1)}, u32[]{:S(2)}, u32[]{:S(2)}) collective-permute-start(bf16[128,512]{1,0:T(8,128)(2,1)S(1)} %get-tuple-element.126), channel_id=1, source_target_pairs={{0,9},{1,8},{8,1},{9,0},{2,11},{3,10},{10,3},{11,2},{4,13},{5,12},... | collective-permute-start | bytes 393224 | tf_op jit(solution)/shard_map/ppermute | solution.py:338
  4.2 70.8 %collective-permute-start = (bf16[256,4096]{1,0:T(8,128)(2,1)S(1)}, bf16[256,4096]{1,0:T(8,128)(2,1)}, u32[]{:S(2)}, u32[]{:S(2)}) collective-permute-start(bf16[256,4096]{1,0:T(8,128)(2,1)S(1)} %bitcast.76), channel_id=1, source_target_pairs={{0,1},{1,0},{2,3},{3,2},{4,5},{5,4},{6,7},{7,6},{8,9},{9,8},{10,11... | collective-permute-start | bytes 6291464 | tf_op jit(solution)/shard_map/ppermute | solution.py:333
  11.2 26.1 %collective-permute-start.4 = (bf16[528,512]{1,0:T(8,128)(2,1)S(1)}, bf16[528,512]{1,0:T(8,128)(2,1)S(1)}, u32[]{:S(2)}, u32[]{:S(2)}) collective-permute-start(bf16[528,512]{1,0:T(8,128)(2,1)S(1)} %maximum_maximum_fusion.refs_2_.refs_4_), channel_id=1, source_target_pairs={{0,2},{2,4},{4,6},{6,0},{1,3},{3,5},{5,7},{7,1},{8,10},{10,12},{12... | collective-permute-start | bytes 1622024 | tf_op jit(solution)/shard_map/ppermute | solution.py:333
  12.9 24.4 %collective-permute-start.5 = (bf16[528,512]{1,0:T(8,128)(2,1)S(1)}, bf16[528,512]{1,0:T(8,128)(2,1)S(1)}, u32[]{:S(2)}, u32[]{:S(2)}) collective-permute-start(bf16[528,512]{1,0:T(8,128)(2,1)S(1)} %maximum_maximum_fusion.refs_2_.refs_4_), channel_id=1, source_target_pairs={{0,16},{16,0},{1,17},{17,1},{2,18},{18,2},{3,19},{19,3},{4,20},{20... | collective-permute-start | bytes 1622024 | tf_op jit(solution)/shard_map/ppermute | solution.py:333
  14.4 27.5 %collective-permute-start.8 = (bf16[128,4096]{1,0:T(8,128)(2,1)S(1)}, bf16[128,4096]{1,0:T(8,128)(2,1)S(1)}, u32[]{:S(2)}, u32[]{:S(2)}) collective-permute-start(bf16[128,4096]{1,0:T(8,128)(2,1)S(1)} %copy-done.11), channel_id=1, source_target_pairs={{0,8},{8,0},{1,9},{9,1},{2,10},{10,2},{3,11},{11,3},{4,12},{12,4},... | collective-permute-start | bytes 3145736 | tf_op jit(solution)/shard_map/ppermute | solution.py:333
  15.9 25.9 %collective-permute-start.6 = (bf16[528,512]{1,0:T(8,128)(2,1)S(1)}, bf16[528,512]{1,0:T(8,128)(2,1)}, u32[]{:S(2)}, u32[]{:S(2)}) collective-permute-start(bf16[528,512]{1,0:T(8,128)(2,1)S(1)} %maximum_maximum_fusion.refs_2_.refs_4_), channel_id=1, source_target_pairs={{0,6},{2,0},{4,2},{6,4},{1,7},{3,1},{5,3},{7,5},{8,14},{10,8},{12,... | collective-permute-start | bytes 1622024 | tf_op jit(solution)/shard_map/ppermute | solution.py:333
  38.1 14.2 %collective-permute-start.7 = (bf16[528,512]{1,0:T(8,128)(2,1)S(1)}, bf16[528,512]{1,0:T(8,128)(2,1)S(1)}, u32[]{:S(2)}, u32[]{:S(2)}) collective-permute-start(bf16[528,512]{1,0:T(8,128)(2,1)S(1)} %collective-permute-done.4.refs_4_.refs_6_), channel_id=1, source_target_pairs={{0,16},{16,0},{1,17},{17,1},{2,18},{18,2},{3,19},{19,3},{4,20},{20... | collective-permute-start | bytes 1622024 | tf_op jit(solution)/shard_map/ppermute | solution.py:333
  40.3 27.0 %collective-permute-start.11 = (bf16[128,4096]{1,0:T(8,128)(2,1)}, bf16[128,4096]{1,0:T(8,128)(2,1)}, u32[]{:S(2)}, u32[]{:S(2)}) collective-permute-start(bf16[128,4096]{1,0:T(8,128)(2,1)} %get-tuple-element.75), channel_id=1, source_target_pairs={{0,8},{8,0},{1,9},{9,1},{2,10},{10,2},{3,11},{11,3},{4,12},{12,4},... | collective-permute-start | bytes 3145736 | tf_op jit(solution)/shard_map/ppermute | solution.py:333
  52.4 12.8 %collective-permute-start.10 = (bf16[528,512]{1,0:T(8,128)(2,1)}, bf16[528,512]{1,0:T(8,128)(2,1)}, u32[]{:S(2)}, u32[]{:S(2)}) collective-permute-start(bf16[528,512]{1,0:T(8,128)(2,1)} %collective-permute-done.6.refs_6_.refs_8_), channel_id=1, source_target_pairs={{0,16},{16,0},{1,17},{17,1},{2,18},{18,2},{3,19},{19,3},{4,20},{20... | collective-permute-start | bytes 1622024 | tf_op jit(solution)/shard_map/ppermute | solution.py:333
  53.8 10.5 %collective-permute-start.9 = (bf16[256,512]{1,0:T(8,128)(2,1)}, bf16[256,512]{1,0:T(8,128)(2,1)}, u32[]{:S(2)}, u32[]{:S(2)}) collective-permute-start(bf16[256,512]{1,0:T(8,128)(2,1)} %slice.63), channel_id=1, source_target_pairs={{0,2},{2,4},{4,6},{6,0},{1,3},{3,5},{5,7},{7,1},{8,10},{10,12},{12... | collective-permute-start | bytes 786440 | tf_op jit(solution)/shard_map/ppermute | solution.py:333
  57.1 6.8 %collective-permute-start.12 = (bf16[272,512]{1,0:T(8,128)(2,1)}, bf16[272,512]{1,0:T(8,128)(2,1)S(1)}, u32[]{:S(2)}, u32[]{:S(2)}) collective-permute-start(bf16[272,512]{1,0:T(8,128)(2,1)} %slice.64), channel_id=1, source_target_pairs={{0,6},{2,0},{4,2},{6,4},{1,7},{3,1},{5,3},{7,5},{8,14},{10,8},{12,... | collective-permute-start | bytes 835592 | tf_op jit(solution)/shard_map/ppermute | solution.py:333
  63.8 6.5 %collective-permute-start.14 = (bf16[272,512]{1,0:T(8,128)(2,1)S(1)}, bf16[272,512]{1,0:T(8,128)(2,1)S(1)}, u32[]{:S(2)}, u32[]{:S(2)}) collective-permute-start(bf16[272,512]{1,0:T(8,128)(2,1)S(1)} %collective-permute-done.12.refs_10_.refs_12_), channel_id=1, source_target_pairs={{0,16},{16,0},{1,17},{17,1},{2,18},{18,2},{3,19},{19,3},{4,20},{20... | collective-permute-start | bytes 835592 | tf_op jit(solution)/shard_map/ppermute | solution.py:333
  65.2 8.0 %collective-permute-start.13 = (bf16[256,512]{1,0:T(8,128)(2,1)}, bf16[256,512]{1,0:T(8,128)(2,1)S(1)}, u32[]{:S(2)}, u32[]{:S(2)}) collective-permute-start(bf16[256,512]{1,0:T(8,128)(2,1)} %collective-permute-done.9.refs_8_.refs_10_), channel_id=1, source_target_pairs={{0,16},{16,0},{1,17},{17,1},{2,18},{18,2},{3,19},{19,3},{4,20},{20... | collective-permute-start | bytes 786440 | tf_op jit(solution)/shard_map/ppermute | solution.py:333
  66.6 16.0 %collective-permute-start.16 = (bf16[128,4096]{1,0:T(8,128)(2,1)}, bf16[128,4096]{1,0:T(8,128)(2,1)}, u32[]{:S(2)}, u32[]{:S(2)}) collective-permute-start(bf16[128,4096]{1,0:T(8,128)(2,1)} %copy-done.9), channel_id=1, source_target_pairs={{0,1},{1,0},{2,3},{3,2},{4,5},{5,4},{6,7},{7,6},{8,9},{9,8},{10,11... | collective-permute-start | bytes 3145736 | tf_op jit(solution)/shard_map/ppermute | solution.py:333
  73.9 8.7 %collective-permute-start.17 = (bf16[128,4096]{1,0:T(8,128)(2,1)}, bf16[128,4096]{1,0:T(8,128)(2,1)}, u32[]{:S(2)}, u32[]{:S(2)}) collective-permute-start(bf16[128,4096]{1,0:T(8,128)(2,1)} %collective-permute-done.11.refs_1_), channel_id=1, source_target_pairs={{0,1},{1,0},{2,3},{3,2},{4,5},{5,4},{6,7},{7,6},{8,9},{9,8},{10,11... | collective-permute-start | bytes 3145736 | tf_op jit(solution)/shard_map/ppermute | solution.py:333
  81.9 10.0 %collective-permute-start.15 = (bf16[256,512]{1,0:T(8,128)(2,1)}, bf16[256,512]{1,0:T(8,128)(2,1)S(1)}, u32[]{:S(2)}, u32[]{:S(2)}) collective-permute-start(bf16[256,512]{1,0:T(8,128)(2,1)} %get-tuple-element.80), channel_id=1, source_target_pairs={{0,1},{1,0},{2,3},{3,2},{4,5},{5,4},{6,7},{7,6},{8,9},{9,8},{10,11... | collective-permute-start | bytes 786440 | tf_op jit(solution)/shard_map/ppermute | solution.py:333
  90.4 22.4 %collective-permute-start.18 = (bf16[256,512]{1,0:T(8,128)(2,1)}, bf16[256,512]{1,0:T(8,128)(2,1)S(1)}, u32[]{:S(2)}, u32[]{:S(2)}) collective-permute-start(bf16[256,512]{1,0:T(8,128)(2,1)} %get-tuple-element.84), channel_id=1, source_target_pairs={{0,8},{8,0},{1,9},{9,1},{2,10},{10,2},{3,11},{11,3},{4,12},{12,4},... | collective-permute-start | bytes 786440 | tf_op jit(solution)/shard_map/ppermute | solution.py:333
  94.8 5.1 %collective-permute-start.23 = (bf16[2,128,128]{2,1,0:T(8,128)(2,1)S(1)}, bf16[2,128,128]{2,1,0:T(8,128)(2,1)S(1)}, u32[]{:S(2)}, u32[]{:S(2)}) collective-permute-start(bf16[2,128,128]{2,1,0:T(8,128)(2,1)S(1)} %get-tuple-element.91), channel_id=1, source_target_pairs={{0,3},{1,2},{2,1},{3,0},{4,7},{5,6},{6,5},{7,4},{8,11},{9,10},{10,... | collective-permute-start | bytes 196616 | tf_op jit(solution)/shard_map/ppermute | solution.py:399
  94.8 7.1 %collective-permute-start.24 = (bf16[2,128,128]{2,1,0:T(8,128)(2,1)S(1)}, bf16[2,128,128]{2,1,0:T(8,128)(2,1)S(1)}, u32[]{:S(2)}, u32[]{:S(2)}) collective-permute-start(bf16[2,128,128]{2,1,0:T(8,128)(2,1)S(1)} %get-tuple-element.92), channel_id=1, source_target_pairs={{0,4},{1,5},{2,6},{3,7},{4,0},{5,1},{6,2},{7,3},{8,12},{9,13},{10,... | collective-permute-start | bytes 196616 | tf_op jit(solution)/shard_map/ppermute | solution.py:399
  96.2 6.4 %collective-permute-start.25 = (bf16[2,128,128]{2,1,0:T(8,128)(2,1)S(1)}, bf16[2,128,128]{2,1,0:T(8,128)(2,1)S(1)}, u32[]{:S(2)}, u32[]{:S(2)}) collective-permute-start(bf16[2,128,128]{2,1,0:T(8,128)(2,1)S(1)} %get-tuple-element.93), channel_id=1, source_target_pairs={{0,5},{1,4},{2,7},{3,6},{4,1},{5,0},{6,3},{7,2},{8,13},{9,12},{10,... | collective-permute-start | bytes 196616 | tf_op jit(solution)/shard_map/ppermute | solution.py:399
  97.5 15.3 %collective-permute-start.20 = (bf16[2,128,512]{2,1,0:T(8,128)(2,1)S(1)}, bf16[2,128,512]{2,1,0:T(8,128)(2,1)S(1)}, u32[]{:S(2)}, u32[]{:S(2)}) collective-permute-start(bf16[2,128,512]{2,1,0:T(8,128)(2,1)S(1)} %pad_maximum_fusion.4), channel_id=1, source_target_pairs={{0,1},{1,2},{2,3},{3,4},{4,5},{5,6},{6,7},{8,9},{9,10},{10,11},{11... | collective-permute-start | bytes 786440 | tf_op jit(solution)/shard_map/ppermute | solution.py:404
  99.9 12.9 %collective-permute-start.19 = (bf16[256,512]{1,0:T(8,128)(2,1)S(1)}, bf16[256,512]{1,0:T(8,128)(2,1)S(1)}, u32[]{:S(2)}, u32[]{:S(2)}) collective-permute-start(bf16[256,512]{1,0:T(8,128)(2,1)S(1)} %copy-done.13), channel_id=1, source_target_pairs={{0,9},{1,8},{8,1},{9,0},{2,11},{3,10},{10,3},{11,2},{4,13},{5,12},... | collective-permute-start | bytes 786440 | tf_op jit(solution)/shard_map/ppermute | solution.py:338
  102.6 10.2 %collective-permute-start.27 = (bf16[2,128,128]{2,1,0:T(8,128)(2,1)S(1)}, bf16[2,128,128]{2,1,0:T(8,128)(2,1)S(1)}, u32[]{:S(2)}, u32[]{:S(2)}) collective-permute-start(bf16[2,128,128]{2,1,0:T(8,128)(2,1)S(1)} %get-tuple-element.95), channel_id=1, source_target_pairs={{0,7},{1,6},{2,5},{3,4},{4,3},{5,2},{6,1},{7,0},{8,15},{9,14},{10,... | collective-permute-start | bytes 196616 | tf_op jit(solution)/shard_map/ppermute | solution.py:399
  112.9 7.7 %collective-permute-start.28 = (bf16[2,128,512]{2,1,0:T(8,128)(2,1)S(1)}, bf16[2,128,512]{2,1,0:T(8,128)(2,1)S(1)}, u32[]{:S(2)}, u32[]{:S(2)}) collective-permute-start(bf16[2,128,512]{2,1,0:T(8,128)(2,1)S(1)} %pad_maximum_fusion.5), channel_id=1, source_target_pairs={{0,1},{1,2},{2,3},{3,4},{4,5},{5,6},{6,7},{8,9},{9,10},{10,11},{11... | collective-permute-start | bytes 786440 | tf_op jit(solution)/shard_map/ppermute | solution.py:404
  116.0 6.9 %collective-permute-start.30 = (bf16[2,128,128]{2,1,0:T(8,128)(2,1)S(1)}, bf16[2,128,128]{2,1,0:T(8,128)(2,1)S(1)}, u32[]{:S(2)}, u32[]{:S(2)}) collective-permute-start(bf16[2,128,128]{2,1,0:T(8,128)(2,1)S(1)} %get-tuple-element.111), channel_id=1, source_target_pairs={{0,2},{1,3},{2,0},{3,1},{4,6},{5,7},{6,4},{7,5},{8,10},{9,11},{10,... | collective-permute-start | bytes 196616 | tf_op jit(solution)/shard_map/ppermute | solution.py:399
  116.1 12.0 %collective-permute-start.31 = (bf16[2,128,128]{2,1,0:T(8,128)(2,1)S(1)}, bf16[2,128,128]{2,1,0:T(8,128)(2,1)S(1)}, u32[]{:S(2)}, u32[]{:S(2)}) collective-permute-start(bf16[2,128,128]{2,1,0:T(8,128)(2,1)S(1)} %get-tuple-element.112), channel_id=1, source_target_pairs={{0,3},{1,2},{2,1},{3,0},{4,7},{5,6},{6,5},{7,4},{8,11},{9,10},{10,... | collective-permute-start | bytes 196616 | tf_op jit(solution)/shard_map/ppermute | solution.py:399
  117.9 10.2 %collective-permute-start.32 = (bf16[2,128,128]{2,1,0:T(8,128)(2,1)S(1)}, bf16[2,128,128]{2,1,0:T(8,128)(2,1)S(1)}, u32[]{:S(2)}, u32[]{:S(2)}) collective-permute-start(bf16[2,128,128]{2,1,0:T(8,128)(2,1)S(1)} %get-tuple-element.113), channel_id=1, source_target_pairs={{0,4},{1,5},{2,6},{3,7},{4,0},{5,1},{6,2},{7,3},{8,12},{9,13},{10,... | collective-permute-start | bytes 196616 | tf_op jit(solution)/shard_map/ppermute | solution.py:399
  120.6 7.8 %collective-permute-start.33 = (bf16[2,128,128]{2,1,0:T(8,128)(2,1)S(1)}, bf16[2,128,128]{2,1,0:T(8,128)(2,1)S(1)}, u32[]{:S(2)}, u32[]{:S(2)}) collective-permute-start(bf16[2,128,128]{2,1,0:T(8,128)(2,1)S(1)} %get-tuple-element.114), channel_id=1, source_target_pairs={{0,5},{1,4},{2,7},{3,6},{4,1},{5,0},{6,3},{7,2},{8,13},{9,12},{10,... | collective-permute-start | bytes 196616 | tf_op jit(solution)/shard_map/ppermute | solution.py:399
  120.7 10.8 %collective-permute-start.34 = (bf16[2,128,128]{2,1,0:T(8,128)(2,1)S(1)}, bf16[2,128,128]{2,1,0:T(8,128)(2,1)S(1)}, u32[]{:S(2)}, u32[]{:S(2)}) collective-permute-start(bf16[2,128,128]{2,1,0:T(8,128)(2,1)S(1)} %get-tuple-element.115), channel_id=1, source_target_pairs={{0,6},{1,7},{2,4},{3,5},{4,2},{5,3},{6,0},{7,1},{8,14},{9,15},{10,... | collective-permute-start | bytes 196616 | tf_op jit(solution)/shard_map/ppermute | solution.py:399
  122.9 9.7 %collective-permute-start.35 = (bf16[2,128,128]{2,1,0:T(8,128)(2,1)S(1)}, bf16[2,128,128]{2,1,0:T(8,128)(2,1)S(1)}, u32[]{:S(2)}, u32[]{:S(2)}) collective-permute-start(bf16[2,128,128]{2,1,0:T(8,128)(2,1)S(1)} %get-tuple-element.116), channel_id=1, source_target_pairs={{0,7},{1,6},{2,5},{3,4},{4,3},{5,2},{6,1},{7,0},{8,15},{9,14},{10,... | collective-permute-start | bytes 196616 | tf_op jit(solution)/shard_map/ppermute | solution.py:399
  (19 other events, 206.0 us)

commit v5 on v4

--- a/solution.py
+++ b/solution.py
@@ -172,7 +172,7 @@
         cost_estimate=pl.CostEstimate(
             flops=8 * tokens * columns * BLOCK, bytes_accessed=8 * tokens * columns, transcendentals=2 * tokens * columns
         ),
-        compiler_params=pltpu.CompilerParams(vmem_limit_bytes=24 * 1024 * 1024),
+        compiler_params=pltpu.CompilerParams(vmem_limit_bytes=14 * 1024 * 1024),
     )(where, queries, own, own, prev, prev)
     q_spec = pl.BlockSpec((tokens, width), lambda h, place, where: (0, h))
     digit = jnp.arange(DH)[:, None] - jnp.arange(width)[None] // DH
@@ -199,7 +199,7 @@
         cost_estimate=pl.CostEstimate(
             flops=4 * tokens * columns * BLOCK, bytes_accessed=8 * tokens * columns, transcendentals=tokens * columns
         ),
-        compiler_params=pltpu.CompilerParams(vmem_limit_bytes=24 * 1024 * 1024),
+        compiler_params=pltpu.CompilerParams(vmem_limit_bytes=(10 << 20) + 4 * sum(array.nbytes for array in arrived)),
     )(place, where, queries, near, logs, spread, *arrived)
 
 
@@ -276,7 +276,7 @@
         cost_estimate=pl.CostEstimate(
             flops=2 * tokens * depth * width, bytes_accessed=2 * (tokens + width) * depth, transcendentals=0
         ),
-        compiler_params=pltpu.CompilerParams(vmem_limit_bytes=60 * 1024 * 1024),
+        compiler_params=pltpu.CompilerParams(vmem_limit_bytes=14 * 1024 * 1024),
     )(places, *token_runs, *arrays)
 
 
@@ -308,7 +308,7 @@
             scratch_shapes=[pltpu.VMEM((2, *same.shape), jnp.bfloat16)],
         ),
         out_shape=[jax.ShapeDtypeStruct((capacity, BLOCK, DH), jnp.bfloat16)] * devices,
-        compiler_params=pltpu.CompilerParams(vmem_limit_bytes=16 * 1024 * 1024),
+        compiler_params=pltpu.CompilerParams(vmem_limit_bytes=6 * 1024 * 1024),
     )(wanted.reshape(-1), part, same, diff)
 
 
@@ -350,23 +350,22 @@
     notes = by_core(notes[:1], from_c[rows : rows + 1]).reshape(-1, half)
     unit = jnp.concatenate([ours, theirs, notes, jnp.zeros((14, half), jnp.bfloat16)])
 
-    early, late = jnp.split(tokens[0], 2)
-    early, late, unit = lax.optimization_barrier((early, late, unit))
-    x_early = over_x(early)
-    x_late = over_x(late)
+    whole, unit = lax.optimization_barrier((tokens[0], unit))
+    x_tokens = over_x(whole)
     c_tokens = over_c(tokens[0])
 
     deep = 2 * rows
-    from_up, from_down = up(unit), down(unit)
+    from_up = up(unit)
     y_unit = over_y(unit)
-    from_up, y_unit = lax.optimization_barrier((from_up, y_unit))
+    from_up, y_unit, again = lax.optimization_barrier((from_up, y_unit, unit))
+    from_down = down(again)
     y_up = over_y(from_up)
-    from_down, y_up, x_early = lax.optimization_barrier((from_down, y_up, x_early))
+    from_down, y_up = lax.optimization_barrier((from_down, y_up))
     y_down = over_y(from_down)
     far_ours, far_theirs = up(from_up[:deep]), down(from_down[deep:])
     far_ours, y_down = lax.optimization_barrier((far_ours, y_down))
     y_ours, y_theirs = over_y(far_ours), over_y(far_theirs)
-    x_late, far_theirs, y_ours, y_theirs = lax.optimization_barrier((x_late, far_theirs, y_ours, y_theirs))
+    x_tokens, far_theirs, y_ours, y_theirs = lax.optimization_barrier((x_tokens, far_theirs, y_ours, y_theirs))
     arrays, pieces, places = [], [], []
     for value, across, from_z, kinds in (
         (unit, y_unit, z, (0, 1)),
@@ -381,8 +380,7 @@
                 places.append((from_y * 2 + (x ^ kind)) * chips + from_z % chips)
             arrays.append(array)
     places = jnp.stack(places).astype(jnp.int32)
-    xc_early = over_c(x_early)
-    xc_late = over_c(x_late)
+    xc_tokens = over_c(x_tokens)
 
     notes = jnp.stack([unit[2 * deep :], from_up[2 * deep :], from_down[2 * deep :], far_theirs[deep:]])
     notes = notes[:, :2, : targets.size].astype(jnp.int32)
@@ -399,25 +397,20 @@
             lax.ppermute(replies[k], ("z", "c"), [(i, i ^ k) for i in range(devices)]) for k in range(1, devices)
         ]
 
-    def last_block(same, diff):
-        edge = jnp.stack([same[-BLOCK:], diff[-BLOCK:]])
-        return lax.ppermute(edge, ("z", "c"), [(i, i + 1) for i in range(devices - 1)])
-
     same, sent = project([tokens[0], c_tokens], arrays, pieces, places)
     diff = over_c(sent)
-    x_late, sent = lax.optimization_barrier((x_late, sent))
-    x_sent, xc_sent = project([x_early, x_late, xc_early, xc_late], arrays, pieces, places)
+    x_tokens, sent = lax.optimization_barrier((x_tokens, sent))
+    x_sent, xc_sent = project([x_tokens, xc_tokens], arrays, pieces, places)
     x_same, x_diff = over_x(x_sent), over_xc(xc_sent)
     same, diff, x_sent = lax.optimization_barrier((same, diff, x_sent))
     arrived = swap_blocks(pack(wanted, core, same, diff))
-    prev = last_block(same, diff)
-    x_same, x_diff, prev, *arrived = lax.optimization_barrier((x_same, x_diff, prev, *arrived))
-    x_prev = last_block(x_same, x_diff)
+    x_same, x_diff, *arrived = lax.optimization_barrier((x_same, x_diff, *arrived))
     arrived += swap_blocks(pack(wanted, core, x_same, x_diff))
 
     own = jnp.stack([same, diff, x_same, x_diff]).reshape(2, 2, *same.shape)
+    prev = lax.ppermute(own[:, :, -BLOCK:], ("z", "c"), [(i, i + 1) for i in range(devices - 1)])
     where = jnp.stack([(me == 0).astype(jnp.int32), x, c, 1 - c]).astype(jnp.int32)
-    return attend(place, where, queries[0], own, jnp.stack([prev, x_prev]), arrived)[None]
+    return attend(place, where, queries[0], own, prev, arrived)[None]
 
 
 def solution(mesh):

time: 140 us -> 134 us (0.957)
  local copies, waits for them, and re-layouts: 9.76 us -> 2.27 us
  other arithmetic: 4.02 us -> 6.01 us
  Pallas kernels: 27.1 us -> 25.5 us
  waiting for transfers between devices: 62 us -> 63.6 us
    ppermute x18 -> x16, waiting for transfers between devices: 45.4 us -> 49.7 us  [along(): lax.ppermute(value, axis, [(i, (i + step) % count) for i in range(count)])]
    ppermute x14, starting transfers between devices: 12 us -> 16 us  [swap_blocks(): lax.ppermute(replies[k], ('z', 'c'), [(i, i ^ k) for i in range(devices)])]
    pallas_call x2, Pallas kernels: 14.6 us -> 11.9 us  [project(): pl.pallas_call(functools.partial(project_kernel, len(token_runs), len(arr...]
    slice x2, local copies, waits for them, and re-layouts: 2.41 us -> 0.04 us  [local_split(): far_ours, far_theirs = (up(from_up[:deep]), down(from_down[deep:]))]
    ppermute x2 -> x1, starting transfers between devices: 4.53 us -> 2.2 us  [local_split(): lax.ppermute(own[:, :, -BLOCK:], ('z', 'c'), [(i, i + 1) for i in range(d...]
    unnamed x31 -> x13, local copies, waits for them, and re-layouts: 2.37 us -> 0.8 us
    split x1 -> x0, local copies, waits for them, and re-layouts: 1.52 us -> none  [local_split(): early, late = jnp.split(tokens[0], 2)]
    another operation x4, local copies, waits for them, and re-layouts: 1.44 us -> 0.01 us  [local_split(): jnp.stack([unit[2 * deep:], from_up[2 * deep:], from_down[2 * deep:], far...]
  transfers between devices with their start and end apart: 36 -> 33, of which waited for: 14 -> 18; matrix products, arithmetic and copies ran while one was open for 7% -> 4% of each run, Pallas kernels for 15% -> 14%
where the time goes in v5:
time: 134 us; the launch traced here: 132 us
  waiting for transfers between devices  63.6 us (47%)
  starting transfers between devices  34.2 us (26%)
  Pallas kernels  25.5 us (19%)
  other arithmetic  6.01 us (4%)
  local copies, waits for them, and re-layouts  2.27 us (2%)
    ppermute x16, waiting for transfers between devices, along(): lax.ppermute(value, axis, [(i, (i + step) % count) for i in range(count)])  49.7 us
    ppermute x14, starting transfers between devices, swap_blocks(): lax.ppermute(replies[k], ('z', 'c'), [(i, i ^ k) for i in range(devices)])  16 us
    ppermute x16, starting transfers between devices, along(): lax.ppermute(value, axis, [(i, (i + step) % count) for i in range(count)])  14.8 us
    ppermute x14, waiting for transfers between devices, swap_blocks(): lax.ppermute(replies[k], ('z', 'c'), [(i, i ^ k) for i in range(devices)])  12.3 us
    pallas_call x2, Pallas kernels, project(): pl.pallas_call(functools.partial(project_kernel, len(token_runs), len(arr...  11.9 us
    pallas_call x1, Pallas kernels, attend(): pl.pallas_call(functools.partial(far_kernel, len(arrived)), grid_spec=plt...  5.71 us
    pallas_call x1, Pallas kernels, attend(): pl.pallas_call(near_kernel, grid_spec=pltpu.PrefetchScalarGridSpec(num_sc...  5.26 us
  transfers between devices with their start and end apart: 33, of which 18 were waited for; matrix products, arithmetic and copies ran while one was open for 4% of the time, Pallas kernels for 14%

profile of v5, /device:TPU:16, one launch (start us, length us, event | category | flops | bytes accessed | tf_op | source)
XLA Modules:
  0.0 132.0 jit_solution(15910056727063050532)
XLA Ops:
  1.1 1.6 %collective-permute-start.2 = (bf16[128,512]{1,0:T(8,128)(2,1)S(1)}, bf16[128,512]{1,0:T(8,128)(2,1)S(1)}, u32[]{:S(2)}, u32[]{:S(2)}) collective-permute-start(bf16[128,512]{1,0:T(8,128)(2,1)S(1)} %get-tuple-element.119), channel_id=1, source_target_pairs={{0,8},{8,0},{1,9},{9,1},{2,10},{10,2},{3,11},{11,3},{4,12},{12,4},... | collective-permute-start | bytes 393224 | tf_op jit(solution)/shard_map/ppermute | solution.py:333
  3.7 3.5 %collective-permute-done.2 = bf16[128,512]{1,0:T(8,128)(2,1)S(1)} collective-permute-done((bf16[128,512]{1,0:T(8,128)(2,1)S(1)}, bf16[128,512]{1,0:T(8,128)(2,1)S(1)}, u32[]{:S(2)}, u32[]{:S(2)}) %collective-permute-start.2) | collective-permute-done | bytes 131104 | tf_op jit(solution)/shard_map/ppermute | solution.py:333
  10.2 1.6 %collective-permute-start.4 = (bf16[528,512]{1,0:T(8,128)(2,1)S(1)}, bf16[528,512]{1,0:T(8,128)(2,1)S(1)}, u32[]{:S(2)}, u32[]{:S(2)}) collective-permute-start(bf16[528,512]{1,0:T(8,128)(2,1)S(1)} %maximum_maximum_fusion.refs_2_), channel_id=1, source_target_pairs={{0,2},{2,4},{4,6},{6,0},{1,3},{3,5},{5,7},{7,1},{8,10},{10,12},{12... | collective-permute-start | bytes 1622024 | tf_op jit(solution)/shard_map/ppermute | solution.py:333
  11.8 1.5 %collective-permute-start.5 = (bf16[528,512]{1,0:T(8,128)(2,1)S(1)}, bf16[528,512]{1,0:T(8,128)(2,1)S(1)}, u32[]{:S(2)}, u32[]{:S(2)}) collective-permute-start(bf16[528,512]{1,0:T(8,128)(2,1)S(1)} %maximum_maximum_fusion.refs_2_), channel_id=1, source_target_pairs={{0,16},{16,0},{1,17},{17,1},{2,18},{18,2},{3,19},{19,3},{4,20},{20... | collective-permute-start | bytes 1622024 | tf_op jit(solution)/shard_map/ppermute | solution.py:333
  13.3 11.8 %collective-permute-done.4.refs_4_ = bf16[528,512]{1,0:T(8,128)(2,1)S(1)} collective-permute-done((bf16[528,512]{1,0:T(8,128)(2,1)S(1)}, bf16[528,512]{1,0:T(8,128)(2,1)S(1)}, u32[]{:S(2)}, u32[]{:S(2)}) %collective-permute-start.4) | collective-permute-done | bytes 540704 | tf_op jit(solution)/shard_map/ppermute | solution.py:333
  25.1 1.3 collective-permute-done.5.refs_3_
  26.9 1.5 %collective-permute-start.7 = (bf16[528,512]{1,0:T(8,128)(2,1)S(1)}, bf16[528,512]{1,0:T(8,128)(2,1)S(1)}, u32[]{:S(2)}, u32[]{:S(2)}) collective-permute-start(bf16[528,512]{1,0:T(8,128)(2,1)S(1)} %collective-permute-done.4.refs_4_), channel_id=1, source_target_pairs={{0,16},{16,0},{1,17},{17,1},{2,18},{18,2},{3,19},{19,3},{4,20},{20... | collective-permute-start | bytes 1622024 | tf_op jit(solution)/shard_map/ppermute | solution.py:333
  28.4 11.9 %collective-permute-done.6.refs_6_ = bf16[528,512]{1,0:T(8,128)(2,1)S(1)} collective-permute-done((bf16[528,512]{1,0:T(8,128)(2,1)S(1)}, bf16[528,512]{1,0:T(8,128)(2,1)S(1)}, u32[]{:S(2)}, u32[]{:S(2)}) %collective-permute-start.6) | collective-permute-done | bytes 540704 | tf_op jit(solution)/shard_map/ppermute | solution.py:333
  40.5 1.5 %collective-permute-start.9 = (bf16[528,512]{1,0:T(8,128)(2,1)S(1)}, bf16[528,512]{1,0:T(8,128)(2,1)S(1)}, u32[]{:S(2)}, u32[]{:S(2)}) collective-permute-start(bf16[528,512]{1,0:T(8,128)(2,1)S(1)} %collective-permute-done.6.refs_6_), channel_id=1, source_target_pairs={{0,16},{16,0},{1,17},{17,1},{2,18},{18,2},{3,19},{19,3},{4,20},{20... | collective-permute-start | bytes 1622024 | tf_op jit(solution)/shard_map/ppermute | solution.py:333
  42.1 2.1 %collective-permute-start.8 = (bf16[256,512]{1,0:T(8,128)(2,1)S(1)}, bf16[256,512]{1,0:T(8,128)(2,1)}, u32[]{:S(2)}, u32[]{:S(2)}) collective-permute-start(bf16[256,512]{1,0:T(8,128)(2,1)S(1)} %slice.52), channel_id=1, source_target_pairs={{0,2},{2,4},{4,6},{6,0},{1,3},{3,5},{5,7},{7,1},{8,10},{10,12},{12... | collective-permute-start | bytes 786440 | tf_op jit(solution)/shard_map/ppermute | solution.py:333
  44.4 12.4 %collective-permute-done.11.refs_10_ = bf16[272,512]{1,0:T(8,128)(2,1)S(1)} collective-permute-done((bf16[272,512]{1,0:T(8,128)(2,1)S(1)}, bf16[272,512]{1,0:T(8,128)(2,1)S(1)}, u32[]{:S(2)}, u32[]{:S(2)}) %collective-permute-start.11) | collective-permute-done | bytes 278560 | tf_op jit(solution)/shard_map/ppermute | solution.py:333
  57.2 1.5 %collective-permute-start.12 = (bf16[256,512]{1,0:T(8,128)(2,1)}, bf16[256,512]{1,0:T(8,128)(2,1)}, u32[]{:S(2)}, u32[]{:S(2)}) collective-permute-start(bf16[256,512]{1,0:T(8,128)(2,1)} %collective-permute-done.8.refs_8_), channel_id=1, source_target_pairs={{0,16},{16,0},{1,17},{17,1},{2,18},{18,2},{3,19},{19,3},{4,20},{20... | collective-permute-start | bytes 786440 | tf_op jit(solution)/shard_map/ppermute | solution.py:333
  60.2 5.9 %collective-permute-done.13.refs_11_ = bf16[272,512]{1,0:T(8,128)(2,1)} collective-permute-done((bf16[272,512]{1,0:T(8,128)(2,1)S(1)}, bf16[272,512]{1,0:T(8,128)(2,1)}, u32[]{:S(2)}, u32[]{:S(2)}) %collective-permute-start.13) | collective-permute-done | bytes 278560 | tf_op jit(solution)/shard_map/ppermute | solution.py:333
  66.0 2.8 %collective-permute-done.12.refs_9_ = bf16[256,512]{1,0:T(8,128)(2,1)} collective-permute-done((bf16[256,512]{1,0:T(8,128)(2,1)}, bf16[256,512]{1,0:T(8,128)(2,1)}, u32[]{:S(2)}, u32[]{:S(2)}) %collective-permute-start.12) | collective-permute-done | bytes 262176 | tf_op jit(solution)/shard_map/ppermute | solution.py:333
  68.9 6.0 %shard_map.64 = (bf16[256,512]{1,0:T(8,128)(2,1)S(1)}, bf16[256,512]{1,0:T(8,128)(2,1)}) custom-call(s32[16]{0:T(128)S(1)} %stack.148.place_ref, bf16[256,4096]{1,0:T(8,128)(2,1)} %bitcast.21.refs_0_, bf16[256,4096]{1,0:T(8,128)(2,1)} %collective-permute-done.refs_1_, bf16[528,512]{1,0:T(8,128)(2,1)S(1)} %maximum_maximum_fusion.refs_2_, ...), custom_call_target="tpu_custom_call" | custom-call | flops 2147483648 | bytes 8388608 | tf_op jit(solution)/shard_map/pallas_call | solution.py:261
  77.9 6.0 %shard_map.65 = (bf16[256,512]{1,0:T(8,128)(2,1)}, bf16[256,512]{1,0:T(8,128)(2,1)}) custom-call(s32[16]{0:T(128)S(1)} %stack.148.place_ref, bf16[256,4096]{1,0:T(8,128)(2,1)} %collective-permute-done.10.refs_0_, bf16[256,4096]{1,0:T(8,128)(2,1)} %collective-permute-done.15.refs_1_, bf16[528,512]{1,0:T(8,128)(2,1)S(1)} %maximum_maximum_fusion.refs_2_, ...), custom_call_target="tpu_custom_call" | custom-call | flops 2147483648 | bytes 8388608 | tf_op jit(solution)/shard_map/pallas_call | solution.py:261
  83.9 1.8 %shard_map.66 = (bf16[2,128,128]{2,1,0:T(8,128)(2,1)S(1)}, bf16[2,128,128]{2,1,0:T(8,128)(2,1)S(1)}, bf16[2,128,128]{2,1,0:T(8,128)(2,1)S(1)}, bf16[2,128,128]{2...) custom-call(s32[16]{0:T(128)S(1)} %select_n.204.row_ref, ...), custom_call_target="tpu_custom_call" | custom-call | tf_op jit(solution)/shard_map/pallas_call | solution.py:301
  86.3 1.6 %collective-permute-start.20 = (bf16[2,128,128]{2,1,0:T(8,128)(2,1)S(1)}, bf16[2,128,128]{2,1,0:T(8,128)(2,1)S(1)}, u32[]{:S(2)}, u32[]{:S(2)}) collective-permute-start(bf16[2,128,128]{2,1,0:T(8,128)(2,1)S(1)} %get-tuple-element.88), channel_id=1, source_target_pairs={{0,3},{1,2},{2,1},{3,0},{4,7},{5,6},{6,5},{7,4},{8,11},{9,10},{10,... | collective-permute-start | bytes 196616 | tf_op jit(solution)/shard_map/ppermute | solution.py:397
  87.9 1.7 %collective-permute-start.21 = (bf16[2,128,128]{2,1,0:T(8,128)(2,1)S(1)}, bf16[2,128,128]{2,1,0:T(8,128)(2,1)S(1)}, u32[]{:S(2)}, u32[]{:S(2)}) collective-permute-start(bf16[2,128,128]{2,1,0:T(8,128)(2,1)S(1)} %get-tuple-element.89), channel_id=1, source_target_pairs={{0,4},{1,5},{2,6},{3,7},{4,0},{5,1},{6,2},{7,3},{8,12},{9,13},{10,... | collective-permute-start | bytes 196616 | tf_op jit(solution)/shard_map/ppermute | solution.py:397
  91.0 1.3 %collective-permute-start.22 = (bf16[2,128,128]{2,1,0:T(8,128)(2,1)S(1)}, bf16[2,128,128]{2,1,0:T(8,128)(2,1)S(1)}, u32[]{:S(2)}, u32[]{:S(2)}) collective-permute-start(bf16[2,128,128]{2,1,0:T(8,128)(2,1)S(1)} %get-tuple-element.90), channel_id=1, source_target_pairs={{0,5},{1,4},{2,7},{3,6},{4,1},{5,0},{6,3},{7,2},{8,13},{9,12},{10,... | collective-permute-start | bytes 196616 | tf_op jit(solution)/shard_map/ppermute | solution.py:397
  92.3 1.9 %collective-permute-start.23 = (bf16[2,128,128]{2,1,0:T(8,128)(2,1)S(1)}, bf16[2,128,128]{2,1,0:T(8,128)(2,1)S(1)}, u32[]{:S(2)}, u32[]{:S(2)}) collective-permute-start(bf16[2,128,128]{2,1,0:T(8,128)(2,1)S(1)} %get-tuple-element.91), channel_id=1, source_target_pairs={{0,6},{1,7},{2,4},{3,5},{4,2},{5,3},{6,0},{7,1},{8,14},{9,15},{10,... | collective-permute-start | bytes 196616 | tf_op jit(solution)/shard_map/ppermute | solution.py:397
  94.7 1.4 %collective-permute-done.22.refs_5_ = bf16[2,128,128]{2,1,0:T(8,128)(2,1)S(1)} collective-permute-done((bf16[2,128,128]{2,1,0:T(8,128)(2,1)S(1)}, bf16[2,128,128]{2,1,0:T(8,128)(2,1)S(1)}, u32[]{:S(2)}, u32[]{:S(2)}) %collective-permute-start.22) | collective-permute-done | bytes 65568 | tf_op jit(solution)/shard_map/ppermute | solution.py:397
  96.1 5.9 %collective-permute-done.23.refs_6_ = bf16[2,128,128]{2,1,0:T(8,128)(2,1)S(1)} collective-permute-done((bf16[2,128,128]{2,1,0:T(8,128)(2,1)S(1)}, bf16[2,128,128]{2,1,0:T(8,128)(2,1)S(1)}, u32[]{:S(2)}, u32[]{:S(2)}) %collective-permute-start.23) | collective-permute-done | bytes 65568 | tf_op jit(solution)/shard_map/ppermute | solution.py:397
  103.2 1.3 pad_maximum_fusion
  104.6 2.2 %collective-permute-start.25 = (bf16[2,2,128,512]{3,2,1,0:T(8,128)(2,1)S(1)}, bf16[2,2,128,512]{3,2,1,0:T(8,128)(2,1)S(1)}, u32[]{:S(2)}, u32[]{:S(2)}) collective-permute-start(bf16[2,2,128,512]{3,2,1,0:T(8,128)(2,1)S(1)} %slice.64), channel_id=1, source_target_pairs={{0,1},{1,2},{2,3},{3,4},{4,5},{5,6},{6,7},{8,9},{9,10},{10,11},{11... | collective-permute-start | bytes 1572872 | tf_op jit(solution)/shard_map/ppermute | solution.py:411
  108.5 1.8 %collective-permute-start.28 = (bf16[2,128,128]{2,1,0:T(8,128)(2,1)S(1)}, bf16[2,128,128]{2,1,0:T(8,128)(2,1)S(1)}, u32[]{:S(2)}, u32[]{:S(2)}) collective-permute-start(bf16[2,128,128]{2,1,0:T(8,128)(2,1)S(1)} %get-tuple-element.108), channel_id=1, source_target_pairs={{0,3},{1,2},{2,1},{3,0},{4,7},{5,6},{6,5},{7,4},{8,11},{9,10},{10,... | collective-permute-start | bytes 196616 | tf_op jit(solution)/shard_map/ppermute | solution.py:397
  110.3 1.7 %collective-permute-start.29 = (bf16[2,128,128]{2,1,0:T(8,128)(2,1)S(1)}, bf16[2,128,128]{2,1,0:T(8,128)(2,1)S(1)}, u32[]{:S(2)}, u32[]{:S(2)}) collective-permute-start(bf16[2,128,128]{2,1,0:T(8,128)(2,1)S(1)} %get-tuple-element.109), channel_id=1, source_target_pairs={{0,4},{1,5},{2,6},{3,7},{4,0},{5,1},{6,2},{7,3},{8,12},{9,13},{10,... | collective-permute-start | bytes 196616 | tf_op jit(solution)/shard_map/ppermute | solution.py:397
  113.3 2.1 %collective-permute-start.31 = (bf16[2,128,128]{2,1,0:T(8,128)(2,1)S(1)}, bf16[2,128,128]{2,1,0:T(8,128)(2,1)S(1)}, u32[]{:S(2)}, u32[]{:S(2)}) collective-permute-start(bf16[2,128,128]{2,1,0:T(8,128)(2,1)S(1)} %get-tuple-element.111), channel_id=1, source_target_pairs={{0,6},{1,7},{2,4},{3,5},{4,2},{5,3},{6,0},{7,1},{8,14},{9,15},{10,... | collective-permute-start | bytes 196616 | tf_op jit(solution)/shard_map/ppermute | solution.py:397
  115.8 2.4 %collective-permute-start.32 = (bf16[2,128,128]{2,1,0:T(8,128)(2,1)S(1)}, bf16[2,128,128]{2,1,0:T(8,128)(2,1)S(1)}, u32[]{:S(2)}, u32[]{:S(2)}) collective-permute-start(bf16[2,128,128]{2,1,0:T(8,128)(2,1)S(1)} %get-tuple-element.112), channel_id=1, source_target_pairs={{0,7},{1,6},{2,5},{3,4},{4,3},{5,2},{6,1},{7,0},{8,15},{9,14},{10,... | collective-permute-start | bytes 196616 | tf_op jit(solution)/shard_map/ppermute | solution.py:397
  118.2 5.3 %shard_map.67 = (f32[256,4096]{1,0:T(8,128)S(1)}, bf16[256,256]{1,0:T(8,128)(2,1)S(1)}) custom-call(s32[4]{0:T(128)S(1)} %pad_add_fusion.where_ref, bf16[256,4096]{1,0:T(8,128)(2,1)S(1)} %bitcast.56, bf16[2,2,256,512]{3,2,1,0:T(8,128)(2,1)S(1)} %bitcast.54, bf16[2,2,256,512]{3,2,1,0:T(8,128)(2,1)S(1)} %bitcast.55, ...), custom_call_target="tpu_custom_call" | custom-call | flops 1073741824 | bytes 8388608 | tf_op jit(solution)/shard_map/pallas_call | solution.py:151
  124.8 1.5 %collective-permute-done.32.refs_15_ = bf16[2,128,128]{2,1,0:T(8,128)(2,1)S(1)} collective-permute-done((bf16[2,128,128]{2,1,0:T(8,128)(2,1)S(1)}, bf16[2,128,128]{2,1,0:T(8,128)(2,1)S(1)}, u32[]{:S(2)}, u32[]{:S(2)}) %collective-permute-start.32) | collective-permute-done | bytes 65568 | tf_op jit(solution)/shard_map/ppermute | solution.py:397
  126.3 5.7 %shard_map.69 = bf16[256,4096]{1,0:T(8,128)(2,1)} custom-call(s32[16]{0:T(128)S(1)} %add_xor_fusion.place_ref, s32[4]{0:T(128)S(1)} %pad_add_fusion.where_ref, bf16[256,4096]{1,0:T(8,128)(2,1)S(1)} %bitcast.57, f32[256,4096]{1,0:T(8,128)S(1)} %get-tuple-element.95.near_ref, bf16[256,256]{1,0:T(8,128)(2,1)S(1)} %get-tuple-element.96.log_ref, ...), custom_call_target="tpu_custom_call" | custom-call | flops 536870912 | bytes 8388608 | tf_op jit(solution)/shard_map/pallas_call | solution.py:181
  (107 shorter events, 19.3 us)
Async XLA Ops:
  1.1 6.1 %collective-permute-start.2 = (bf16[128,512]{1,0:T(8,128)(2,1)S(1)}, bf16[128,512]{1,0:T(8,128)(2,1)S(1)}, u32[]{:S(2)}, u32[]{:S(2)}) collective-permute-start(bf16[128,512]{1,0:T(8,128)(2,1)S(1)} %get-tuple-element.119), channel_id=1, source_target_pairs={{0,8},{8,0},{1,9},{9,1},{2,10},{10,2},{3,11},{11,3},{4,12},{12,4},... | collective-permute-start | bytes 393224 | tf_op jit(solution)/shard_map/ppermute | solution.py:333
  2.7 5.8 %collective-permute-start.3 = (bf16[128,512]{1,0:T(8,128)(2,1)S(1)}, bf16[128,512]{1,0:T(8,128)(2,1)S(1)}, u32[]{:S(2)}, u32[]{:S(2)}) collective-permute-start(bf16[128,512]{1,0:T(8,128)(2,1)S(1)} %get-tuple-element.120), channel_id=1, source_target_pairs={{0,9},{1,8},{8,1},{9,0},{2,11},{3,10},{10,3},{11,2},{4,13},{5,12},... | collective-permute-start | bytes 393224 | tf_op jit(solution)/shard_map/ppermute | solution.py:338
  2.9 5.6 %collective-permute-start.1 = (bf16[144,512]{1,0:T(8,128)(2,1)S(1)}, bf16[144,512]{1,0:T(8,128)(2,1)S(1)}, u32[]{:S(2)}, u32[]{:S(2)}) collective-permute-start(bf16[144,512]{1,0:T(8,128)(2,1)S(1)} %pad_maximum_fusion.3), channel_id=1, source_target_pairs={{0,1},{1,0},{2,3},{3,2},{4,5},{5,4},{6,7},{7,6},{8,9},{9,8},{10,11... | collective-permute-start | bytes 442376 | tf_op jit(solution)/shard_map/ppermute | solution.py:333
  9.0 59.8 %collective-permute-start.10 = (bf16[256,4096]{1,0:T(8,128)(2,1)}, bf16[256,4096]{1,0:T(8,128)(2,1)}, u32[]{:S(2)}, u32[]{:S(2)}) collective-permute-start(bf16[256,4096]{1,0:T(8,128)(2,1)} %bitcast.21.refs_0_), channel_id=1, source_target_pairs={{0,8},{8,0},{1,9},{9,1},{2,10},{10,2},{3,11},{11,3},{4,12},{12,4},... | collective-permute-start | bytes 6291464 | tf_op jit(solution)/shard_map/ppermute | solution.py:333
  10.2 14.9 %collective-permute-start.4 = (bf16[528,512]{1,0:T(8,128)(2,1)S(1)}, bf16[528,512]{1,0:T(8,128)(2,1)S(1)}, u32[]{:S(2)}, u32[]{:S(2)}) collective-permute-start(bf16[528,512]{1,0:T(8,128)(2,1)S(1)} %maximum_maximum_fusion.refs_2_), channel_id=1, source_target_pairs={{0,2},{2,4},{4,6},{6,0},{1,3},{3,5},{5,7},{7,1},{8,10},{10,12},{12... | collective-permute-start | bytes 1622024 | tf_op jit(solution)/shard_map/ppermute | solution.py:333
  11.8 14.6 %collective-permute-start.5 = (bf16[528,512]{1,0:T(8,128)(2,1)S(1)}, bf16[528,512]{1,0:T(8,128)(2,1)S(1)}, u32[]{:S(2)}, u32[]{:S(2)}) collective-permute-start(bf16[528,512]{1,0:T(8,128)(2,1)S(1)} %maximum_maximum_fusion.refs_2_), channel_id=1, source_target_pairs={{0,16},{16,0},{1,17},{17,1},{2,18},{18,2},{3,19},{19,3},{4,20},{20... | collective-permute-start | bytes 1622024 | tf_op jit(solution)/shard_map/ppermute | solution.py:333
  26.4 13.9 %collective-permute-start.6 = (bf16[528,512]{1,0:T(8,128)(2,1)S(1)}, bf16[528,512]{1,0:T(8,128)(2,1)S(1)}, u32[]{:S(2)}, u32[]{:S(2)}) collective-permute-start(bf16[528,512]{1,0:T(8,128)(2,1)S(1)} %maximum_maximum_fusion.refs_2_), channel_id=1, source_target_pairs={{0,6},{2,0},{4,2},{6,4},{1,7},{3,1},{5,3},{7,5},{8,14},{10,8},{12,... | collective-permute-start | bytes 1622024 | tf_op jit(solution)/shard_map/ppermute | solution.py:333
  26.9 13.6 %collective-permute-start.7 = (bf16[528,512]{1,0:T(8,128)(2,1)S(1)}, bf16[528,512]{1,0:T(8,128)(2,1)S(1)}, u32[]{:S(2)}, u32[]{:S(2)}) collective-permute-start(bf16[528,512]{1,0:T(8,128)(2,1)S(1)} %collective-permute-done.4.refs_4_), channel_id=1, source_target_pairs={{0,16},{16,0},{1,17},{17,1},{2,18},{18,2},{3,19},{19,3},{4,20},{20... | collective-permute-start | bytes 1622024 | tf_op jit(solution)/shard_map/ppermute | solution.py:333
  28.4 40.5 %collective-permute-start = (bf16[256,4096]{1,0:T(8,128)(2,1)}, bf16[256,4096]{1,0:T(8,128)(2,1)}, u32[]{:S(2)}, u32[]{:S(2)}) collective-permute-start(bf16[256,4096]{1,0:T(8,128)(2,1)} %bitcast.21.refs_0_), channel_id=1, source_target_pairs={{0,1},{1,0},{2,3},{3,2},{4,5},{5,4},{6,7},{7,6},{8,9},{9,8},{10,11... | collective-permute-start | bytes 6291464 | tf_op jit(solution)/shard_map/ppermute | solution.py:333
  40.5 16.8 %collective-permute-start.9 = (bf16[528,512]{1,0:T(8,128)(2,1)S(1)}, bf16[528,512]{1,0:T(8,128)(2,1)S(1)}, u32[]{:S(2)}, u32[]{:S(2)}) collective-permute-start(bf16[528,512]{1,0:T(8,128)(2,1)S(1)} %collective-permute-done.6.refs_6_), channel_id=1, source_target_pairs={{0,16},{16,0},{1,17},{17,1},{2,18},{18,2},{3,19},{19,3},{4,20},{20... | collective-permute-start | bytes 1622024 | tf_op jit(solution)/shard_map/ppermute | solution.py:333
  42.1 15.2 %collective-permute-start.8 = (bf16[256,512]{1,0:T(8,128)(2,1)S(1)}, bf16[256,512]{1,0:T(8,128)(2,1)}, u32[]{:S(2)}, u32[]{:S(2)}) collective-permute-start(bf16[256,512]{1,0:T(8,128)(2,1)S(1)} %slice.52), channel_id=1, source_target_pairs={{0,2},{2,4},{4,6},{6,0},{1,3},{3,5},{5,7},{7,1},{8,10},{10,12},{12... | collective-permute-start | bytes 786440 | tf_op jit(solution)/shard_map/ppermute | solution.py:333
  44.2 12.5 %collective-permute-start.11 = (bf16[272,512]{1,0:T(8,128)(2,1)S(1)}, bf16[272,512]{1,0:T(8,128)(2,1)S(1)}, u32[]{:S(2)}, u32[]{:S(2)}) collective-permute-start(bf16[272,512]{1,0:T(8,128)(2,1)S(1)} %slice.53), channel_id=1, source_target_pairs={{0,6},{2,0},{4,2},{6,4},{1,7},{3,1},{5,3},{7,5},{8,14},{10,8},{12,... | collective-permute-start | bytes 835592 | tf_op jit(solution)/shard_map/ppermute | solution.py:333
  56.7 9.3 %collective-permute-start.13 = (bf16[272,512]{1,0:T(8,128)(2,1)S(1)}, bf16[272,512]{1,0:T(8,128)(2,1)}, u32[]{:S(2)}, u32[]{:S(2)}) collective-permute-start(bf16[272,512]{1,0:T(8,128)(2,1)S(1)} %collective-permute-done.11.refs_10_), channel_id=1, source_target_pairs={{0,16},{16,0},{1,17},{17,1},{2,18},{18,2},{3,19},{19,3},{4,20},{20... | collective-permute-start | bytes 835592 | tf_op jit(solution)/shard_map/ppermute | solution.py:333
  57.2 11.6 %collective-permute-start.12 = (bf16[256,512]{1,0:T(8,128)(2,1)}, bf16[256,512]{1,0:T(8,128)(2,1)}, u32[]{:S(2)}, u32[]{:S(2)}) collective-permute-start(bf16[256,512]{1,0:T(8,128)(2,1)} %collective-permute-done.8.refs_8_), channel_id=1, source_target_pairs={{0,16},{16,0},{1,17},{17,1},{2,18},{18,2},{3,19},{19,3},{4,20},{20... | collective-permute-start | bytes 786440 | tf_op jit(solution)/shard_map/ppermute | solution.py:333
  68.8 9.1 %collective-permute-start.15 = (bf16[256,4096]{1,0:T(8,128)(2,1)}, bf16[256,4096]{1,0:T(8,128)(2,1)}, u32[]{:S(2)}, u32[]{:S(2)}) collective-permute-start(bf16[256,4096]{1,0:T(8,128)(2,1)} %collective-permute-done.10.refs_0_), channel_id=1, source_target_pairs={{0,1},{1,0},{2,3},{3,2},{4,5},{5,4},{6,7},{7,6},{8,9},{9,8},{10,11... | collective-permute-start | bytes 6291464 | tf_op jit(solution)/shard_map/ppermute | solution.py:333
  75.6 8.3 %collective-permute-start.14 = (bf16[256,512]{1,0:T(8,128)(2,1)}, bf16[256,512]{1,0:T(8,128)(2,1)}, u32[]{:S(2)}, u32[]{:S(2)}) collective-permute-start(bf16[256,512]{1,0:T(8,128)(2,1)} %get-tuple-element.78), channel_id=1, source_target_pairs={{0,1},{1,0},{2,3},{3,2},{4,5},{5,4},{6,7},{7,6},{8,9},{9,8},{10,11... | collective-permute-start | bytes 786440 | tf_op jit(solution)/shard_map/ppermute | solution.py:333
  85.7 3.9 %collective-permute-start.18 = (bf16[2,128,128]{2,1,0:T(8,128)(2,1)S(1)}, bf16[2,128,128]{2,1,0:T(8,128)(2,1)S(1)}, u32[]{:S(2)}, u32[]{:S(2)}) collective-permute-start(bf16[2,128,128]{2,1,0:T(8,128)(2,1)S(1)} %get-tuple-element.86), channel_id=1, source_target_pairs={{0,1},{1,0},{2,3},{3,2},{4,5},{5,4},{6,7},{7,6},{8,9},{9,8},{10,11... | collective-permute-start | bytes 196616 | tf_op jit(solution)/shard_map/ppermute | solution.py:397
  86.0 17.3 %collective-permute-start.16 = (bf16[256,512]{1,0:T(8,128)(2,1)}, bf16[256,512]{1,0:T(8,128)(2,1)S(1)}, u32[]{:S(2)}, u32[]{:S(2)}) collective-permute-start(bf16[256,512]{1,0:T(8,128)(2,1)} %get-tuple-element.81), channel_id=1, source_target_pairs={{0,8},{8,0},{1,9},{9,1},{2,10},{10,2},{3,11},{11,3},{4,12},{12,4},... | collective-permute-start | bytes 786440 | tf_op jit(solution)/shard_map/ppermute | solution.py:333
  86.0 5.0 %collective-permute-start.19 = (bf16[2,128,128]{2,1,0:T(8,128)(2,1)S(1)}, bf16[2,128,128]{2,1,0:T(8,128)(2,1)S(1)}, u32[]{:S(2)}, u32[]{:S(2)}) collective-permute-start(bf16[2,128,128]{2,1,0:T(8,128)(2,1)S(1)} %get-tuple-element.87), channel_id=1, source_target_pairs={{0,2},{1,3},{2,0},{3,1},{4,6},{5,7},{6,4},{7,5},{8,10},{9,11},{10,... | collective-permute-start | bytes 196616 | tf_op jit(solution)/shard_map/ppermute | solution.py:397
  86.3 6.0 %collective-permute-start.20 = (bf16[2,128,128]{2,1,0:T(8,128)(2,1)S(1)}, bf16[2,128,128]{2,1,0:T(8,128)(2,1)S(1)}, u32[]{:S(2)}, u32[]{:S(2)}) collective-permute-start(bf16[2,128,128]{2,1,0:T(8,128)(2,1)S(1)} %get-tuple-element.88), channel_id=1, source_target_pairs={{0,3},{1,2},{2,1},{3,0},{4,7},{5,6},{6,5},{7,4},{8,11},{9,10},{10,... | collective-permute-start | bytes 196616 | tf_op jit(solution)/shard_map/ppermute | solution.py:397
  87.9 6.8 %collective-permute-start.21 = (bf16[2,128,128]{2,1,0:T(8,128)(2,1)S(1)}, bf16[2,128,128]{2,1,0:T(8,128)(2,1)S(1)}, u32[]{:S(2)}, u32[]{:S(2)}) collective-permute-start(bf16[2,128,128]{2,1,0:T(8,128)(2,1)S(1)} %get-tuple-element.89), channel_id=1, source_target_pairs={{0,4},{1,5},{2,6},{3,7},{4,0},{5,1},{6,2},{7,3},{8,12},{9,13},{10,... | collective-permute-start | bytes 196616 | tf_op jit(solution)/shard_map/ppermute | solution.py:397
  89.6 13.6 %collective-permute-start.17 = (bf16[256,512]{1,0:T(8,128)(2,1)}, bf16[256,512]{1,0:T(8,128)(2,1)S(1)}, u32[]{:S(2)}, u32[]{:S(2)}) collective-permute-start(bf16[256,512]{1,0:T(8,128)(2,1)} %get-tuple-element.84), channel_id=1, source_target_pairs={{0,9},{1,8},{8,1},{9,0},{2,11},{3,10},{10,3},{11,2},{4,13},{5,12},... | collective-permute-start | bytes 786440 | tf_op jit(solution)/shard_map/ppermute | solution.py:338
  91.0 5.1 %collective-permute-start.22 = (bf16[2,128,128]{2,1,0:T(8,128)(2,1)S(1)}, bf16[2,128,128]{2,1,0:T(8,128)(2,1)S(1)}, u32[]{:S(2)}, u32[]{:S(2)}) collective-permute-start(bf16[2,128,128]{2,1,0:T(8,128)(2,1)S(1)} %get-tuple-element.90), channel_id=1, source_target_pairs={{0,5},{1,4},{2,7},{3,6},{4,1},{5,0},{6,3},{7,2},{8,13},{9,12},{10,... | collective-permute-start | bytes 196616 | tf_op jit(solution)/shard_map/ppermute | solution.py:397
  92.3 9.7 %collective-permute-start.23 = (bf16[2,128,128]{2,1,0:T(8,128)(2,1)S(1)}, bf16[2,128,128]{2,1,0:T(8,128)(2,1)S(1)}, u32[]{:S(2)}, u32[]{:S(2)}) collective-permute-start(bf16[2,128,128]{2,1,0:T(8,128)(2,1)S(1)} %get-tuple-element.91), channel_id=1, source_target_pairs={{0,6},{1,7},{2,4},{3,5},{4,2},{5,3},{6,0},{7,1},{8,14},{9,15},{10,... | collective-permute-start | bytes 196616 | tf_op jit(solution)/shard_map/ppermute | solution.py:397
  94.7 8.5 %collective-permute-start.24 = (bf16[2,128,128]{2,1,0:T(8,128)(2,1)S(1)}, bf16[2,128,128]{2,1,0:T(8,128)(2,1)S(1)}, u32[]{:S(2)}, u32[]{:S(2)}) collective-permute-start(bf16[2,128,128]{2,1,0:T(8,128)(2,1)S(1)} %get-tuple-element.92), channel_id=1, source_target_pairs={{0,7},{1,6},{2,5},{3,4},{4,3},{5,2},{6,1},{7,0},{8,15},{9,14},{10,... | collective-permute-start | bytes 196616 | tf_op jit(solution)/shard_map/ppermute | solution.py:397
  104.6 11.2 %collective-permute-start.25 = (bf16[2,2,128,512]{3,2,1,0:T(8,128)(2,1)S(1)}, bf16[2,2,128,512]{3,2,1,0:T(8,128)(2,1)S(1)}, u32[]{:S(2)}, u32[]{:S(2)}) collective-permute-start(bf16[2,2,128,512]{3,2,1,0:T(8,128)(2,1)S(1)} %slice.64), channel_id=1, source_target_pairs={{0,1},{1,2},{2,3},{3,4},{4,5},{5,6},{6,7},{8,9},{9,10},{10,11},{11... | collective-permute-start | bytes 1572872 | tf_op jit(solution)/shard_map/ppermute | solution.py:411
  108.4 5.0 %collective-permute-start.27 = (bf16[2,128,128]{2,1,0:T(8,128)(2,1)S(1)}, bf16[2,128,128]{2,1,0:T(8,128)(2,1)S(1)}, u32[]{:S(2)}, u32[]{:S(2)}) collective-permute-start(bf16[2,128,128]{2,1,0:T(8,128)(2,1)S(1)} %get-tuple-element.107), channel_id=1, source_target_pairs={{0,2},{1,3},{2,0},{3,1},{4,6},{5,7},{6,4},{7,5},{8,10},{9,11},{10,... | collective-permute-start | bytes 196616 | tf_op jit(solution)/shard_map/ppermute | solution.py:397
  108.5 15.0 %collective-permute-start.28 = (bf16[2,128,128]{2,1,0:T(8,128)(2,1)S(1)}, bf16[2,128,128]{2,1,0:T(8,128)(2,1)S(1)}, u32[]{:S(2)}, u32[]{:S(2)}) collective-permute-start(bf16[2,128,128]{2,1,0:T(8,128)(2,1)S(1)} %get-tuple-element.108), channel_id=1, source_target_pairs={{0,3},{1,2},{2,1},{3,0},{4,7},{5,6},{6,5},{7,4},{8,11},{9,10},{10,... | collective-permute-start | bytes 196616 | tf_op jit(solution)/shard_map/ppermute | solution.py:397
  110.3 13.2 %collective-permute-start.29 = (bf16[2,128,128]{2,1,0:T(8,128)(2,1)S(1)}, bf16[2,128,128]{2,1,0:T(8,128)(2,1)S(1)}, u32[]{:S(2)}, u32[]{:S(2)}) collective-permute-start(bf16[2,128,128]{2,1,0:T(8,128)(2,1)S(1)} %get-tuple-element.109), channel_id=1, source_target_pairs={{0,4},{1,5},{2,6},{3,7},{4,0},{5,1},{6,2},{7,3},{8,12},{9,13},{10,... | collective-permute-start | bytes 196616 | tf_op jit(solution)/shard_map/ppermute | solution.py:397
  112.0 11.5 %collective-permute-start.30 = (bf16[2,128,128]{2,1,0:T(8,128)(2,1)S(1)}, bf16[2,128,128]{2,1,0:T(8,128)(2,1)S(1)}, u32[]{:S(2)}, u32[]{:S(2)}) collective-permute-start(bf16[2,128,128]{2,1,0:T(8,128)(2,1)S(1)} %get-tuple-element.110), channel_id=1, source_target_pairs={{0,5},{1,4},{2,7},{3,6},{4,1},{5,0},{6,3},{7,2},{8,13},{9,12},{10,... | collective-permute-start | bytes 196616 | tf_op jit(solution)/shard_map/ppermute | solution.py:397
  113.3 11.5 %collective-permute-start.31 = (bf16[2,128,128]{2,1,0:T(8,128)(2,1)S(1)}, bf16[2,128,128]{2,1,0:T(8,128)(2,1)S(1)}, u32[]{:S(2)}, u32[]{:S(2)}) collective-permute-start(bf16[2,128,128]{2,1,0:T(8,128)(2,1)S(1)} %get-tuple-element.111), channel_id=1, source_target_pairs={{0,6},{1,7},{2,4},{3,5},{4,2},{5,3},{6,0},{7,1},{8,14},{9,15},{10,... | collective-permute-start | bytes 196616 | tf_op jit(solution)/shard_map/ppermute | solution.py:397
  115.8 10.5 %collective-permute-start.32 = (bf16[2,128,128]{2,1,0:T(8,128)(2,1)S(1)}, bf16[2,128,128]{2,1,0:T(8,128)(2,1)S(1)}, u32[]{:S(2)}, u32[]{:S(2)}) collective-permute-start(bf16[2,128,128]{2,1,0:T(8,128)(2,1)S(1)} %get-tuple-element.112), channel_id=1, source_target_pairs={{0,7},{1,6},{2,5},{3,4},{4,3},{5,2},{6,1},{7,0},{8,15},{9,14},{10,... | collective-permute-start | bytes 196616 | tf_op jit(solution)/shard_map/ppermute | solution.py:397
  (7 other events, 75.3 us)

commit v6 on v5

--- a/solution.py
+++ b/solution.py
@@ -393,9 +393,11 @@
     core = c.astype(jnp.int32).reshape(1)
 
     def swap_blocks(replies):
-        return [replies[0]] + [
-            lax.ppermute(replies[k], ("z", "c"), [(i, i ^ k) for i in range(devices)]) for k in range(1, devices)
-        ]
+        swapped = {
+            k: lax.ppermute(replies[k], ("z", "c"), [(i, i ^ k) for i in range(devices)])
+            for k in reversed(range(1, devices))
+        }
+        return [replies[0]] + [swapped[k] for k in range(1, devices)]
 
     same, sent = project([tokens[0], c_tokens], arrays, pieces, places)
     diff = over_c(sent)

time: 134 us -> 134 us (level)
  no operation moved by 1% of the time
where the time goes in v6:
time: 134 us; the launch traced here: 132 us
  waiting for transfers between devices  63.6 us (47%)
  starting transfers between devices  34.2 us (26%)
  Pallas kernels  25.5 us (19%)
  other arithmetic  6.01 us (4%)
  local copies, waits for them, and re-layouts  2.27 us (2%)
    ppermute x16, waiting for transfers between devices, along(): lax.ppermute(value, axis, [(i, (i + step) % count) for i in range(count)])  49.7 us
    ppermute x14, starting transfers between devices, swap_blocks(): lax.ppermute(replies[k], ('z', 'c'), [(i, i ^ k) for i in range(devices)])  16 us
    ppermute x16, starting transfers between devices, along(): lax.ppermute(value, axis, [(i, (i + step) % count) for i in range(count)])  14.8 us
    ppermute x14, waiting for transfers between devices, swap_blocks(): lax.ppermute(replies[k], ('z', 'c'), [(i, i ^ k) for i in range(devices)])  12.3 us
    pallas_call x2, Pallas kernels, project(): pl.pallas_call(functools.partial(project_kernel, len(token_runs), len(arr...  11.9 us
    pallas_call x1, Pallas kernels, attend(): pl.pallas_call(functools.partial(far_kernel, len(arrived)), grid_spec=plt...  5.71 us
    pallas_call x1, Pallas kernels, attend(): pl.pallas_call(near_kernel, grid_spec=pltpu.PrefetchScalarGridSpec(num_sc...  5.26 us
  transfers between devices with their start and end apart: 33, of which 18 were waited for; matrix products, arithmetic and copies ran while one was open for 4% of the time, Pallas kernels for 14%

profile of v6, /device:TPU:16, one launch (start us, length us, event | category | flops | bytes accessed | tf_op | source)
XLA Modules:
  0.0 132.0 jit_solution(15910056727063050532)
XLA Ops:
  1.1 1.6 %collective-permute-start.2 = (bf16[128,512]{1,0:T(8,128)(2,1)S(1)}, bf16[128,512]{1,0:T(8,128)(2,1)S(1)}, u32[]{:S(2)}, u32[]{:S(2)}) collective-permute-start(bf16[128,512]{1,0:T(8,128)(2,1)S(1)} %get-tuple-element.119), channel_id=1, source_target_pairs={{0,8},{8,0},{1,9},{9,1},{2,10},{10,2},{3,11},{11,3},{4,12},{12,4},... | collective-permute-start | bytes 393224 | tf_op jit(solution)/shard_map/ppermute | solution.py:333
  3.7 3.5 %collective-permute-done.2 = bf16[128,512]{1,0:T(8,128)(2,1)S(1)} collective-permute-done((bf16[128,512]{1,0:T(8,128)(2,1)S(1)}, bf16[128,512]{1,0:T(8,128)(2,1)S(1)}, u32[]{:S(2)}, u32[]{:S(2)}) %collective-permute-start.2) | collective-permute-done | bytes 131104 | tf_op jit(solution)/shard_map/ppermute | solution.py:333
  10.2 1.6 %collective-permute-start.4 = (bf16[528,512]{1,0:T(8,128)(2,1)S(1)}, bf16[528,512]{1,0:T(8,128)(2,1)S(1)}, u32[]{:S(2)}, u32[]{:S(2)}) collective-permute-start(bf16[528,512]{1,0:T(8,128)(2,1)S(1)} %maximum_maximum_fusion.refs_2_), channel_id=1, source_target_pairs={{0,2},{2,4},{4,6},{6,0},{1,3},{3,5},{5,7},{7,1},{8,10},{10,12},{12... | collective-permute-start | bytes 1622024 | tf_op jit(solution)/shard_map/ppermute | solution.py:333
  11.8 1.5 %collective-permute-start.5 = (bf16[528,512]{1,0:T(8,128)(2,1)S(1)}, bf16[528,512]{1,0:T(8,128)(2,1)S(1)}, u32[]{:S(2)}, u32[]{:S(2)}) collective-permute-start(bf16[528,512]{1,0:T(8,128)(2,1)S(1)} %maximum_maximum_fusion.refs_2_), channel_id=1, source_target_pairs={{0,16},{16,0},{1,17},{17,1},{2,18},{18,2},{3,19},{19,3},{4,20},{20... | collective-permute-start | bytes 1622024 | tf_op jit(solution)/shard_map/ppermute | solution.py:333
  13.3 11.8 %collective-permute-done.4.refs_4_ = bf16[528,512]{1,0:T(8,128)(2,1)S(1)} collective-permute-done((bf16[528,512]{1,0:T(8,128)(2,1)S(1)}, bf16[528,512]{1,0:T(8,128)(2,1)S(1)}, u32[]{:S(2)}, u32[]{:S(2)}) %collective-permute-start.4) | collective-permute-done | bytes 540704 | tf_op jit(solution)/shard_map/ppermute | solution.py:333
  25.1 1.3 collective-permute-done.5.refs_3_
  26.9 1.5 %collective-permute-start.7 = (bf16[528,512]{1,0:T(8,128)(2,1)S(1)}, bf16[528,512]{1,0:T(8,128)(2,1)S(1)}, u32[]{:S(2)}, u32[]{:S(2)}) collective-permute-start(bf16[528,512]{1,0:T(8,128)(2,1)S(1)} %collective-permute-done.4.refs_4_), channel_id=1, source_target_pairs={{0,16},{16,0},{1,17},{17,1},{2,18},{18,2},{3,19},{19,3},{4,20},{20... | collective-permute-start | bytes 1622024 | tf_op jit(solution)/shard_map/ppermute | solution.py:333
  28.4 11.9 %collective-permute-done.6.refs_6_ = bf16[528,512]{1,0:T(8,128)(2,1)S(1)} collective-permute-done((bf16[528,512]{1,0:T(8,128)(2,1)S(1)}, bf16[528,512]{1,0:T(8,128)(2,1)S(1)}, u32[]{:S(2)}, u32[]{:S(2)}) %collective-permute-start.6) | collective-permute-done | bytes 540704 | tf_op jit(solution)/shard_map/ppermute | solution.py:333
  40.5 1.5 %collective-permute-start.9 = (bf16[528,512]{1,0:T(8,128)(2,1)S(1)}, bf16[528,512]{1,0:T(8,128)(2,1)S(1)}, u32[]{:S(2)}, u32[]{:S(2)}) collective-permute-start(bf16[528,512]{1,0:T(8,128)(2,1)S(1)} %collective-permute-done.6.refs_6_), channel_id=1, source_target_pairs={{0,16},{16,0},{1,17},{17,1},{2,18},{18,2},{3,19},{19,3},{4,20},{20... | collective-permute-start | bytes 1622024 | tf_op jit(solution)/shard_map/ppermute | solution.py:333
  42.1 2.1 %collective-permute-start.8 = (bf16[256,512]{1,0:T(8,128)(2,1)S(1)}, bf16[256,512]{1,0:T(8,128)(2,1)}, u32[]{:S(2)}, u32[]{:S(2)}) collective-permute-start(bf16[256,512]{1,0:T(8,128)(2,1)S(1)} %slice.52), channel_id=1, source_target_pairs={{0,2},{2,4},{4,6},{6,0},{1,3},{3,5},{5,7},{7,1},{8,10},{10,12},{12... | collective-permute-start | bytes 786440 | tf_op jit(solution)/shard_map/ppermute | solution.py:333
  44.4 12.4 %collective-permute-done.11.refs_10_ = bf16[272,512]{1,0:T(8,128)(2,1)S(1)} collective-permute-done((bf16[272,512]{1,0:T(8,128)(2,1)S(1)}, bf16[272,512]{1,0:T(8,128)(2,1)S(1)}, u32[]{:S(2)}, u32[]{:S(2)}) %collective-permute-start.11) | collective-permute-done | bytes 278560 | tf_op jit(solution)/shard_map/ppermute | solution.py:333
  57.2 1.5 %collective-permute-start.12 = (bf16[256,512]{1,0:T(8,128)(2,1)}, bf16[256,512]{1,0:T(8,128)(2,1)}, u32[]{:S(2)}, u32[]{:S(2)}) collective-permute-start(bf16[256,512]{1,0:T(8,128)(2,1)} %collective-permute-done.8.refs_8_), channel_id=1, source_target_pairs={{0,16},{16,0},{1,17},{17,1},{2,18},{18,2},{3,19},{19,3},{4,20},{20... | collective-permute-start | bytes 786440 | tf_op jit(solution)/shard_map/ppermute | solution.py:333
  60.2 5.9 %collective-permute-done.13.refs_11_ = bf16[272,512]{1,0:T(8,128)(2,1)} collective-permute-done((bf16[272,512]{1,0:T(8,128)(2,1)S(1)}, bf16[272,512]{1,0:T(8,128)(2,1)}, u32[]{:S(2)}, u32[]{:S(2)}) %collective-permute-start.13) | collective-permute-done | bytes 278560 | tf_op jit(solution)/shard_map/ppermute | solution.py:333
  66.0 2.8 %collective-permute-done.12.refs_9_ = bf16[256,512]{1,0:T(8,128)(2,1)} collective-permute-done((bf16[256,512]{1,0:T(8,128)(2,1)}, bf16[256,512]{1,0:T(8,128)(2,1)}, u32[]{:S(2)}, u32[]{:S(2)}) %collective-permute-start.12) | collective-permute-done | bytes 262176 | tf_op jit(solution)/shard_map/ppermute | solution.py:333
  68.9 6.0 %shard_map.64 = (bf16[256,512]{1,0:T(8,128)(2,1)S(1)}, bf16[256,512]{1,0:T(8,128)(2,1)}) custom-call(s32[16]{0:T(128)S(1)} %stack.148.place_ref, bf16[256,4096]{1,0:T(8,128)(2,1)} %bitcast.21.refs_0_, bf16[256,4096]{1,0:T(8,128)(2,1)} %collective-permute-done.refs_1_, bf16[528,512]{1,0:T(8,128)(2,1)S(1)} %maximum_maximum_fusion.refs_2_, ...), custom_call_target="tpu_custom_call" | custom-call | flops 2147483648 | bytes 8388608 | tf_op jit(solution)/shard_map/pallas_call | solution.py:261
  77.9 6.0 %shard_map.65 = (bf16[256,512]{1,0:T(8,128)(2,1)}, bf16[256,512]{1,0:T(8,128)(2,1)}) custom-call(s32[16]{0:T(128)S(1)} %stack.148.place_ref, bf16[256,4096]{1,0:T(8,128)(2,1)} %collective-permute-done.10.refs_0_, bf16[256,4096]{1,0:T(8,128)(2,1)} %collective-permute-done.15.refs_1_, bf16[528,512]{1,0:T(8,128)(2,1)S(1)} %maximum_maximum_fusion.refs_2_, ...), custom_call_target="tpu_custom_call" | custom-call | flops 2147483648 | bytes 8388608 | tf_op jit(solution)/shard_map/pallas_call | solution.py:261
  83.9 1.8 %shard_map.66 = (bf16[2,128,128]{2,1,0:T(8,128)(2,1)S(1)}, bf16[2,128,128]{2,1,0:T(8,128)(2,1)S(1)}, bf16[2,128,128]{2,1,0:T(8,128)(2,1)S(1)}, bf16[2,128,128]{2...) custom-call(s32[16]{0:T(128)S(1)} %select_n.204.row_ref, ...), custom_call_target="tpu_custom_call" | custom-call | tf_op jit(solution)/shard_map/pallas_call | solution.py:301
  86.3 1.6 %collective-permute-start.20 = (bf16[2,128,128]{2,1,0:T(8,128)(2,1)S(1)}, bf16[2,128,128]{2,1,0:T(8,128)(2,1)S(1)}, u32[]{:S(2)}, u32[]{:S(2)}) collective-permute-start(bf16[2,128,128]{2,1,0:T(8,128)(2,1)S(1)} %get-tuple-element.88), channel_id=1, source_target_pairs={{0,3},{1,2},{2,1},{3,0},{4,7},{5,6},{6,5},{7,4},{8,11},{9,10},{10,... | collective-permute-start | bytes 196616 | tf_op jit(solution)/shard_map/ppermute | solution.py:397
  87.9 1.7 %collective-permute-start.21 = (bf16[2,128,128]{2,1,0:T(8,128)(2,1)S(1)}, bf16[2,128,128]{2,1,0:T(8,128)(2,1)S(1)}, u32[]{:S(2)}, u32[]{:S(2)}) collective-permute-start(bf16[2,128,128]{2,1,0:T(8,128)(2,1)S(1)} %get-tuple-element.89), channel_id=1, source_target_pairs={{0,4},{1,5},{2,6},{3,7},{4,0},{5,1},{6,2},{7,3},{8,12},{9,13},{10,... | collective-permute-start | bytes 196616 | tf_op jit(solution)/shard_map/ppermute | solution.py:397
  91.0 1.3 %collective-permute-start.22 = (bf16[2,128,128]{2,1,0:T(8,128)(2,1)S(1)}, bf16[2,128,128]{2,1,0:T(8,128)(2,1)S(1)}, u32[]{:S(2)}, u32[]{:S(2)}) collective-permute-start(bf16[2,128,128]{2,1,0:T(8,128)(2,1)S(1)} %get-tuple-element.90), channel_id=1, source_target_pairs={{0,5},{1,4},{2,7},{3,6},{4,1},{5,0},{6,3},{7,2},{8,13},{9,12},{10,... | collective-permute-start | bytes 196616 | tf_op jit(solution)/shard_map/ppermute | solution.py:397
  92.3 1.9 %collective-permute-start.23 = (bf16[2,128,128]{2,1,0:T(8,128)(2,1)S(1)}, bf16[2,128,128]{2,1,0:T(8,128)(2,1)S(1)}, u32[]{:S(2)}, u32[]{:S(2)}) collective-permute-start(bf16[2,128,128]{2,1,0:T(8,128)(2,1)S(1)} %get-tuple-element.91), channel_id=1, source_target_pairs={{0,6},{1,7},{2,4},{3,5},{4,2},{5,3},{6,0},{7,1},{8,14},{9,15},{10,... | collective-permute-start | bytes 196616 | tf_op jit(solution)/shard_map/ppermute | solution.py:397
  94.7 1.4 %collective-permute-done.22.refs_5_ = bf16[2,128,128]{2,1,0:T(8,128)(2,1)S(1)} collective-permute-done((bf16[2,128,128]{2,1,0:T(8,128)(2,1)S(1)}, bf16[2,128,128]{2,1,0:T(8,128)(2,1)S(1)}, u32[]{:S(2)}, u32[]{:S(2)}) %collective-permute-start.22) | collective-permute-done | bytes 65568 | tf_op jit(solution)/shard_map/ppermute | solution.py:397
  96.1 5.9 %collective-permute-done.23.refs_6_ = bf16[2,128,128]{2,1,0:T(8,128)(2,1)S(1)} collective-permute-done((bf16[2,128,128]{2,1,0:T(8,128)(2,1)S(1)}, bf16[2,128,128]{2,1,0:T(8,128)(2,1)S(1)}, u32[]{:S(2)}, u32[]{:S(2)}) %collective-permute-start.23) | collective-permute-done | bytes 65568 | tf_op jit(solution)/shard_map/ppermute | solution.py:397
  103.2 1.3 pad_maximum_fusion
  104.6 2.2 %collective-permute-start.25 = (bf16[2,2,128,512]{3,2,1,0:T(8,128)(2,1)S(1)}, bf16[2,2,128,512]{3,2,1,0:T(8,128)(2,1)S(1)}, u32[]{:S(2)}, u32[]{:S(2)}) collective-permute-start(bf16[2,2,128,512]{3,2,1,0:T(8,128)(2,1)S(1)} %slice.64), channel_id=1, source_target_pairs={{0,1},{1,2},{2,3},{3,4},{4,5},{5,6},{6,7},{8,9},{9,10},{10,11},{11... | collective-permute-start | bytes 1572872 | tf_op jit(solution)/shard_map/ppermute | solution.py:413
  108.5 1.8 %collective-permute-start.28 = (bf16[2,128,128]{2,1,0:T(8,128)(2,1)S(1)}, bf16[2,128,128]{2,1,0:T(8,128)(2,1)S(1)}, u32[]{:S(2)}, u32[]{:S(2)}) collective-permute-start(bf16[2,128,128]{2,1,0:T(8,128)(2,1)S(1)} %get-tuple-element.108), channel_id=1, source_target_pairs={{0,3},{1,2},{2,1},{3,0},{4,7},{5,6},{6,5},{7,4},{8,11},{9,10},{10,... | collective-permute-start | bytes 196616 | tf_op jit(solution)/shard_map/ppermute | solution.py:397
  110.3 1.7 %collective-permute-start.29 = (bf16[2,128,128]{2,1,0:T(8,128)(2,1)S(1)}, bf16[2,128,128]{2,1,0:T(8,128)(2,1)S(1)}, u32[]{:S(2)}, u32[]{:S(2)}) collective-permute-start(bf16[2,128,128]{2,1,0:T(8,128)(2,1)S(1)} %get-tuple-element.109), channel_id=1, source_target_pairs={{0,4},{1,5},{2,6},{3,7},{4,0},{5,1},{6,2},{7,3},{8,12},{9,13},{10,... | collective-permute-start | bytes 196616 | tf_op jit(solution)/shard_map/ppermute | solution.py:397
  113.3 2.1 %collective-permute-start.31 = (bf16[2,128,128]{2,1,0:T(8,128)(2,1)S(1)}, bf16[2,128,128]{2,1,0:T(8,128)(2,1)S(1)}, u32[]{:S(2)}, u32[]{:S(2)}) collective-permute-start(bf16[2,128,128]{2,1,0:T(8,128)(2,1)S(1)} %get-tuple-element.111), channel_id=1, source_target_pairs={{0,6},{1,7},{2,4},{3,5},{4,2},{5,3},{6,0},{7,1},{8,14},{9,15},{10,... | collective-permute-start | bytes 196616 | tf_op jit(solution)/shard_map/ppermute | solution.py:397
  115.8 2.4 %collective-permute-start.32 = (bf16[2,128,128]{2,1,0:T(8,128)(2,1)S(1)}, bf16[2,128,128]{2,1,0:T(8,128)(2,1)S(1)}, u32[]{:S(2)}, u32[]{:S(2)}) collective-permute-start(bf16[2,128,128]{2,1,0:T(8,128)(2,1)S(1)} %get-tuple-element.112), channel_id=1, source_target_pairs={{0,7},{1,6},{2,5},{3,4},{4,3},{5,2},{6,1},{7,0},{8,15},{9,14},{10,... | collective-permute-start | bytes 196616 | tf_op jit(solution)/shard_map/ppermute | solution.py:397
  118.2 5.3 %shard_map.67 = (f32[256,4096]{1,0:T(8,128)S(1)}, bf16[256,256]{1,0:T(8,128)(2,1)S(1)}) custom-call(s32[4]{0:T(128)S(1)} %pad_add_fusion.where_ref, bf16[256,4096]{1,0:T(8,128)(2,1)S(1)} %bitcast.56, bf16[2,2,256,512]{3,2,1,0:T(8,128)(2,1)S(1)} %bitcast.54, bf16[2,2,256,512]{3,2,1,0:T(8,128)(2,1)S(1)} %bitcast.55, ...), custom_call_target="tpu_custom_call" | custom-call | flops 1073741824 | bytes 8388608 | tf_op jit(solution)/shard_map/pallas_call | solution.py:151
  124.8 1.5 %collective-permute-done.32.refs_15_ = bf16[2,128,128]{2,1,0:T(8,128)(2,1)S(1)} collective-permute-done((bf16[2,128,128]{2,1,0:T(8,128)(2,1)S(1)}, bf16[2,128,128]{2,1,0:T(8,128)(2,1)S(1)}, u32[]{:S(2)}, u32[]{:S(2)}) %collective-permute-start.32) | collective-permute-done | bytes 65568 | tf_op jit(solution)/shard_map/ppermute | solution.py:397
  126.3 5.7 %shard_map.69 = bf16[256,4096]{1,0:T(8,128)(2,1)} custom-call(s32[16]{0:T(128)S(1)} %add_xor_fusion.place_ref, s32[4]{0:T(128)S(1)} %pad_add_fusion.where_ref, bf16[256,4096]{1,0:T(8,128)(2,1)S(1)} %bitcast.57, f32[256,4096]{1,0:T(8,128)S(1)} %get-tuple-element.95.near_ref, bf16[256,256]{1,0:T(8,128)(2,1)S(1)} %get-tuple-element.96.log_ref, ...), custom_call_target="tpu_custom_call" | custom-call | flops 536870912 | bytes 8388608 | tf_op jit(solution)/shard_map/pallas_call | solution.py:181
  (107 shorter events, 19.3 us)
Async XLA Ops:
  1.1 6.1 %collective-permute-start.2 = (bf16[128,512]{1,0:T(8,128)(2,1)S(1)}, bf16[128,512]{1,0:T(8,128)(2,1)S(1)}, u32[]{:S(2)}, u32[]{:S(2)}) collective-permute-start(bf16[128,512]{1,0:T(8,128)(2,1)S(1)} %get-tuple-element.119), channel_id=1, source_target_pairs={{0,8},{8,0},{1,9},{9,1},{2,10},{10,2},{3,11},{11,3},{4,12},{12,4},... | collective-permute-start | bytes 393224 | tf_op jit(solution)/shard_map/ppermute | solution.py:333
  2.7 5.8 %collective-permute-start.3 = (bf16[128,512]{1,0:T(8,128)(2,1)S(1)}, bf16[128,512]{1,0:T(8,128)(2,1)S(1)}, u32[]{:S(2)}, u32[]{:S(2)}) collective-permute-start(bf16[128,512]{1,0:T(8,128)(2,1)S(1)} %get-tuple-element.120), channel_id=1, source_target_pairs={{0,9},{1,8},{8,1},{9,0},{2,11},{3,10},{10,3},{11,2},{4,13},{5,12},... | collective-permute-start | bytes 393224 | tf_op jit(solution)/shard_map/ppermute | solution.py:338
  2.9 5.6 %collective-permute-start.1 = (bf16[144,512]{1,0:T(8,128)(2,1)S(1)}, bf16[144,512]{1,0:T(8,128)(2,1)S(1)}, u32[]{:S(2)}, u32[]{:S(2)}) collective-permute-start(bf16[144,512]{1,0:T(8,128)(2,1)S(1)} %pad_maximum_fusion.3), channel_id=1, source_target_pairs={{0,1},{1,0},{2,3},{3,2},{4,5},{5,4},{6,7},{7,6},{8,9},{9,8},{10,11... | collective-permute-start | bytes 442376 | tf_op jit(solution)/shard_map/ppermute | solution.py:333
  9.0 59.8 %collective-permute-start.10 = (bf16[256,4096]{1,0:T(8,128)(2,1)}, bf16[256,4096]{1,0:T(8,128)(2,1)}, u32[]{:S(2)}, u32[]{:S(2)}) collective-permute-start(bf16[256,4096]{1,0:T(8,128)(2,1)} %bitcast.21.refs_0_), channel_id=1, source_target_pairs={{0,8},{8,0},{1,9},{9,1},{2,10},{10,2},{3,11},{11,3},{4,12},{12,4},... | collective-permute-start | bytes 6291464 | tf_op jit(solution)/shard_map/ppermute | solution.py:333
  10.2 14.9 %collective-permute-start.4 = (bf16[528,512]{1,0:T(8,128)(2,1)S(1)}, bf16[528,512]{1,0:T(8,128)(2,1)S(1)}, u32[]{:S(2)}, u32[]{:S(2)}) collective-permute-start(bf16[528,512]{1,0:T(8,128)(2,1)S(1)} %maximum_maximum_fusion.refs_2_), channel_id=1, source_target_pairs={{0,2},{2,4},{4,6},{6,0},{1,3},{3,5},{5,7},{7,1},{8,10},{10,12},{12... | collective-permute-start | bytes 1622024 | tf_op jit(solution)/shard_map/ppermute | solution.py:333
  11.8 14.6 %collective-permute-start.5 = (bf16[528,512]{1,0:T(8,128)(2,1)S(1)}, bf16[528,512]{1,0:T(8,128)(2,1)S(1)}, u32[]{:S(2)}, u32[]{:S(2)}) collective-permute-start(bf16[528,512]{1,0:T(8,128)(2,1)S(1)} %maximum_maximum_fusion.refs_2_), channel_id=1, source_target_pairs={{0,16},{16,0},{1,17},{17,1},{2,18},{18,2},{3,19},{19,3},{4,20},{20... | collective-permute-start | bytes 1622024 | tf_op jit(solution)/shard_map/ppermute | solution.py:333
  26.4 13.9 %collective-permute-start.6 = (bf16[528,512]{1,0:T(8,128)(2,1)S(1)}, bf16[528,512]{1,0:T(8,128)(2,1)S(1)}, u32[]{:S(2)}, u32[]{:S(2)}) collective-permute-start(bf16[528,512]{1,0:T(8,128)(2,1)S(1)} %maximum_maximum_fusion.refs_2_), channel_id=1, source_target_pairs={{0,6},{2,0},{4,2},{6,4},{1,7},{3,1},{5,3},{7,5},{8,14},{10,8},{12,... | collective-permute-start | bytes 1622024 | tf_op jit(solution)/shard_map/ppermute | solution.py:333
  26.9 13.6 %collective-permute-start.7 = (bf16[528,512]{1,0:T(8,128)(2,1)S(1)}, bf16[528,512]{1,0:T(8,128)(2,1)S(1)}, u32[]{:S(2)}, u32[]{:S(2)}) collective-permute-start(bf16[528,512]{1,0:T(8,128)(2,1)S(1)} %collective-permute-done.4.refs_4_), channel_id=1, source_target_pairs={{0,16},{16,0},{1,17},{17,1},{2,18},{18,2},{3,19},{19,3},{4,20},{20... | collective-permute-start | bytes 1622024 | tf_op jit(solution)/shard_map/ppermute | solution.py:333
  28.4 40.5 %collective-permute-start = (bf16[256,4096]{1,0:T(8,128)(2,1)}, bf16[256,4096]{1,0:T(8,128)(2,1)}, u32[]{:S(2)}, u32[]{:S(2)}) collective-permute-start(bf16[256,4096]{1,0:T(8,128)(2,1)} %bitcast.21.refs_0_), channel_id=1, source_target_pairs={{0,1},{1,0},{2,3},{3,2},{4,5},{5,4},{6,7},{7,6},{8,9},{9,8},{10,11... | collective-permute-start | bytes 6291464 | tf_op jit(solution)/shard_map/ppermute | solution.py:333
  40.5 16.8 %collective-permute-start.9 = (bf16[528,512]{1,0:T(8,128)(2,1)S(1)}, bf16[528,512]{1,0:T(8,128)(2,1)S(1)}, u32[]{:S(2)}, u32[]{:S(2)}) collective-permute-start(bf16[528,512]{1,0:T(8,128)(2,1)S(1)} %collective-permute-done.6.refs_6_), channel_id=1, source_target_pairs={{0,16},{16,0},{1,17},{17,1},{2,18},{18,2},{3,19},{19,3},{4,20},{20... | collective-permute-start | bytes 1622024 | tf_op jit(solution)/shard_map/ppermute | solution.py:333
  42.1 15.2 %collective-permute-start.8 = (bf16[256,512]{1,0:T(8,128)(2,1)S(1)}, bf16[256,512]{1,0:T(8,128)(2,1)}, u32[]{:S(2)}, u32[]{:S(2)}) collective-permute-start(bf16[256,512]{1,0:T(8,128)(2,1)S(1)} %slice.52), channel_id=1, source_target_pairs={{0,2},{2,4},{4,6},{6,0},{1,3},{3,5},{5,7},{7,1},{8,10},{10,12},{12... | collective-permute-start | bytes 786440 | tf_op jit(solution)/shard_map/ppermute | solution.py:333
  44.2 12.5 %collective-permute-start.11 = (bf16[272,512]{1,0:T(8,128)(2,1)S(1)}, bf16[272,512]{1,0:T(8,128)(2,1)S(1)}, u32[]{:S(2)}, u32[]{:S(2)}) collective-permute-start(bf16[272,512]{1,0:T(8,128)(2,1)S(1)} %slice.53), channel_id=1, source_target_pairs={{0,6},{2,0},{4,2},{6,4},{1,7},{3,1},{5,3},{7,5},{8,14},{10,8},{12,... | collective-permute-start | bytes 835592 | tf_op jit(solution)/shard_map/ppermute | solution.py:333
  56.7 9.3 %collective-permute-start.13 = (bf16[272,512]{1,0:T(8,128)(2,1)S(1)}, bf16[272,512]{1,0:T(8,128)(2,1)}, u32[]{:S(2)}, u32[]{:S(2)}) collective-permute-start(bf16[272,512]{1,0:T(8,128)(2,1)S(1)} %collective-permute-done.11.refs_10_), channel_id=1, source_target_pairs={{0,16},{16,0},{1,17},{17,1},{2,18},{18,2},{3,19},{19,3},{4,20},{20... | collective-permute-start | bytes 835592 | tf_op jit(solution)/shard_map/ppermute | solution.py:333
  57.2 11.6 %collective-permute-start.12 = (bf16[256,512]{1,0:T(8,128)(2,1)}, bf16[256,512]{1,0:T(8,128)(2,1)}, u32[]{:S(2)}, u32[]{:S(2)}) collective-permute-start(bf16[256,512]{1,0:T(8,128)(2,1)} %collective-permute-done.8.refs_8_), channel_id=1, source_target_pairs={{0,16},{16,0},{1,17},{17,1},{2,18},{18,2},{3,19},{19,3},{4,20},{20... | collective-permute-start | bytes 786440 | tf_op jit(solution)/shard_map/ppermute | solution.py:333
  68.8 9.1 %collective-permute-start.15 = (bf16[256,4096]{1,0:T(8,128)(2,1)}, bf16[256,4096]{1,0:T(8,128)(2,1)}, u32[]{:S(2)}, u32[]{:S(2)}) collective-permute-start(bf16[256,4096]{1,0:T(8,128)(2,1)} %collective-permute-done.10.refs_0_), channel_id=1, source_target_pairs={{0,1},{1,0},{2,3},{3,2},{4,5},{5,4},{6,7},{7,6},{8,9},{9,8},{10,11... | collective-permute-start | bytes 6291464 | tf_op jit(solution)/shard_map/ppermute | solution.py:333
  75.6 8.3 %collective-permute-start.14 = (bf16[256,512]{1,0:T(8,128)(2,1)}, bf16[256,512]{1,0:T(8,128)(2,1)}, u32[]{:S(2)}, u32[]{:S(2)}) collective-permute-start(bf16[256,512]{1,0:T(8,128)(2,1)} %get-tuple-element.78), channel_id=1, source_target_pairs={{0,1},{1,0},{2,3},{3,2},{4,5},{5,4},{6,7},{7,6},{8,9},{9,8},{10,11... | collective-permute-start | bytes 786440 | tf_op jit(solution)/shard_map/ppermute | solution.py:333
  85.7 3.9 %collective-permute-start.18 = (bf16[2,128,128]{2,1,0:T(8,128)(2,1)S(1)}, bf16[2,128,128]{2,1,0:T(8,128)(2,1)S(1)}, u32[]{:S(2)}, u32[]{:S(2)}) collective-permute-start(bf16[2,128,128]{2,1,0:T(8,128)(2,1)S(1)} %get-tuple-element.86), channel_id=1, source_target_pairs={{0,1},{1,0},{2,3},{3,2},{4,5},{5,4},{6,7},{7,6},{8,9},{9,8},{10,11... | collective-permute-start | bytes 196616 | tf_op jit(solution)/shard_map/ppermute | solution.py:397
  86.0 17.3 %collective-permute-start.16 = (bf16[256,512]{1,0:T(8,128)(2,1)}, bf16[256,512]{1,0:T(8,128)(2,1)S(1)}, u32[]{:S(2)}, u32[]{:S(2)}) collective-permute-start(bf16[256,512]{1,0:T(8,128)(2,1)} %get-tuple-element.81), channel_id=1, source_target_pairs={{0,8},{8,0},{1,9},{9,1},{2,10},{10,2},{3,11},{11,3},{4,12},{12,4},... | collective-permute-start | bytes 786440 | tf_op jit(solution)/shard_map/ppermute | solution.py:333
  86.0 5.0 %collective-permute-start.19 = (bf16[2,128,128]{2,1,0:T(8,128)(2,1)S(1)}, bf16[2,128,128]{2,1,0:T(8,128)(2,1)S(1)}, u32[]{:S(2)}, u32[]{:S(2)}) collective-permute-start(bf16[2,128,128]{2,1,0:T(8,128)(2,1)S(1)} %get-tuple-element.87), channel_id=1, source_target_pairs={{0,2},{1,3},{2,0},{3,1},{4,6},{5,7},{6,4},{7,5},{8,10},{9,11},{10,... | collective-permute-start | bytes 196616 | tf_op jit(solution)/shard_map/ppermute | solution.py:397
  86.3 6.0 %collective-permute-start.20 = (bf16[2,128,128]{2,1,0:T(8,128)(2,1)S(1)}, bf16[2,128,128]{2,1,0:T(8,128)(2,1)S(1)}, u32[]{:S(2)}, u32[]{:S(2)}) collective-permute-start(bf16[2,128,128]{2,1,0:T(8,128)(2,1)S(1)} %get-tuple-element.88), channel_id=1, source_target_pairs={{0,3},{1,2},{2,1},{3,0},{4,7},{5,6},{6,5},{7,4},{8,11},{9,10},{10,... | collective-permute-start | bytes 196616 | tf_op jit(solution)/shard_map/ppermute | solution.py:397
  87.9 6.8 %collective-permute-start.21 = (bf16[2,128,128]{2,1,0:T(8,128)(2,1)S(1)}, bf16[2,128,128]{2,1,0:T(8,128)(2,1)S(1)}, u32[]{:S(2)}, u32[]{:S(2)}) collective-permute-start(bf16[2,128,128]{2,1,0:T(8,128)(2,1)S(1)} %get-tuple-element.89), channel_id=1, source_target_pairs={{0,4},{1,5},{2,6},{3,7},{4,0},{5,1},{6,2},{7,3},{8,12},{9,13},{10,... | collective-permute-start | bytes 196616 | tf_op jit(solution)/shard_map/ppermute | solution.py:397
  89.6 13.6 %collective-permute-start.17 = (bf16[256,512]{1,0:T(8,128)(2,1)}, bf16[256,512]{1,0:T(8,128)(2,1)S(1)}, u32[]{:S(2)}, u32[]{:S(2)}) collective-permute-start(bf16[256,512]{1,0:T(8,128)(2,1)} %get-tuple-element.84), channel_id=1, source_target_pairs={{0,9},{1,8},{8,1},{9,0},{2,11},{3,10},{10,3},{11,2},{4,13},{5,12},... | collective-permute-start | bytes 786440 | tf_op jit(solution)/shard_map/ppermute | solution.py:338
  91.0 5.1 %collective-permute-start.22 = (bf16[2,128,128]{2,1,0:T(8,128)(2,1)S(1)}, bf16[2,128,128]{2,1,0:T(8,128)(2,1)S(1)}, u32[]{:S(2)}, u32[]{:S(2)}) collective-permute-start(bf16[2,128,128]{2,1,0:T(8,128)(2,1)S(1)} %get-tuple-element.90), channel_id=1, source_target_pairs={{0,5},{1,4},{2,7},{3,6},{4,1},{5,0},{6,3},{7,2},{8,13},{9,12},{10,... | collective-permute-start | bytes 196616 | tf_op jit(solution)/shard_map/ppermute | solution.py:397
  92.3 9.7 %collective-permute-start.23 = (bf16[2,128,128]{2,1,0:T(8,128)(2,1)S(1)}, bf16[2,128,128]{2,1,0:T(8,128)(2,1)S(1)}, u32[]{:S(2)}, u32[]{:S(2)}) collective-permute-start(bf16[2,128,128]{2,1,0:T(8,128)(2,1)S(1)} %get-tuple-element.91), channel_id=1, source_target_pairs={{0,6},{1,7},{2,4},{3,5},{4,2},{5,3},{6,0},{7,1},{8,14},{9,15},{10,... | collective-permute-start | bytes 196616 | tf_op jit(solution)/shard_map/ppermute | solution.py:397
  94.7 8.5 %collective-permute-start.24 = (bf16[2,128,128]{2,1,0:T(8,128)(2,1)S(1)}, bf16[2,128,128]{2,1,0:T(8,128)(2,1)S(1)}, u32[]{:S(2)}, u32[]{:S(2)}) collective-permute-start(bf16[2,128,128]{2,1,0:T(8,128)(2,1)S(1)} %get-tuple-element.92), channel_id=1, source_target_pairs={{0,7},{1,6},{2,5},{3,4},{4,3},{5,2},{6,1},{7,0},{8,15},{9,14},{10,... | collective-permute-start | bytes 196616 | tf_op jit(solution)/shard_map/ppermute | solution.py:397
  104.6 11.2 %collective-permute-start.25 = (bf16[2,2,128,512]{3,2,1,0:T(8,128)(2,1)S(1)}, bf16[2,2,128,512]{3,2,1,0:T(8,128)(2,1)S(1)}, u32[]{:S(2)}, u32[]{:S(2)}) collective-permute-start(bf16[2,2,128,512]{3,2,1,0:T(8,128)(2,1)S(1)} %slice.64), channel_id=1, source_target_pairs={{0,1},{1,2},{2,3},{3,4},{4,5},{5,6},{6,7},{8,9},{9,10},{10,11},{11... | collective-permute-start | bytes 1572872 | tf_op jit(solution)/shard_map/ppermute | solution.py:413
  108.4 5.0 %collective-permute-start.27 = (bf16[2,128,128]{2,1,0:T(8,128)(2,1)S(1)}, bf16[2,128,128]{2,1,0:T(8,128)(2,1)S(1)}, u32[]{:S(2)}, u32[]{:S(2)}) collective-permute-start(bf16[2,128,128]{2,1,0:T(8,128)(2,1)S(1)} %get-tuple-element.107), channel_id=1, source_target_pairs={{0,2},{1,3},{2,0},{3,1},{4,6},{5,7},{6,4},{7,5},{8,10},{9,11},{10,... | collective-permute-start | bytes 196616 | tf_op jit(solution)/shard_map/ppermute | solution.py:397
  108.5 15.0 %collective-permute-start.28 = (bf16[2,128,128]{2,1,0:T(8,128)(2,1)S(1)}, bf16[2,128,128]{2,1,0:T(8,128)(2,1)S(1)}, u32[]{:S(2)}, u32[]{:S(2)}) collective-permute-start(bf16[2,128,128]{2,1,0:T(8,128)(2,1)S(1)} %get-tuple-element.108), channel_id=1, source_target_pairs={{0,3},{1,2},{2,1},{3,0},{4,7},{5,6},{6,5},{7,4},{8,11},{9,10},{10,... | collective-permute-start | bytes 196616 | tf_op jit(solution)/shard_map/ppermute | solution.py:397
  110.3 13.2 %collective-permute-start.29 = (bf16[2,128,128]{2,1,0:T(8,128)(2,1)S(1)}, bf16[2,128,128]{2,1,0:T(8,128)(2,1)S(1)}, u32[]{:S(2)}, u32[]{:S(2)}) collective-permute-start(bf16[2,128,128]{2,1,0:T(8,128)(2,1)S(1)} %get-tuple-element.109), channel_id=1, source_target_pairs={{0,4},{1,5},{2,6},{3,7},{4,0},{5,1},{6,2},{7,3},{8,12},{9,13},{10,... | collective-permute-start | bytes 196616 | tf_op jit(solution)/shard_map/ppermute | solution.py:397
  112.0 11.5 %collective-permute-start.30 = (bf16[2,128,128]{2,1,0:T(8,128)(2,1)S(1)}, bf16[2,128,128]{2,1,0:T(8,128)(2,1)S(1)}, u32[]{:S(2)}, u32[]{:S(2)}) collective-permute-start(bf16[2,128,128]{2,1,0:T(8,128)(2,1)S(1)} %get-tuple-element.110), channel_id=1, source_target_pairs={{0,5},{1,4},{2,7},{3,6},{4,1},{5,0},{6,3},{7,2},{8,13},{9,12},{10,... | collective-permute-start | bytes 196616 | tf_op jit(solution)/shard_map/ppermute | solution.py:397
  113.3 11.5 %collective-permute-start.31 = (bf16[2,128,128]{2,1,0:T(8,128)(2,1)S(1)}, bf16[2,128,128]{2,1,0:T(8,128)(2,1)S(1)}, u32[]{:S(2)}, u32[]{:S(2)}) collective-permute-start(bf16[2,128,128]{2,1,0:T(8,128)(2,1)S(1)} %get-tuple-element.111), channel_id=1, source_target_pairs={{0,6},{1,7},{2,4},{3,5},{4,2},{5,3},{6,0},{7,1},{8,14},{9,15},{10,... | collective-permute-start | bytes 196616 | tf_op jit(solution)/shard_map/ppermute | solution.py:397
  115.8 10.5 %collective-permute-start.32 = (bf16[2,128,128]{2,1,0:T(8,128)(2,1)S(1)}, bf16[2,128,128]{2,1,0:T(8,128)(2,1)S(1)}, u32[]{:S(2)}, u32[]{:S(2)}) collective-permute-start(bf16[2,128,128]{2,1,0:T(8,128)(2,1)S(1)} %get-tuple-element.112), channel_id=1, source_target_pairs={{0,7},{1,6},{2,5},{3,4},{4,3},{5,2},{6,1},{7,0},{8,15},{9,14},{10,... | collective-permute-start | bytes 196616 | tf_op jit(solution)/shard_map/ppermute | solution.py:397
  (7 other events, 75.3 us)
